TPU v7x, 32 devices: a whole 2x2x4 slice. The times are simulated.
32 devices in a mesh: pole: 2 (over x), prow: 16 (over z, y, core).
Axes of the slice: x: 2, y: 2, z: 4, core: 2. Of those that a mesh axis runs over, the one named last changes fastest.
Arguments:
- factor_blocks: bfloat16 [256, 4, 128, 128], P(('pole', 'prow')), parts along dimension 0, may hold values from -0.25 to 0.25
- inverse_blocks: bfloat16 [64, 32, 128, 128], P(('pole', 'prow')), parts along dimension 0, may hold values from -6 to 6
- diag_factor_inv: float32 [256, 128, 128], P(('pole', 'prow')), parts along dimension 0, may hold values from -6 to 6
- structure: int32 [128, 4], replicated, may hold values from 0 to 31, all different within a row; in each aligned block of 8 rows (0 to 7, 8 to 15, ...) no two rows name the same one
Outputs:
- diag_inverse: float32 [256, 128, 128], P(('pole', 'prow')), parts along dimension 0
There are 2 independent parts, one for each index of `pole`. A program takes and returns all parts, laid end to end along the dimension named above; an argument that names none is the same for every part. Nothing has to cross between parts.
Inputs may be any that keep to these rules, and one draw needn't show every extreme that they name: `structure`: the 4 entries of a row are distinct, and within the rows of one device (aligned blocks of 8 rows) no ancestor is named twice; every ancestor is named by some row.
All inputs are finite; a program needn't handle non-finite values.
Results may differ from a plain program's by a relative error of at most 0.0021.
Values may be sent and summed in bfloat16 or wider, within the bound.
No kernel may reach another device: no remote copies, remote signals or barrier semaphores. Data moves between devices by JAX's collectives and lax.ppermute only.
A program may use at most 128 MiB of HBM per device.

v0:
```python
import jax
import jax.numpy as jnp
from jax import lax
from jax.sharding import PartitionSpec as P


def shards(factor_blocks, inverse_blocks, diag_factor_inv, structure):
    devices = lax.axis_size("prow")
    my_index = lax.axis_index("prow")
    local_cols = factor_blocks.shape[0]
    length = factor_blocks.shape[1]
    block_width = factor_blocks.shape[2]
    local_rows = inverse_blocks.shape[0]
    ancestors = inverse_blocks.shape[1]
    by_device = structure.reshape(devices, local_cols, length)
    my_struct = lax.dynamic_slice_in_dim(structure, my_index * local_cols, local_cols, 0)
    my_ancestors = my_index * local_rows + jnp.arange(local_rows, dtype=jnp.int32)
    is_named = jnp.any(by_device[:, :, :, None] == my_ancestors[None, None, None, :], axis=2)
    chosen = jnp.sum(is_named.astype(jnp.int32)[:, :, :, None] * by_device[:, :, None, :], axis=1)
    flat_index = jnp.arange(local_rows, dtype=jnp.int32)[None, :, None] * ancestors + chosen
    flat_inverse = inverse_blocks.reshape(local_rows * ancestors, block_width, block_width)
    picked = jnp.take(flat_inverse, flat_index, axis=0)
    column_named = my_struct[:, :, None] == jnp.arange(ancestors, dtype=jnp.int32)[None, None, :]
    column_named = jnp.any(column_named, axis=1).astype(jnp.int32)
    owner_col = jnp.sum(column_named * jnp.arange(local_cols, dtype=jnp.int32)[:, None], axis=0)
    outgoing = jnp.take(factor_blocks, owner_col, axis=0)
    incoming = lax.all_to_all(outgoing, "prow", split_axis=0, concat_axis=0, tiled=True)
    incoming = incoming.reshape(devices, local_rows, length, block_width, block_width)
    product = jnp.einsum("parxy,paryz->paxz", picked, incoming, preferred_element_type=jnp.float32)
    product = product.astype(jnp.bfloat16)
    is_self = (chosen == my_ancestors[None, :, None]).astype(jnp.bfloat16)
    own_block = jnp.einsum("par,parxy->paxy", is_self, incoming, preferred_element_type=jnp.float32)
    own_block = own_block.astype(jnp.bfloat16)
    partial_value = jnp.einsum(
        "paix,paiz->paxz", own_block, product, preferred_element_type=jnp.float32
    )
    partial_value = partial_value.reshape(ancestors, block_width, block_width)
    returned = lax.all_to_all(partial_value, "prow", split_axis=0, concat_axis=0, tiled=True)
    partials = jnp.take(returned, my_struct, axis=0)
    summed = jnp.sum(partials, axis=1)
    return diag_factor_inv + summed


def solution(mesh):
    placed = (
        P(("pole", "prow"), None, None, None),
        P(("pole", "prow"), None, None, None),
        P(("pole", "prow"), None, None),
        P(),
    )
    return jax.shard_map(
        shards,
        mesh=mesh,
        in_specs=placed,
        out_specs=P(("pole", "prow"), None, None),
        check_vma=False,
    )
```

profile of v0, /device:TPU:13, one launch (start us, length us, event | category | flops | bytes accessed | tf_op | source)
XLA Modules:
  0.0 179.6 jit_solution(7730846005400744175)
XLA Ops:
  0.0 0.0 copy-start
  0.0 0.9 compare_select_fusion.2
  0.9 0.1 fusion.10
  1.0 4.3 %gather_fusion = bf16[32,4,128,128]{3,2,1,0:T(8,128)(2,1)} fusion(bf16[8,4,128,128]{3,2,1,0:T(8,128)(2,1)} %param.4, s32[1024]{0:T(1024)S(1)} %pad_clamp_fusion.2), kind=kCustom, calls=%fused_computation | custom fusion | bytes 8388736 | tf_op jit(solution)/shard_map/jit(_take)/gather | solution.py:26
  5.3 4.6 %broadcast_select_fusion = bf16[32,4,128,128]{3,2,1,0:T(8,128)(2,1)} fusion(bf16[32,4,128,128]{3,2,1,0:T(8,128)(2,1)} %gather_fusion, pred[32]{0:T(512)(128)(4,1)S(1)} %compare_and_fusion.1), kind=kLoop, calls=%fused_computation.6 | loop fusion | flops 2097152 | bytes 8388640 | tf_op jit(solution)/shard_map/jit(_take)/select_n | solution.py:26
  10.0 0.0 copy-start.2
  10.0 6.7 %all-to-all-start = ((bf16[32,4,128,128]{3,2,1,0:T(8,128)(2,1)}), bf16[32,4,128,128]{3,2,1,0:T(8,128)(2,1)}, u32[]{:S(2)}, u32[]{:S(2)}) async-start(bf16[32,4,128,128]{3,2,1,0:T(8,128)(2,1)} %broadcast_select_fusion), calls=%async_computation | async-start | bytes 8388608 | tf_op jit(solution)/shard_map/all_to_all | solution.py:27
  16.6 0.0 copy-done.2
  16.6 0.1 eq.36
  16.7 0.1 copy.20
  16.8 0.1 compare_reduce_fusion
  16.9 0.1 compare_select_fusion
  17.0 0.1 copy.23
  17.1 0.1 reshape.85
  17.2 0.1 compare_convert_fusion
  17.3 0.1 copy.22
  17.4 0.1 copy.32
  17.5 0.0 copy-done
  17.5 3.1 %gather_fusion.1 = bf16[128,128,128]{2,1,0:T(8,128)(2,1)} fusion(bf16[64,128,128]{2,1,0:T(8,128)(2,1)S(1)} %bitcast.25, s32[1024]{0:T(1024)S(1)} %pad_clamp_fusion.1), kind=kCustom, calls=%fused_computation.1 | custom fusion | bytes 8389120 | tf_op jit(solution)/shard_map/jit(_take)/gather | solution.py:22
  20.6 88.5 %all-to-all-done = bf16[32,4,128,128]{3,2,1,0:T(8,128)(2,1)} async-done(((bf16[32,4,128,128]{3,2,1,0:T(8,128)(2,1)}), bf16[32,4,128,128]{3,2,1,0:T(8,128)(2,1)}, u32[]{:S(2)}, u32[]{:S(2)}) %all-to-all-start) | async-done | bytes 4194336 | tf_op jit(solution)/shard_map/all_to_all | solution.py:27
  109.1 3.6 %multiply_reduce_fusion = bf16[16,2,128,128]{3,2,1,0:T(8,128)(2,1)S(1)} fusion(bf16[16,2,4,128,128]{4,3,2,1,0:T(8,128)(2,1)} %bitcast.2, f32[16,2,4]{2,1,0:T(2,128)S(1)} %copy.32), kind=kLoop, calls=%fused_computation.3 | loop fusion | flops 5767168 | bytes 5243392
  112.7 1.3 copy.30
  114.0 6.8 %fusion.7 = f32[16,2,128,128]{3,2,1,0:T(8,128)} fusion(bf16[16,2,4,128,128]{4,3,2,1,0:T(8,128)(2,1)} %bitcast.2, bf16[16,2,4,128,128]{4,3,2,1,0:T(8,128)(2,1)} %bitcast.26, pred[16,2,4]{2,1,0:T(4,128)(4,1)S(1)} %copy.22, bf16[16,2,128,128]{2,3,1,0:T(8,128)(2,1)} %copy.30), kind=kOutput, calls=%fused_computation.11 | convolution fusion | flops 673710080 | bytes 11534464 | tf_op jit(solution)/shard_map/paix,paiz->paxz/dot_general | solution.py:34
  120.9 4.9 %all-to-all-start.1 = ((f32[32,128,128]{2,1,0:T(8,128)}), f32[32,128,128]{2,1,0:T(8,128)}, u32[]{:S(2)}, u32[]{:S(2)}) async-start(f32[32,128,128]{2,1,0:T(8,128)} %bitcast.27), calls=%async_computation.1 | async-start | bytes 4194304 | tf_op jit(solution)/shard_map/all_to_all | solution.py:38
  125.8 0.0 copy-start.1
  125.8 0.1 copy.19
  125.9 0.1 copy.24
  126.0 0.1 reshape.93
  126.1 47.2 %all-to-all-done.1 = f32[32,128,128]{2,1,0:T(8,128)} async-done(((f32[32,128,128]{2,1,0:T(8,128)}), f32[32,128,128]{2,1,0:T(8,128)}, u32[]{:S(2)}, u32[]{:S(2)}) %all-to-all-start.1) | async-done | bytes 2097184 | tf_op jit(solution)/shard_map/all_to_all | solution.py:38
  173.3 3.6 %gather_fusion.2 = f32[32,128,128]{2,1,0:T(8,128)} fusion(f32[32,128,128]{2,1,0:T(8,128)} %all-to-all-done.1, s32[1024]{0:T(1024)S(1)} %pad_clamp_fusion), kind=kCustom, calls=%fused_computation.2 | custom fusion | bytes 4194432 | tf_op jit(solution)/shard_map/jit(_take)/gather | solution.py:39
  176.9 1.9 %select_reduce_fusion = f32[8,128,128]{2,1,0:T(8,128)S(1)} fusion(pred[8,4]{1,0:T(8,128)(4,1)S(1)} %copy.19, f32[32,128,128]{2,1,0:T(8,128)} %gather_fusion.2), kind=kLoop, calls=%fused_computation.9 | loop fusion | flops 917504 | bytes 2621472 | tf_op jit(solution)/shard_map/reduce_sum | solution.py:40
  178.8 0.0 copy-done.1
  178.8 0.9 add.108
  (10 shorter events, 0.1 us)
Async XLA Ops:
  0.0 17.5 %copy-start = (bf16[2,32,128,128]{3,2,1,0:T(8,128)(2,1)S(1)}, bf16[2,32,128,128]{3,2,1,0:T(8,128)(2,1)}, u32[]{:S(2)}) copy-start(bf16[2,32,128,128]{3,2,1,0:T(8,128)(2,1)} %param.5) | copy-start | bytes 6291460
  10.0 6.7 %copy-start.2 = (s32[128,4]{0,1:T(4,128)S(1)}, s32[128,4]{0,1:T(4,128)}, u32[]{:S(2)}) copy-start(s32[128,4]{0,1:T(4,128)} %param.7) | copy-start | bytes 6148
  10.0 99.2 %all-to-all-start = ((bf16[32,4,128,128]{3,2,1,0:T(8,128)(2,1)}), bf16[32,4,128,128]{3,2,1,0:T(8,128)(2,1)}, u32[]{:S(2)}, u32[]{:S(2)}) async-start(bf16[32,4,128,128]{3,2,1,0:T(8,128)(2,1)} %broadcast_select_fusion), calls=%async_computation | async-start | bytes 8388608 | tf_op jit(solution)/shard_map/all_to_all | solution.py:27
  120.9 52.4 %all-to-all-start.1 = ((f32[32,128,128]{2,1,0:T(8,128)}), f32[32,128,128]{2,1,0:T(8,128)}, u32[]{:S(2)}, u32[]{:S(2)}) async-start(f32[32,128,128]{2,1,0:T(8,128)} %bitcast.27), calls=%async_computation.1 | async-start | bytes 4194304 | tf_op jit(solution)/shard_map/all_to_all | solution.py:38
  125.8 53.0 %copy-start.1 = (f32[8,128,128]{2,1,0:T(8,128)S(1)}, f32[8,128,128]{2,1,0:T(8,128)}, u32[]{:S(2)}) copy-start(f32[8,128,128]{2,1,0:T(8,128)} %param.6) | copy-start | bytes 1572868
where the time goes:
time: 180 us
  waiting for transfers between devices  136 us (76%)
  local copies, waits for them, and re-layouts  13.1 us (7%)
  other arithmetic  12.3 us (7%)
  starting transfers between devices  11.6 us (6%)
  matrix products  6.83 us (4%)
    all_to_all x1, waiting for transfers between devices, shards(): lax.all_to_all(outgoing, 'prow', split_axis=0, concat_axis=0, tiled=True)  88.5 us
    all_to_all x1, waiting for transfers between devices, shards(): lax.all_to_all(partial_value, 'prow', split_axis=0, concat_axis=0, tiled=...  47.2 us
    dot_general x1, matrix products, shards(): jnp.einsum('paix,paiz->paxz', own_block, product, preferred_element_type=...  6.83 us
    all_to_all x1, starting transfers between devices, shards(): lax.all_to_all(outgoing, 'prow', split_axis=0, concat_axis=0, tiled=True)  6.69 us
    all_to_all x1, starting transfers between devices, shards(): lax.all_to_all(partial_value, 'prow', split_axis=0, concat_axis=0, tiled=...  4.9 us
    select_n x2, other arithmetic, shards(): outgoing = jnp.take(factor_blocks, owner_col, axis=0)  4.64 us
    gather x1, local copies, waits for them, and re-layouts, shards(): outgoing = jnp.take(factor_blocks, owner_col, axis=0)  4.29 us
    unnamed x2, other arithmetic  3.67 us
  transfers between devices with their start and end apart: 2, of which 2 were waited for; matrix products, arithmetic and copies ran while one was open for 2% of the time, Pallas kernels for 0%

commit v1 on v0

v1 whole, which is shorter than its diff:
```python
import functools

import jax
import jax.numpy as jnp
from jax import lax
from jax.experimental import pallas as pl
from jax.experimental.pallas import tpu as pltpu
from jax.sharding import PartitionSpec as P


def pack_kernel(n, cols, me_ref, st_ref, inv_ref, send_ref, diag_ref, idx_v, idx_s, sem, sem_d, sem_i):
    length, total = st_ref.shape
    rows = inv_ref.shape[0]
    others = length - 1
    me = me_ref[0]
    for j in range(rows):
        pltpu.make_async_copy(inv_ref.at[j, me * rows + j], diag_ref.at[j], sem_d).start()
    st = [st_ref[r : r + 1, :] for r in range(length)]
    lines = []
    for j in range(rows):
        row = me * rows + j
        for q in range(others):
            line = jnp.zeros((1, total), jnp.int32)
            for r in range(length):
                s = q if q < r else q + 1
                line = jnp.where(st[r] == row, st[s], line)
            lines.append(line)
    pad = idx_v.shape[0] - len(lines)
    lines.append(jnp.zeros((pad, total), jnp.int32))
    picks = jnp.concatenate(lines, axis=0).astype(jnp.float32)
    first = lax.broadcasted_iota(jnp.int32, (total, idx_v.shape[1]), 1) * cols
    place = lax.broadcasted_iota(jnp.int32, (total, idx_v.shape[1]), 0)
    group = ((place >= first) & (place < first + cols)).astype(jnp.float32)
    table = jnp.dot(picks, group, preferred_element_type=jnp.float32, precision=lax.Precision.HIGHEST)
    idx_v[...] = table.astype(jnp.int32)
    copy = pltpu.make_async_copy(idx_v, idx_s, sem_i)
    copy.start()
    copy.wait()

    def to_device(p, carry):
        for j in range(rows):
            for q in range(others):
                c = idx_s[j * others + q, p]
                pltpu.make_async_copy(inv_ref.at[j, c], send_ref.at[p, j, q], sem).start()
        return carry

    lax.fori_loop(0, n, to_device, 0)
    pltpu.make_async_copy(diag_ref, diag_ref, sem_d).wait()
    pltpu.make_async_copy(send_ref, send_ref, sem).wait()


def level_kernel(me_ref, st_ref, recv_ref, diag_ref, fac_ref, dfi_ref, out_ref, mat, sems):
    cols = fac_ref.shape[0]
    width = out_ref.shape[1]
    length = fac_ref.shape[1] // width
    rows = diag_ref.shape[1]
    me = me_ref[0]

    for k in range(cols):
        for r in range(length):
            anc = st_ref[(me * cols + k) * length + r]
            owner = lax.div(anc, rows)
            local = lax.rem(anc, rows)
            here = pl.ds(r * width, width)
            for s in range(length):
                if s == r:
                    src = diag_ref.at[lax.bitwise_xor(owner, me), local]
                else:
                    src = recv_ref.at[owner, local, s if s < r else s - 1]
                pltpu.make_async_copy(src, mat.at[k, here, pl.ds(s * width, width)], sems.at[k]).start()
    for k in range(cols):
        pltpu.make_async_copy(mat.at[k], mat.at[k], sems.at[k]).wait()
        fac = fac_ref[k]
        product = jnp.dot(mat[k], fac, preferred_element_type=jnp.float32).astype(jnp.bfloat16)
        term = lax.dot_general(fac, product, (((0,), (0,)), ((), ())), preferred_element_type=jnp.float32)
        out_ref[k] = dfi_ref[k] + term


def shards(n, factor_blocks, inverse_blocks, diag_factor_inv, structure):
    cols, length, width, _ = factor_blocks.shape
    rows, ancestors = inverse_blocks.shape[:2]
    total = structure.shape[0]
    me = lax.axis_index("prow").astype(jnp.int32)
    me1 = me.reshape(1)
    smem = pl.BlockSpec(memory_space=pltpu.SMEM)
    vmem = pl.BlockSpec(memory_space=pltpu.VMEM)
    hbm = pl.BlockSpec(memory_space=pl.ANY)
    lines = -(-rows * (length - 1) // 8) * 8
    lanes = -(-n // 128) * 128
    send, diag = pl.pallas_call(
        functools.partial(pack_kernel, n, cols),
        out_shape=(
            jax.ShapeDtypeStruct((n, rows, length - 1, width, width), jnp.bfloat16),
            jax.ShapeDtypeStruct((rows, width, width), jnp.bfloat16),
        ),
        in_specs=[smem, vmem, hbm],
        out_specs=(hbm, hbm),
        scratch_shapes=[
            pltpu.VMEM((lines, lanes), jnp.int32),
            pltpu.SMEM((lines, lanes), jnp.int32),
            pltpu.SemaphoreType.DMA,
            pltpu.SemaphoreType.DMA,
            pltpu.SemaphoreType.DMA,
        ],
    )(me1, structure.T, inverse_blocks)
    recv = lax.all_to_all(send, "prow", split_axis=0, concat_axis=0, tiled=True)
    held = diag.reshape(1, rows, width, width)
    mask = 1
    while mask < n:
        came = lax.ppermute(held, "prow", [(i, i ^ mask) for i in range(n)])
        held = jnp.concatenate([held, came], axis=0)
        mask *= 2
    return pl.pallas_call(
        level_kernel,
        out_shape=jax.ShapeDtypeStruct((cols, width, width), jnp.float32),
        in_specs=[smem, smem, hbm, hbm, vmem, vmem],
        out_specs=vmem,
        scratch_shapes=[
            pltpu.VMEM((cols, length * width, length * width), jnp.bfloat16),
            pltpu.SemaphoreType.DMA((cols,)),
        ],
        compiler_params=pltpu.CompilerParams(vmem_limit_bytes=32 * 2**20),
    )(me1, structure.reshape(-1), recv, held, factor_blocks.reshape(cols, length * width, width), diag_factor_inv)


def solution(mesh):
    placed = (
        P(("pole", "prow"), None, None, None),
        P(("pole", "prow"), None, None, None),
        P(("pole", "prow"), None, None),
        P(),
    )
    return jax.shard_map(
        functools.partial(shards, mesh.shape["prow"]),
        mesh=mesh,
        in_specs=placed,
        out_specs=P(("pole", "prow"), None, None),
        check_vma=False,
    )
```

time: 180 us -> 213 us (1.18)
  the two profiles are of different devices: /device:TPU:13 before, /device:TPU:0 now
where the time goes in v1:
time: 213 us; the launch traced here: 212 us
  Pallas kernels  106 us (50%)
  waiting for transfers between devices  82.1 us (39%)
  starting transfers between devices  14.3 us (7%)
  local copies, waits for them, and re-layouts  7.99 us (4%)
    pallas_call x1, Pallas kernels, shards(): pl.pallas_call(functools.partial(pack_kernel, n, cols), out_shape=(jax.Sh...  99.1 us
    ppermute x4, waiting for transfers between devices, shards(): came = lax.ppermute(held, 'prow', [(i, i ^ mask) for i in range(n)])  82.1 us
    all_to_all x1, starting transfers between devices, shards(): recv = lax.all_to_all(send, 'prow', split_axis=0, concat_axis=0, tiled=True)  7.53 us
    pallas_call x1, Pallas kernels, shards(): pl.pallas_call(level_kernel, out_shape=jax.ShapeDtypeStruct((cols, width,...  7.17 us
    unnamed x19, local copies, waits for them, and re-layouts  6.97 us
    ppermute x4, starting transfers between devices, shards(): came = lax.ppermute(held, 'prow', [(i, i ^ mask) for i in range(n)])  6.82 us
  transfers between devices with their start and end apart: 5, of which 4 were waited for; matrix products, arithmetic and copies ran while one was open for 2% of the time, Pallas kernels for 0%

profile of v1, /device:TPU:0, one launch (start us, length us, event | category | flops | bytes accessed | tf_op | source)
XLA Modules:
  0.0 212.4 jit_solution(4261975730883206845)
XLA Ops:
  0.0 99.1 %shard_map.46 = (bf16[16,2,3,128,128]{4,3,2,1,0:T(8,128)(2,1)}, bf16[2,128,128]{2,1,0:T(8,128)(2,1)}) custom-call(s32[1]{0:T(128)} %bitcast.me_ref, s32[4,128]{1,0:T(4,128)} %bitcast.10, bf16[2,32,128,128]{3,2,1,0:T(8,128)(2,1)} %inv_ref.1), custom_call_target="tpu_custom_call" | custom-call | tf_op jit(solution)/shard_map/pallas_call | solution.py:90
  99.1 0.0 copy-start.4
  99.1 0.0 copy-start.6
  99.1 7.5 %all-to-all-start = ((bf16[16,2,3,128,128]{4,3,2,1,0:T(8,128)(2,1)}), bf16[16,2,3,128,128]{4,3,2,1,0:T(8,128)(2,1)S(1)}, u32[]{:S(2)}, u32[]{:S(2)}) async-start(bf16[16,2,3,128,128]{4,3,2,1,0:T(8,128)(2,1)} %get-tuple-element.7), calls=%async_computation | async-start | bytes 6291456 | tf_op jit(solution)/shard_map/all_to_all | solution.py:106
  106.7 0.0 copy-done.4
  106.7 0.5 collective-permute-start
  107.1 1.0 collective-permute-done
  108.1 0.0 copy-start.5
  108.1 1.9 collective-permute-start.1
  110.0 20.5 %collective-permute-done.1 = bf16[2,2,128,128]{3,2,1,0:T(8,128)(2,1)S(1)} collective-permute-done((bf16[2,2,128,128]{3,2,1,0:T(8,128)(2,1)S(1)}, bf16[2,2,128,128]{3,2,1,0:T(8,128)(2,1)S(1)}, u32[]{:S(2)}, u32[]{:S(2)}) %collective-permute-start.1) | collective-permute-done | bytes 131104 | tf_op jit(solution)/shard_map/ppermute | solution.py:110
  130.4 0.7 pad_maximum_fusion.1
  131.2 0.0 copy-done.5
  131.2 0.0 collective-permute-start.2
  131.2 0.0 copy-done.6
  131.2 0.7 copy.5
  131.9 0.9 reshape.13.st_ref
  132.9 31.3 %collective-permute-done.2 = bf16[4,2,128,128]{3,2,1,0:T(8,128)(2,1)S(1)} collective-permute-done((bf16[4,2,128,128]{3,2,1,0:T(8,128)(2,1)}, bf16[4,2,128,128]{3,2,1,0:T(8,128)(2,1)S(1)}, u32[]{:S(2)}, u32[]{:S(2)}) %collective-permute-start.2) | collective-permute-done | bytes 262176 | tf_op jit(solution)/shard_map/ppermute | solution.py:110
  164.2 0.9 pad_maximum_fusion
  165.1 4.5 %collective-permute-start.3 = (bf16[8,2,128,128]{3,2,1,0:T(8,128)(2,1)S(1)}, bf16[8,2,128,128]{3,2,1,0:T(8,128)(2,1)S(1)}, u32[]{:S(2)}, u32[]{:S(2)}) collective-permute-start(bf16[8,2,128,128]{3,2,1,0:T(8,128)(2,1)S(1)} %pad_maximum_fusion), channel_id=1, source_target_pairs={{0,8},{1,9},{2,10},{3,11},{4,12},{5,13},{6,14},{7,15},{8,0},{9,1},... | collective-permute-start | bytes 1572872 | tf_op jit(solution)/shard_map/ppermute | solution.py:110
  169.6 0.8 constant_dynamic-update-slice_fusion.4
  170.4 0.9 constant_dynamic-update-slice_fusion.3
  171.3 29.4 %collective-permute-done.3 = bf16[8,2,128,128]{3,2,1,0:T(8,128)(2,1)S(1)} collective-permute-done((bf16[8,2,128,128]{3,2,1,0:T(8,128)(2,1)S(1)}, bf16[8,2,128,128]{3,2,1,0:T(8,128)(2,1)S(1)}, u32[]{:S(2)}, u32[]{:S(2)}) %collective-permute-start.3) | collective-permute-done | bytes 524320 | tf_op jit(solution)/shard_map/ppermute | solution.py:110
  200.7 0.1 constant_dynamic-update-slice_fusion.diag_ref
  200.8 0.0 copy-start
  200.8 1.0 copy-done
  201.8 0.0 all-to-all-done.recv_ref
  201.8 0.0 copy-start.1
  201.8 1.2 copy-done.1
  203.0 0.0 copy-start.2
  203.0 1.2 copy-done.2
  204.2 0.0 copy-start.3
  204.2 1.0 copy-done.3
  205.3 7.2 %shard_map.47 = f32[8,128,128]{2,1,0:T(8,128)} custom-call(s32[1]{0:T(128)} %bitcast.me_ref, s32[512]{0:T(512)S(1)} %reshape.13.st_ref, bf16[16,2,3,128,128]{4,3,2,1,0:T(8,128)(2,1)S(1)} %all-to-all-done.recv_ref, bf16[16,2,128,128]{3,2,1,0:T(8,128)(2,1)S(1)} %copy-done.1, bf16[8,512,128]{2,1,0:T(8,128)(2,1)S(1)} %bitcast.5, f32[8,128,128]{2,1,0:T(8,128)S(1)} %copy-done.3), custom_call_target="tpu_custom_call" | custom-call | tf_op jit(solution)/shard_map/pallas_call | solution.py:113
  (3 shorter events, 0.1 us)
Async XLA Ops:
  99.1 7.6 %copy-start.4 = (bf16[2,128,128]{2,1,0:T(8,128)(2,1)S(1)}, bf16[2,128,128]{2,1,0:T(8,128)(2,1)}, u32[]{:S(2)}) copy-start(bf16[2,128,128]{2,1,0:T(8,128)(2,1)} %get-tuple-element.8) | copy-start | bytes 196612
  99.1 32.1 %copy-start.6 = (s32[128,4]{0,1:T(4,128)S(1)}, s32[128,4]{0,1:T(4,128)}, u32[]{:S(2)}) copy-start(s32[128,4]{0,1:T(4,128)} %param.7) | copy-start | bytes 6148
  99.1 102.7 %all-to-all-start = ((bf16[16,2,3,128,128]{4,3,2,1,0:T(8,128)(2,1)}), bf16[16,2,3,128,128]{4,3,2,1,0:T(8,128)(2,1)S(1)}, u32[]{:S(2)}, u32[]{:S(2)}) async-start(bf16[16,2,3,128,128]{4,3,2,1,0:T(8,128)(2,1)} %get-tuple-element.7), calls=%async_computation | async-start | bytes 6291456 | tf_op jit(solution)/shard_map/all_to_all | solution.py:106
  106.7 1.4 collective-permute-start
  108.1 23.1 %copy-start.5 = (bf16[1,2,128,128]{3,2,1,0:T(8,128)(2,1)}, bf16[1,2,128,128]{3,2,1,0:T(8,128)(2,1)S(1)}, u32[]{:S(2)}) copy-start(bf16[1,2,128,128]{3,2,1,0:T(8,128)(2,1)S(1)} %collective-permute-done) | copy-start | bytes 196612
  108.1 22.3 %collective-permute-start.1 = (bf16[2,2,128,128]{3,2,1,0:T(8,128)(2,1)S(1)}, bf16[2,2,128,128]{3,2,1,0:T(8,128)(2,1)S(1)}, u32[]{:S(2)}, u32[]{:S(2)}) collective-permute-start(bf16[2,2,128,128]{3,2,1,0:T(8,128)(2,1)S(1)} %pad_maximum_fusion.2), channel_id=1, source_target_pairs={{0,2},{1,3},{2,0},{3,1},{4,6},{5,7},{6,4},{7,5},{8,10},{9,11},{10,... | collective-permute-start | bytes 393224 | tf_op jit(solution)/shard_map/ppermute | solution.py:110
  131.2 33.0 %collective-permute-start.2 = (bf16[4,2,128,128]{3,2,1,0:T(8,128)(2,1)}, bf16[4,2,128,128]{3,2,1,0:T(8,128)(2,1)S(1)}, u32[]{:S(2)}, u32[]{:S(2)}) collective-permute-start(bf16[4,2,128,128]{3,2,1,0:T(8,128)(2,1)} %pad_maximum_fusion.1), channel_id=1, source_target_pairs={{0,4},{1,5},{2,6},{3,7},{4,0},{5,1},{6,2},{7,3},{8,12},{9,13},{10,... | collective-permute-start | bytes 786440 | tf_op jit(solution)/shard_map/ppermute | solution.py:110
  165.1 35.6 %collective-permute-start.3 = (bf16[8,2,128,128]{3,2,1,0:T(8,128)(2,1)S(1)}, bf16[8,2,128,128]{3,2,1,0:T(8,128)(2,1)S(1)}, u32[]{:S(2)}, u32[]{:S(2)}) collective-permute-start(bf16[8,2,128,128]{3,2,1,0:T(8,128)(2,1)S(1)} %pad_maximum_fusion), channel_id=1, source_target_pairs={{0,8},{1,9},{2,10},{3,11},{4,12},{5,13},{6,14},{7,15},{8,0},{9,1},... | collective-permute-start | bytes 1572872 | tf_op jit(solution)/shard_map/ppermute | solution.py:110
  200.8 1.0 copy-start
  201.8 1.2 copy-start.1
  203.0 1.2 copy-start.2
  204.2 1.0 copy-start.3

commit v2 on v1

v2 whole, which is shorter than its diff:
```python
import functools

import jax
import jax.numpy as jnp
from jax import lax
from jax.experimental import pallas as pl
from jax.experimental.pallas import tpu as pltpu
from jax.sharding import PartitionSpec as P


def diag_kernel(me_ref, inv_ref, diag_ref, sem):
    rows = inv_ref.shape[0]
    for j in range(rows):
        pltpu.make_async_copy(inv_ref.at[j, me_ref[0] * rows + j], diag_ref.at[0, j], sem.at[j]).start()
    for j in range(rows):
        pltpu.make_async_copy(inv_ref.at[j, 0], diag_ref.at[0, j], sem.at[j]).wait()


def pack_kernel(n, cols, me_ref, st_ref, inv_ref, send_ref, send_v, idx_v, idx_s, sem_i, sem_o):
    length, total = st_ref.shape
    rows = inv_ref.shape[0]
    others = length - 1
    me = me_ref[0]
    st = [st_ref[r : r + 1, :] for r in range(length)]
    lines = []
    for j in range(rows):
        row = me * rows + j
        for q in range(others):
            line = jnp.zeros((1, total), jnp.int32)
            for r in range(length):
                line = jnp.where(st[r] == row, st[q if q < r else q + 1], line)
            lines.append(line)
    lines.append(jnp.zeros((idx_v.shape[0] - len(lines), total), jnp.int32))
    picks = jnp.concatenate(lines, axis=0).astype(jnp.float32)
    grid = (total, idx_v.shape[1])
    first = lax.broadcasted_iota(jnp.int32, grid, 1) * cols
    place = lax.broadcasted_iota(jnp.int32, grid, 0)
    group = ((place >= first) & (place < first + cols)).astype(jnp.float32)
    table = jnp.dot(picks, group, preferred_element_type=jnp.float32, precision=lax.Precision.HIGHEST)
    idx_v[...] = table.astype(jnp.int32)
    copy = pltpu.make_async_copy(idx_v, idx_s, sem_i)
    copy.start()
    copy.wait()

    def to_device(p, carry):
        for j in range(rows):
            for q in range(others):
                send_v[p, j, q] = inv_ref[j, idx_s[j * others + q, p]]
        pltpu.make_async_copy(send_v.at[p], send_ref.at[p], sem_o).start()
        return carry

    lax.fori_loop(0, n, to_device, 0)
    pltpu.make_async_copy(send_v, send_ref, sem_o).wait()


def level_kernel(quad, me_ref, st_ref, recv_ref, *rest):
    diag_refs, rest = rest[:quad], rest[quad:]
    fac_ref, dfi_ref, out_ref, diag_v, fac_v, dfi_v, out_v, sems, sem_d, sem_g, sem_o = rest
    cols, deep, width = fac_v.shape
    length = deep // width
    rows = recv_ref.shape[1]
    steps = diag_refs[0].shape[0]
    me = me_ref[0]
    for a in range(quad):
        for t in range(steps):
            owner = lax.bitwise_xor(lax.rem(me + t * quad, steps * quad), a)
            pltpu.make_async_copy(diag_refs[a].at[t], diag_v.at[pl.ds(owner * rows, rows)], sem_g).start()
    fetch = [pltpu.make_async_copy(fac_ref.at[k], fac_v.at[k], sems.at[k]) for k in range(cols)]
    fetch_d = pltpu.make_async_copy(dfi_ref, dfi_v, sem_d)
    for f in fetch:
        f.start()
    fetch_d.start()
    pltpu.make_async_copy(diag_v, diag_v, sem_g).wait()
    for k in range(cols):
        fetch[k].wait()
        fac = fac_v[k]
        product = []
        for r in range(length):
            anc = st_ref[r, me * cols + k]
            owner, local = lax.div(anc, rows), lax.rem(anc, rows)
            line = [diag_v[anc] if s == r else recv_ref[owner, local, s if s < r else s - 1] for s in range(length)]
            line = jnp.concatenate(line, axis=1)
            product.append(jnp.dot(line, fac, preferred_element_type=jnp.float32).astype(jnp.bfloat16))
        product = jnp.concatenate(product, axis=0)
        term = lax.dot_general(fac, product, (((0,), (0,)), ((), ())), preferred_element_type=jnp.float32)
        if k == 0:
            fetch_d.wait()
        out_v[k] = dfi_v[k] + term
        pltpu.make_async_copy(out_v.at[k], out_ref.at[k], sem_o).start()
    pltpu.make_async_copy(out_v, out_ref, sem_o).wait()


def shards(n, factor_blocks, inverse_blocks, diag_factor_inv, structure):
    cols, length, width, _ = factor_blocks.shape
    rows, ancestors = inverse_blocks.shape[:2]
    total = structure.shape[0]
    me = lax.axis_index("prow").astype(jnp.int32)
    me1 = me.reshape(1)
    smem = pl.BlockSpec(memory_space=pltpu.SMEM)
    vmem = pl.BlockSpec(memory_space=pltpu.VMEM)
    hbm = pl.BlockSpec(memory_space=pltpu.HBM)
    quad = 4
    steps = n // quad

    diag = pl.pallas_call(
        diag_kernel,
        out_shape=jax.ShapeDtypeStruct((1, rows, width, width), jnp.bfloat16),
        in_specs=[smem, hbm],
        out_specs=vmem,
        scratch_shapes=[pltpu.SemaphoreType.DMA((rows,))],
    )(me1, inverse_blocks)
    held = [diag]
    for t in range(1, steps):
        held.append(lax.ppermute(diag, "prow", [((i + t * quad) % n, i) for i in range(n)]))
    held = jnp.concatenate(held, axis=0)
    lines = -(-rows * (length - 1) // 8) * 8
    lanes = -(-n // 128) * 128
    send = pl.pallas_call(
        functools.partial(pack_kernel, n, cols),
        out_shape=jax.ShapeDtypeStruct((n, rows, length - 1, width, width), jnp.bfloat16),
        in_specs=[smem, vmem, vmem],
        out_specs=hbm,
        scratch_shapes=[
            pltpu.VMEM((n, rows, length - 1, width, width), jnp.bfloat16),
            pltpu.VMEM((lines, lanes), jnp.int32),
            pltpu.SMEM((lines, lanes), jnp.int32),
            pltpu.SemaphoreType.DMA,
            pltpu.SemaphoreType.DMA,
        ],
        compiler_params=pltpu.CompilerParams(vmem_limit_bytes=40 * 2**20),
    )(me1, structure.T, inverse_blocks)
    send, held = lax.optimization_barrier((send, held))
    spread = [held]
    for a in range(1, quad):
        spread.append(lax.ppermute(held, "prow", [(i ^ a, i) for i in range(n)]))
    recv = lax.all_to_all(send, "prow", split_axis=0, concat_axis=0, tiled=True)
    deep = length * width
    return pl.pallas_call(
        functools.partial(level_kernel, quad),
        out_shape=jax.ShapeDtypeStruct((cols, width, width), jnp.float32),
        in_specs=[smem, smem, vmem] + [hbm] * (quad + 2),
        out_specs=hbm,
        scratch_shapes=[
            pltpu.VMEM((ancestors, width, width), jnp.bfloat16),
            pltpu.VMEM((cols, deep, width), jnp.bfloat16),
            pltpu.VMEM((cols, width, width), jnp.float32),
            pltpu.VMEM((cols, width, width), jnp.float32),
            pltpu.SemaphoreType.DMA((cols,)),
            pltpu.SemaphoreType.DMA,
            pltpu.SemaphoreType.DMA,
            pltpu.SemaphoreType.DMA,
        ],
        compiler_params=pltpu.CompilerParams(vmem_limit_bytes=48 * 2**20),
    )(me1, structure.T, recv, *spread, factor_blocks.reshape(cols, deep, width), diag_factor_inv)


def solution(mesh):
    placed = (
        P(("pole", "prow"), None, None, None),
        P(("pole", "prow"), None, None, None),
        P(("pole", "prow"), None, None),
        P(),
    )
    return jax.shard_map(
        functools.partial(shards, mesh.shape["prow"]),
        mesh=mesh,
        in_specs=placed,
        out_specs=P(("pole", "prow"), None, None),
        check_vma=False,
    )
```

time: 213 us -> 99.9 us (0.47)
  the two profiles are of different devices: /device:TPU:0 before, /device:TPU:13 now
where the time goes in v2:
time: 99.9 us; the launch traced here: 99.5 us
  waiting for transfers between devices  67.7 us (68%)
  starting transfers between devices  12.1 us (12%)
  Pallas kernels  11.7 us (12%)
  local copies, waits for them, and re-layouts  7.91 us (8%)
    all_to_all x1, waiting for transfers between devices, shards(): recv = lax.all_to_all(send, 'prow', split_axis=0, concat_axis=0, tiled=True)  39.1 us
    ppermute x3, waiting for transfers between devices, shards(): spread.append(lax.ppermute(held, 'prow', [(i ^ a, i) for i in range(n)]))  26.5 us
    unnamed x24, local copies, waits for them, and re-layouts  7.91 us
    pallas_call x1, Pallas kernels, shards(): pl.pallas_call(functools.partial(level_kernel, quad), out_shape=jax.Shape...  7.63 us
    all_to_all x1, starting transfers between devices, shards(): recv = lax.all_to_all(send, 'prow', split_axis=0, concat_axis=0, tiled=True)  6.15 us
    ppermute x3, starting transfers between devices, shards(): lax.ppermute(diag, 'prow', [((i + t * quad) % n, i) for i in range(n)])  3.83 us
    pallas_call x1, Pallas kernels, shards(): pl.pallas_call(functools.partial(pack_kernel, n, cols), out_shape=jax.Sha...  2.45 us
    ppermute x3, starting transfers between devices, shards(): spread.append(lax.ppermute(held, 'prow', [(i ^ a, i) for i in range(n)]))  2.15 us
  transfers between devices with their start and end apart: 7, of which 4 were waited for; matrix products, arithmetic and copies ran while one was open for 0% of the time, Pallas kernels for 2%

profile of v2, /device:TPU:13, one launch (start us, length us, event | category | flops | bytes accessed | tf_op | source)
XLA Modules:
  0.0 99.5 jit_solution(12915315556990800653)
XLA Ops:
  0.0 0.0 copy-start
  0.0 1.6 %shard_map.47 = bf16[1,2,128,128]{3,2,1,0:T(8,128)(2,1)} custom-call(s32[1]{0:T(128)} %bitcast.me_ref, bf16[2,32,128,128]{3,2,1,0:T(8,128)(2,1)} %inv_ref.3), custom_call_target="tpu_custom_call" | custom-call | tf_op jit(solution)/shard_map/pallas_call | solution.py:105
  1.6 1.3 %collective-permute-start.2 = (bf16[1,2,128,128]{3,2,1,0:T(8,128)(2,1)}, bf16[1,2,128,128]{3,2,1,0:T(8,128)(2,1)S(1)}, u32[]{:S(2)}, u32[]{:S(2)}) collective-permute-start(bf16[1,2,128,128]{3,2,1,0:T(8,128)(2,1)} %shard_map.47), channel_id=1, source_target_pairs={{12,0},{13,1},{14,2},{15,3},{0,4},{1,5},{2,6},{3,7},{4,8},{5,9},{6... | collective-permute-start | bytes 196616 | tf_op jit(solution)/shard_map/ppermute | solution.py:114
  2.9 1.1 %collective-permute-start.1 = (bf16[1,2,128,128]{3,2,1,0:T(8,128)(2,1)}, bf16[1,2,128,128]{3,2,1,0:T(8,128)(2,1)S(1)}, u32[]{:S(2)}, u32[]{:S(2)}) collective-permute-start(bf16[1,2,128,128]{3,2,1,0:T(8,128)(2,1)} %shard_map.47), channel_id=1, source_target_pairs={{8,0},{9,1},{10,2},{11,3},{12,4},{13,5},{14,6},{15,7},{0,8},{1,9},... | collective-permute-start | bytes 196616 | tf_op jit(solution)/shard_map/ppermute | solution.py:114
  4.0 1.4 %collective-permute-start = (bf16[1,2,128,128]{3,2,1,0:T(8,128)(2,1)}, bf16[1,2,128,128]{3,2,1,0:T(8,128)(2,1)S(1)}, u32[]{:S(2)}, u32[]{:S(2)}) collective-permute-start(bf16[1,2,128,128]{3,2,1,0:T(8,128)(2,1)} %shard_map.47), channel_id=1, source_target_pairs={{4,0},{5,1},{6,2},{7,3},{8,4},{9,5},{10,6},{11,7},{12,8},{13,9},{1... | collective-permute-start | bytes 196616 | tf_op jit(solution)/shard_map/ppermute | solution.py:114
  5.4 0.0 copy-done
  5.4 0.0 copy-start.9
  5.4 0.7 copy-done.9
  6.1 0.0 copy-start.11
  6.1 2.5 %shard_map.46 = bf16[16,2,3,128,128]{4,3,2,1,0:T(8,128)(2,1)} custom-call(s32[1]{0:T(128)} %bitcast.me_ref, s32[4,128]{1,0:T(4,128)S(1)} %bitcast.4, bf16[2,32,128,128]{3,2,1,0:T(8,128)(2,1)S(1)} %copy-done), custom_call_target="tpu_custom_call" | custom-call | tf_op jit(solution)/shard_map/pallas_call | solution.py:118
  8.6 0.0 collective-permute-done.2
  8.6 0.0 collective-permute-done.1
  8.6 2.0 %collective-permute-done = bf16[1,2,128,128]{3,2,1,0:T(8,128)(2,1)S(1)} collective-permute-done((bf16[1,2,128,128]{3,2,1,0:T(8,128)(2,1)}, bf16[1,2,128,128]{3,2,1,0:T(8,128)(2,1)S(1)}, u32[]{:S(2)}, u32[]{:S(2)}) %collective-permute-start) | collective-permute-done | bytes 65568 | tf_op jit(solution)/shard_map/ppermute | solution.py:114
  10.6 0.0 copy-done.11
  10.6 0.0 copy-start.10
  10.6 6.1 %all-to-all-start = ((bf16[16,2,3,128,128]{4,3,2,1,0:T(8,128)(2,1)}), bf16[16,2,3,128,128]{4,3,2,1,0:T(8,128)(2,1)S(1)}, u32[]{:S(2)}, u32[]{:S(2)}) async-start(bf16[16,2,3,128,128]{4,3,2,1,0:T(8,128)(2,1)} %shard_map.46), calls=%async_computation | async-start | bytes 6291456 | tf_op jit(solution)/shard_map/all_to_all | solution.py:136
  16.8 0.5 collective-permute-start.5
  17.3 1.2 %collective-permute-start.4 = (bf16[4,2,128,128]{3,2,1,0:T(8,128)(2,1)S(1)}, bf16[4,2,128,128]{3,2,1,0:T(8,128)(2,1)S(1)}, u32[]{:S(2)}, u32[]{:S(2)}) collective-permute-start(bf16[4,2,128,128]{3,2,1,0:T(8,128)(2,1)S(1)} %pad_maximum_fusion.rest_0_), channel_id=1, source_target_pairs={{2,0},{3,1},{0,2},{1,3},{6,4},{7,5},{4,6},{5,7},{10,8},{11,9},{8,1... | collective-permute-start | bytes 786440 | tf_op jit(solution)/shard_map/ppermute | solution.py:135
  18.5 0.4 collective-permute-start.3
  18.9 22.2 %collective-permute-done.5.rest_3_ = bf16[4,2,128,128]{3,2,1,0:T(8,128)(2,1)S(1)} collective-permute-done((bf16[4,2,128,128]{3,2,1,0:T(8,128)(2,1)S(1)}, bf16[4,2,128,128]{3,2,1,0:T(8,128)(2,1)S(1)}, u32[]{:S(2)}, u32[]{:S(2)}) %collective-permute-start.5) | collective-permute-done | bytes 262176 | tf_op jit(solution)/shard_map/ppermute | solution.py:135
  41.2 0.0 copy-start.3
  41.2 0.7 copy-done.3
  41.9 4.3 %collective-permute-done.4.rest_2_ = bf16[4,2,128,128]{3,2,1,0:T(8,128)(2,1)S(1)} collective-permute-done((bf16[4,2,128,128]{3,2,1,0:T(8,128)(2,1)S(1)}, bf16[4,2,128,128]{3,2,1,0:T(8,128)(2,1)S(1)}, u32[]{:S(2)}, u32[]{:S(2)}) %collective-permute-start.4) | collective-permute-done | bytes 262176 | tf_op jit(solution)/shard_map/ppermute | solution.py:135
  46.2 0.0 copy-start.5
  46.2 0.7 copy-done.5
  46.9 0.0 collective-permute-done.3.rest_1_
  46.9 0.0 copy-start.7
  46.9 0.7 copy-done.7
  47.6 39.1 %all-to-all-done.recv_ref = bf16[16,2,3,128,128]{4,3,2,1,0:T(8,128)(2,1)S(1)} async-done(((bf16[16,2,3,128,128]{4,3,2,1,0:T(8,128)(2,1)}), bf16[16,2,3,128,128]{4,3,2,1,0:T(8,128)(2,1)S(1)}, u32[]{:S(2)}, u32[]{:S(2)}) %all-to-all-start) | async-done | bytes 3145760 | tf_op jit(solution)/shard_map/all_to_all | solution.py:136
  86.7 0.0 copy-done.10
  86.7 0.0 copy-start.1
  86.7 1.2 %copy-done.1 = bf16[8,4,128,128]{3,2,1,0:T(8,128)(2,1)S(1)} copy-done((bf16[8,4,128,128]{3,2,1,0:T(8,128)(2,1)S(1)}, bf16[8,4,128,128]{3,2,1,0:T(8,128)(2,1)}, u32[]{:S(2)}) %copy-start.1) | copy-done | bytes 1048600
  88.0 0.0 copy-start.2
  88.0 1.0 %copy-done.2 = f32[8,128,128]{2,1,0:T(8,128)S(1)} copy-done((f32[8,128,128]{2,1,0:T(8,128)S(1)}, f32[8,128,128]{2,1,0:T(8,128)}, u32[]{:S(2)}) %copy-start.2) | copy-done | bytes 524312
  89.0 0.0 copy-start.4
  89.0 0.9 copy-done.4
  89.9 0.0 copy-start.6
  89.9 0.9 copy-done.6
  90.9 0.0 copy-start.8
  90.9 0.9 copy-done.8
  91.8 7.6 %shard_map.48 = f32[8,128,128]{2,1,0:T(8,128)} custom-call(s32[1]{0:T(128)} %bitcast.me_ref, s32[4,128]{1,0:T(4,128)S(1)} %bitcast.5, bf16[16,2,3,128,128]{4,3,2,1,0:T(8,128)(2,1)S(1)} %all-to-all-done.recv_ref, bf16[4,2,128,128]{3,2,1,0:T(8,128)(2,1)S(1)} %pad_maximum_fusion.rest_0_, bf16[4,2,128,128]{3,2,1,0:T(8,128)(2,1)S(1)} %copy-done.8, ...), custom_call_target="tpu_custom_call" | custom-call | tf_op jit(solution)/shard_map/pallas_call | solution.py:138
  (1 shorter events, 0.0 us)
Async XLA Ops:
  0.0 5.4 %copy-start = (bf16[2,32,128,128]{3,2,1,0:T(8,128)(2,1)S(1)}, bf16[2,32,128,128]{3,2,1,0:T(8,128)(2,1)}, u32[]{:S(2)}) copy-start(bf16[2,32,128,128]{3,2,1,0:T(8,128)(2,1)} %inv_ref.3) | copy-start | bytes 6291460
  1.6 7.0 %collective-permute-start.2 = (bf16[1,2,128,128]{3,2,1,0:T(8,128)(2,1)}, bf16[1,2,128,128]{3,2,1,0:T(8,128)(2,1)S(1)}, u32[]{:S(2)}, u32[]{:S(2)}) collective-permute-start(bf16[1,2,128,128]{3,2,1,0:T(8,128)(2,1)} %shard_map.47), channel_id=1, source_target_pairs={{12,0},{13,1},{14,2},{15,3},{0,4},{1,5},{2,6},{3,7},{4,8},{5,9},{6... | collective-permute-start | bytes 196616 | tf_op jit(solution)/shard_map/ppermute | solution.py:114
  2.9 5.6 %collective-permute-start.1 = (bf16[1,2,128,128]{3,2,1,0:T(8,128)(2,1)}, bf16[1,2,128,128]{3,2,1,0:T(8,128)(2,1)S(1)}, u32[]{:S(2)}, u32[]{:S(2)}) collective-permute-start(bf16[1,2,128,128]{3,2,1,0:T(8,128)(2,1)} %shard_map.47), channel_id=1, source_target_pairs={{8,0},{9,1},{10,2},{11,3},{12,4},{13,5},{14,6},{15,7},{0,8},{1,9},... | collective-permute-start | bytes 196616 | tf_op jit(solution)/shard_map/ppermute | solution.py:114
  4.0 6.6 %collective-permute-start = (bf16[1,2,128,128]{3,2,1,0:T(8,128)(2,1)}, bf16[1,2,128,128]{3,2,1,0:T(8,128)(2,1)S(1)}, u32[]{:S(2)}, u32[]{:S(2)}) collective-permute-start(bf16[1,2,128,128]{3,2,1,0:T(8,128)(2,1)} %shard_map.47), channel_id=1, source_target_pairs={{4,0},{5,1},{6,2},{7,3},{8,4},{9,5},{10,6},{11,7},{12,8},{13,9},{1... | collective-permute-start | bytes 196616 | tf_op jit(solution)/shard_map/ppermute | solution.py:114
  5.4 0.7 copy-start.9
  6.1 4.5 %copy-start.11 = (bf16[1,2,128,128]{3,2,1,0:T(8,128)(2,1)S(1)}, bf16[1,2,128,128]{3,2,1,0:T(8,128)(2,1)}, u32[]{:S(2)}) copy-start(bf16[1,2,128,128]{3,2,1,0:T(8,128)(2,1)} %shard_map.47) | copy-start | bytes 196612
  10.6 76.1 %copy-start.10 = (s32[128,4]{0,1:T(4,128)S(1)}, s32[128,4]{0,1:T(4,128)}, u32[]{:S(2)}) copy-start(s32[128,4]{0,1:T(4,128)} %param.7) | copy-start | bytes 6148
  10.6 76.1 %all-to-all-start = ((bf16[16,2,3,128,128]{4,3,2,1,0:T(8,128)(2,1)}), bf16[16,2,3,128,128]{4,3,2,1,0:T(8,128)(2,1)S(1)}, u32[]{:S(2)}, u32[]{:S(2)}) async-start(bf16[16,2,3,128,128]{4,3,2,1,0:T(8,128)(2,1)} %shard_map.46), calls=%async_computation | async-start | bytes 6291456 | tf_op jit(solution)/shard_map/all_to_all | solution.py:136
  16.8 24.4 %collective-permute-start.5 = (bf16[4,2,128,128]{3,2,1,0:T(8,128)(2,1)S(1)}, bf16[4,2,128,128]{3,2,1,0:T(8,128)(2,1)S(1)}, u32[]{:S(2)}, u32[]{:S(2)}) collective-permute-start(bf16[4,2,128,128]{3,2,1,0:T(8,128)(2,1)S(1)} %pad_maximum_fusion.rest_0_), channel_id=1, source_target_pairs={{3,0},{2,1},{1,2},{0,3},{7,4},{6,5},{5,6},{4,7},{11,8},{10,9},{9,1... | collective-permute-start | bytes 786440 | tf_op jit(solution)/shard_map/ppermute | solution.py:135
  17.3 28.9 %collective-permute-start.4 = (bf16[4,2,128,128]{3,2,1,0:T(8,128)(2,1)S(1)}, bf16[4,2,128,128]{3,2,1,0:T(8,128)(2,1)S(1)}, u32[]{:S(2)}, u32[]{:S(2)}) collective-permute-start(bf16[4,2,128,128]{3,2,1,0:T(8,128)(2,1)S(1)} %pad_maximum_fusion.rest_0_), channel_id=1, source_target_pairs={{2,0},{3,1},{0,2},{1,3},{6,4},{7,5},{4,6},{5,7},{10,8},{11,9},{8,1... | collective-permute-start | bytes 786440 | tf_op jit(solution)/shard_map/ppermute | solution.py:135
  18.5 28.4 %collective-permute-start.3 = (bf16[4,2,128,128]{3,2,1,0:T(8,128)(2,1)S(1)}, bf16[4,2,128,128]{3,2,1,0:T(8,128)(2,1)S(1)}, u32[]{:S(2)}, u32[]{:S(2)}) collective-permute-start(bf16[4,2,128,128]{3,2,1,0:T(8,128)(2,1)S(1)} %pad_maximum_fusion.rest_0_), channel_id=1, source_target_pairs={{1,0},{0,1},{3,2},{2,3},{5,4},{4,5},{7,6},{6,7},{9,8},{8,9},{11,10... | collective-permute-start | bytes 786440 | tf_op jit(solution)/shard_map/ppermute | solution.py:135
  41.2 0.7 copy-start.3
  46.2 0.7 copy-start.5
  46.9 0.7 copy-start.7
  86.7 1.2 %copy-start.1 = (bf16[8,4,128,128]{3,2,1,0:T(8,128)(2,1)S(1)}, bf16[8,4,128,128]{3,2,1,0:T(8,128)(2,1)}, u32[]{:S(2)}) copy-start(bf16[8,4,128,128]{3,2,1,0:T(8,128)(2,1)} %param.4) | copy-start | bytes 3145732
  88.0 1.0 %copy-start.2 = (f32[8,128,128]{2,1,0:T(8,128)S(1)}, f32[8,128,128]{2,1,0:T(8,128)}, u32[]{:S(2)}) copy-start(f32[8,128,128]{2,1,0:T(8,128)} %rest_5_.1) | copy-start | bytes 1572868
  89.0 0.9 copy-start.4
  89.9 0.9 copy-start.6
  90.9 0.9 copy-start.8

commit v3 on v2

v3 whole, which is shorter than its diff:
```python
import functools

import jax
import jax.numpy as jnp
from jax import lax
from jax.experimental import pallas as pl
from jax.experimental.pallas import tpu as pltpu
from jax.sharding import PartitionSpec as P


def pack_kernel(n, cols, me_ref, st_ref, inv_ref, send_ref, diag_ref, inv_v, send_v, idx_v, idx_s, sem, sem_i, sem_d, sem_o):
    length, total = st_ref.shape
    rows = inv_ref.shape[0]
    others = length - 1
    me = me_ref[0]
    fetch = pltpu.make_async_copy(inv_ref, inv_v, sem)
    fetch.start()
    st = [st_ref[r : r + 1, :] for r in range(length)]
    lines = []
    for j in range(rows):
        row = me * rows + j
        for q in range(others):
            line = jnp.zeros((1, total), jnp.int32)
            for r in range(length):
                line = jnp.where(st[r] == row, st[q if q < r else q + 1], line)
            lines.append(line)
    lines.append(jnp.zeros((idx_v.shape[0] - len(lines), total), jnp.int32))
    picks = jnp.concatenate(lines, axis=0).astype(jnp.float32)
    grid = (total, idx_v.shape[1])
    first = lax.broadcasted_iota(jnp.int32, grid, 1) * cols
    place = lax.broadcasted_iota(jnp.int32, grid, 0)
    group = ((place >= first) & (place < first + cols)).astype(jnp.float32)
    table = jnp.dot(picks, group, preferred_element_type=jnp.float32, precision=lax.Precision.HIGHEST)
    idx_v[...] = table.astype(jnp.int32)
    copy = pltpu.make_async_copy(idx_v, idx_s, sem_i)
    copy.start()
    copy.wait()
    fetch.wait()
    for j in range(rows):
        pltpu.make_async_copy(inv_v.at[j, me * rows + j], diag_ref.at[0, j], sem_d).start()

    def to_device(p, carry):
        for j in range(rows):
            for q in range(others):
                send_v[p, j, q] = inv_v[j, idx_s[j * others + q, p]]
        pltpu.make_async_copy(send_v.at[p], send_ref.at[p], sem_o).start()
        return carry

    lax.fori_loop(0, n, to_device, 0)
    pltpu.make_async_copy(send_v, send_ref, sem_o).wait()
    pltpu.make_async_copy(diag_ref, diag_ref, sem_d).wait()


def level_kernel(quad, me_ref, st_ref, recv_ref, *rest):
    diag_refs, rest = rest[:quad], rest[quad:]
    fac_ref, dfi_ref, out_ref, diag_v, line_v, out_v, sems, sem_o = rest
    cols, deep, width = fac_ref.shape
    length = deep // width
    rows = recv_ref.shape[1]
    steps = diag_refs[0].shape[0]
    me = me_ref[0]
    for k in range(cols):
        for r in range(length):
            anc = st_ref[r, me * cols + k]
            src = recv_ref.at[lax.div(anc, rows), lax.rem(anc, rows)]
            pltpu.make_async_copy(src, line_v.at[k, r], sems.at[k]).start()
    for a in range(quad):
        for t in range(steps):
            owner = lax.bitwise_xor(lax.rem(me + t * quad, steps * quad), a)
            diag_v[pl.ds(owner * rows, rows)] = diag_refs[a][t]
    for k in range(cols):
        fac = fac_ref[k]
        pltpu.make_async_copy(line_v.at[k], line_v.at[k], sems.at[k]).wait()
        product = []
        for r in range(length):
            anc = st_ref[r, me * cols + k]
            line = [diag_v[anc] if s == r else line_v[k, r, s if s < r else s - 1] for s in range(length)]
            line = jnp.concatenate(line, axis=1)
            product.append(jnp.dot(line, fac, preferred_element_type=jnp.float32).astype(jnp.bfloat16))
        product = jnp.concatenate(product, axis=0)
        term = lax.dot_general(fac, product, (((0,), (0,)), ((), ())), preferred_element_type=jnp.float32)
        out_v[k] = dfi_ref[k] + term
        pltpu.make_async_copy(out_v.at[k], out_ref.at[k], sem_o).start()
    pltpu.make_async_copy(out_v, out_ref, sem_o).wait()


def shards(n, factor_blocks, inverse_blocks, diag_factor_inv, structure):
    cols, length, width, _ = factor_blocks.shape
    rows, ancestors = inverse_blocks.shape[:2]
    total = structure.shape[0]
    me = lax.axis_index("prow").astype(jnp.int32)
    me1 = me.reshape(1)
    smem = pl.BlockSpec(memory_space=pltpu.SMEM)
    vmem = pl.BlockSpec(memory_space=pltpu.VMEM)
    hbm = pl.BlockSpec(memory_space=pltpu.HBM)
    quad = 4
    steps = n // quad

    lines = -(-rows * (length - 1) // 8) * 8
    lanes = -(-n // 128) * 128
    send, diag = pl.pallas_call(
        functools.partial(pack_kernel, n, cols),
        out_shape=(
            jax.ShapeDtypeStruct((n, rows, length - 1, width, width), jnp.bfloat16),
            jax.ShapeDtypeStruct((1, rows, width, width), jnp.bfloat16),
        ),
        in_specs=[smem, vmem, hbm],
        out_specs=(hbm, hbm),
        scratch_shapes=[
            pltpu.VMEM(inverse_blocks.shape, jnp.bfloat16),
            pltpu.VMEM((n, rows, length - 1, width, width), jnp.bfloat16),
            pltpu.VMEM((lines, lanes), jnp.int32),
            pltpu.SMEM((lines, lanes), jnp.int32),
            pltpu.SemaphoreType.DMA,
            pltpu.SemaphoreType.DMA,
            pltpu.SemaphoreType.DMA,
            pltpu.SemaphoreType.DMA,
        ],
        compiler_params=pltpu.CompilerParams(vmem_limit_bytes=56 * 2**20),
    )(me1, structure.T, inverse_blocks)
    recv = lax.all_to_all(send, "prow", split_axis=0, concat_axis=0, tiled=True)
    held = [diag]
    for t in range(1, steps):
        held.append(lax.ppermute(diag, "prow", [((i + t * quad) % n, i) for i in range(n)]))
    held = jnp.concatenate(held, axis=0)
    spread = [held]
    for a in range(1, quad):
        spread.append(lax.ppermute(held, "prow", [(i ^ a, i) for i in range(n)]))
    deep = length * width
    return pl.pallas_call(
        functools.partial(level_kernel, quad),
        out_shape=jax.ShapeDtypeStruct((cols, width, width), jnp.float32),
        in_specs=[smem, smem, hbm] + [vmem] * (quad + 2),
        out_specs=hbm,
        scratch_shapes=[
            pltpu.VMEM((ancestors, width, width), jnp.bfloat16),
            pltpu.VMEM((cols, length, length - 1, width, width), jnp.bfloat16),
            pltpu.VMEM((cols, width, width), jnp.float32),
            pltpu.SemaphoreType.DMA((cols,)),
            pltpu.SemaphoreType.DMA,
        ],
        compiler_params=pltpu.CompilerParams(vmem_limit_bytes=51 * 2**20),
    )(me1, structure.T, recv, *spread, factor_blocks.reshape(cols, deep, width), diag_factor_inv)


def solution(mesh):
    placed = (
        P(("pole", "prow"), None, None, None),
        P(("pole", "prow"), None, None, None),
        P(("pole", "prow"), None, None),
        P(),
    )
    return jax.shard_map(
        functools.partial(shards, mesh.shape["prow"]),
        mesh=mesh,
        in_specs=placed,
        out_specs=P(("pole", "prow"), None, None),
        check_vma=False,
    )
```

time: 99.9 us -> 108 us (1.081); the launches traced: 99.5 us -> 106 us
  waiting for transfers between devices: 67.7 us -> 83.8 us
  local copies, waits for them, and re-layouts: 7.91 us -> 0.07 us
  Pallas kernels: 11.7 us -> 9.91 us
    ppermute x3, waiting for transfers between devices: 2.02 us -> 71.7 us  [shards(): lax.ppermute(diag, 'prow', [((i + t * quad) % n, i) for i in range(n)])]
    all_to_all x1, waiting for transfers between devices: 39.1 us -> 0.01 us  [shards(): recv = lax.all_to_all(send, 'prow', split_axis=0, concat_axis=0, tiled=True)]
    ppermute x3, waiting for transfers between devices: 26.5 us -> 12.1 us  [shards(): spread.append(lax.ppermute(held, 'prow', [(i ^ a, i) for i in range(n)]))]
    unnamed x24 -> x11, local copies, waits for them, and re-layouts: 7.91 us -> 0.06 us
    pallas_call x1, Pallas kernels: 7.63 us -> 5.95 us  [shards(): pl.pallas_call(functools.partial(level_kernel, quad), out_shape=jax.Shape...]
    pallas_call x2 -> x1, Pallas kernels: 4.02 us -> 3.96 us  [shards(): pl.pallas_call(functools.partial(pack_kernel, n, cols), out_shape=(jax.Sh...]
  transfers between devices with their start and end apart: 7 -> 7, of which waited for: 4 -> 3; matrix products, arithmetic and copies ran while one was open for 0% -> 0% of each run, Pallas kernels for 2% -> 0%
where the time goes in v3:
time: 108 us; the launch traced here: 106 us
  waiting for transfers between devices  83.8 us (78%)
  starting transfers between devices  12.6 us (12%)
  Pallas kernels  9.91 us (9%)
    ppermute x3, waiting for transfers between devices, shards(): lax.ppermute(diag, 'prow', [((i + t * quad) % n, i) for i in range(n)])  71.7 us
    ppermute x3, waiting for transfers between devices, shards(): spread.append(lax.ppermute(held, 'prow', [(i ^ a, i) for i in range(n)]))  12.1 us
    all_to_all x1, starting transfers between devices, shards(): recv = lax.all_to_all(send, 'prow', split_axis=0, concat_axis=0, tiled=True)  6.7 us
    pallas_call x1, Pallas kernels, shards(): pl.pallas_call(functools.partial(level_kernel, quad), out_shape=jax.Shape...  5.95 us
    pallas_call x1, Pallas kernels, shards(): pl.pallas_call(functools.partial(pack_kernel, n, cols), out_shape=(jax.Sh...  3.96 us
    ppermute x3, starting transfers between devices, shards(): lax.ppermute(diag, 'prow', [((i + t * quad) % n, i) for i in range(n)])  3.6 us
    ppermute x3, starting transfers between devices, shards(): spread.append(lax.ppermute(held, 'prow', [(i ^ a, i) for i in range(n)]))  2.29 us
  transfers between devices with their start and end apart: 7, of which 3 were waited for; matrix products, arithmetic and copies ran while one was open for 0% of the time, Pallas kernels for 0%

profile of v3, /device:TPU:13, one launch (start us, length us, event | category | flops | bytes accessed | tf_op | source)
XLA Modules:
  0.0 106.5 jit_solution(17187688431571689692)
XLA Ops:
  0.0 4.0 %shard_map.46 = (bf16[16,2,3,128,128]{4,3,2,1,0:T(8,128)(2,1)}, bf16[1,2,128,128]{3,2,1,0:T(8,128)(2,1)}) custom-call(s32[1]{0:T(128)} %bitcast.me_ref, s32[4,128]{1,0:T(4,128)} %bitcast.4, bf16[2,32,128,128]{3,2,1,0:T(8,128)(2,1)} %inv_ref.1), custom_call_target="tpu_custom_call" | custom-call | tf_op jit(solution)/shard_map/pallas_call | solution.py:101
  4.0 0.0 copy-start.3
  4.0 0.0 copy-start
  4.0 0.0 copy-start.1
  4.0 0.0 copy-start.2
  4.0 6.7 %all-to-all-start = ((bf16[16,2,3,128,128]{4,3,2,1,0:T(8,128)(2,1)}), bf16[16,2,3,128,128]{4,3,2,1,0:T(8,128)(2,1)}, u32[]{:S(2)}, u32[]{:S(2)}) async-start(bf16[16,2,3,128,128]{4,3,2,1,0:T(8,128)(2,1)} %get-tuple-element.7), calls=%async_computation | async-start | bytes 6291456 | tf_op jit(solution)/shard_map/all_to_all | solution.py:121
  10.7 0.0 copy-done.3
  10.7 1.2 %collective-permute-start.2 = (bf16[1,2,128,128]{3,2,1,0:T(8,128)(2,1)S(1)}, bf16[1,2,128,128]{3,2,1,0:T(8,128)(2,1)S(1)}, u32[]{:S(2)}, u32[]{:S(2)}) collective-permute-start(bf16[1,2,128,128]{3,2,1,0:T(8,128)(2,1)S(1)} %copy-done.3), channel_id=1, source_target_pairs={{12,0},{13,1},{14,2},{15,3},{0,4},{1,5},{2,6},{3,7},{4,8},{5,9},{6... | collective-permute-start | bytes 196616 | tf_op jit(solution)/shard_map/ppermute | solution.py:124
  12.0 1.2 %collective-permute-start.1 = (bf16[1,2,128,128]{3,2,1,0:T(8,128)(2,1)S(1)}, bf16[1,2,128,128]{3,2,1,0:T(8,128)(2,1)S(1)}, u32[]{:S(2)}, u32[]{:S(2)}) collective-permute-start(bf16[1,2,128,128]{3,2,1,0:T(8,128)(2,1)S(1)} %copy-done.3), channel_id=1, source_target_pairs={{8,0},{9,1},{10,2},{11,3},{12,4},{13,5},{14,6},{15,7},{0,8},{1,9},... | collective-permute-start | bytes 196616 | tf_op jit(solution)/shard_map/ppermute | solution.py:124
  13.1 1.2 %collective-permute-start = (bf16[1,2,128,128]{3,2,1,0:T(8,128)(2,1)S(1)}, bf16[1,2,128,128]{3,2,1,0:T(8,128)(2,1)S(1)}, u32[]{:S(2)}, u32[]{:S(2)}) collective-permute-start(bf16[1,2,128,128]{3,2,1,0:T(8,128)(2,1)S(1)} %copy-done.3), channel_id=1, source_target_pairs={{4,0},{5,1},{6,2},{7,3},{8,4},{9,5},{10,6},{11,7},{12,8},{13,9},{1... | collective-permute-start | bytes 196616 | tf_op jit(solution)/shard_map/ppermute | solution.py:124
  14.3 71.7 %collective-permute-done = bf16[1,2,128,128]{3,2,1,0:T(8,128)(2,1)S(1)} collective-permute-done((bf16[1,2,128,128]{3,2,1,0:T(8,128)(2,1)S(1)}, bf16[1,2,128,128]{3,2,1,0:T(8,128)(2,1)S(1)}, u32[]{:S(2)}, u32[]{:S(2)}) %collective-permute-start) | collective-permute-done | bytes 65568 | tf_op jit(solution)/shard_map/ppermute | solution.py:124
  86.1 0.0 collective-permute-done.1
  86.1 0.0 collective-permute-done.2
  86.1 1.1 %collective-permute-start.5 = (bf16[4,2,128,128]{3,2,1,0:T(8,128)(2,1)S(1)}, bf16[4,2,128,128]{3,2,1,0:T(8,128)(2,1)S(1)}, u32[]{:S(2)}, u32[]{:S(2)}) collective-permute-start(bf16[4,2,128,128]{3,2,1,0:T(8,128)(2,1)S(1)} %constant_dynamic-update-slice_fusion.rest_0_), channel_id=1, source_target_pairs={{3,0},{2,1},{1,2},{0,3},{7,4},{6,5},{5,6},{4,7},{11,8},{10,9},{9,1... | collective-permute-start | bytes 786440 | tf_op jit(solution)/shard_map/ppermute | solution.py:128
  87.2 1.2 %collective-permute-start.4 = (bf16[4,2,128,128]{3,2,1,0:T(8,128)(2,1)S(1)}, bf16[4,2,128,128]{3,2,1,0:T(8,128)(2,1)S(1)}, u32[]{:S(2)}, u32[]{:S(2)}) collective-permute-start(bf16[4,2,128,128]{3,2,1,0:T(8,128)(2,1)S(1)} %constant_dynamic-update-slice_fusion.rest_0_), channel_id=1, source_target_pairs={{2,0},{3,1},{0,2},{1,3},{6,4},{7,5},{4,6},{5,7},{10,8},{11,9},{8,1... | collective-permute-start | bytes 786440 | tf_op jit(solution)/shard_map/ppermute | solution.py:128
  88.4 0.0 collective-permute-start.3
  88.4 6.5 %collective-permute-done.5.rest_3_ = bf16[4,2,128,128]{3,2,1,0:T(8,128)(2,1)S(1)} collective-permute-done((bf16[4,2,128,128]{3,2,1,0:T(8,128)(2,1)S(1)}, bf16[4,2,128,128]{3,2,1,0:T(8,128)(2,1)S(1)}, u32[]{:S(2)}, u32[]{:S(2)}) %collective-permute-start.5) | collective-permute-done | bytes 262176 | tf_op jit(solution)/shard_map/ppermute | solution.py:128
  94.9 5.6 %collective-permute-done.4.rest_2_ = bf16[4,2,128,128]{3,2,1,0:T(8,128)(2,1)S(1)} collective-permute-done((bf16[4,2,128,128]{3,2,1,0:T(8,128)(2,1)S(1)}, bf16[4,2,128,128]{3,2,1,0:T(8,128)(2,1)S(1)}, u32[]{:S(2)}, u32[]{:S(2)}) %collective-permute-start.4) | collective-permute-done | bytes 262176 | tf_op jit(solution)/shard_map/ppermute | solution.py:128
  100.5 0.0 collective-permute-done.3.rest_1_
  100.5 0.0 all-to-all-done.recv_ref
  100.5 0.0 copy-done
  100.5 0.0 copy-done.1
  100.5 0.0 copy-done.2
  100.5 5.9 %shard_map.47 = f32[8,128,128]{2,1,0:T(8,128)} custom-call(s32[1]{0:T(128)} %bitcast.me_ref, s32[4,128]{1,0:T(4,128)S(1)} %bitcast.5, bf16[16,2,3,128,128]{4,3,2,1,0:T(8,128)(2,1)} %all-to-all-done.recv_ref, bf16[4,2,128,128]{3,2,1,0:T(8,128)(2,1)S(1)} %constant_dynamic-update-slice_fusion.rest_0_, ...), custom_call_target="tpu_custom_call" | custom-call | tf_op jit(solution)/shard_map/pallas_call | solution.py:130
  (4 shorter events, 0.0 us)
Async XLA Ops:
  4.0 6.7 %copy-start.3 = (bf16[1,2,128,128]{3,2,1,0:T(8,128)(2,1)S(1)}, bf16[1,2,128,128]{3,2,1,0:T(8,128)(2,1)}, u32[]{:S(2)}) copy-start(bf16[1,2,128,128]{3,2,1,0:T(8,128)(2,1)} %get-tuple-element.8) | copy-start | bytes 196612
  4.0 96.5 %copy-start = (bf16[8,4,128,128]{3,2,1,0:T(8,128)(2,1)S(1)}, bf16[8,4,128,128]{3,2,1,0:T(8,128)(2,1)}, u32[]{:S(2)}) copy-start(bf16[8,4,128,128]{3,2,1,0:T(8,128)(2,1)} %param.4) | copy-start | bytes 3145732
  4.0 96.5 %copy-start.1 = (f32[8,128,128]{2,1,0:T(8,128)S(1)}, f32[8,128,128]{2,1,0:T(8,128)}, u32[]{:S(2)}) copy-start(f32[8,128,128]{2,1,0:T(8,128)} %rest_5_.1) | copy-start | bytes 1572868
  4.0 96.5 %copy-start.2 = (s32[128,4]{0,1:T(4,128)S(1)}, s32[128,4]{0,1:T(4,128)}, u32[]{:S(2)}) copy-start(s32[128,4]{0,1:T(4,128)} %param.7) | copy-start | bytes 6148
  4.0 96.5 %all-to-all-start = ((bf16[16,2,3,128,128]{4,3,2,1,0:T(8,128)(2,1)}), bf16[16,2,3,128,128]{4,3,2,1,0:T(8,128)(2,1)}, u32[]{:S(2)}, u32[]{:S(2)}) async-start(bf16[16,2,3,128,128]{4,3,2,1,0:T(8,128)(2,1)} %get-tuple-element.7), calls=%async_computation | async-start | bytes 6291456 | tf_op jit(solution)/shard_map/all_to_all | solution.py:121
  10.7 75.4 %collective-permute-start.2 = (bf16[1,2,128,128]{3,2,1,0:T(8,128)(2,1)S(1)}, bf16[1,2,128,128]{3,2,1,0:T(8,128)(2,1)S(1)}, u32[]{:S(2)}, u32[]{:S(2)}) collective-permute-start(bf16[1,2,128,128]{3,2,1,0:T(8,128)(2,1)S(1)} %copy-done.3), channel_id=1, source_target_pairs={{12,0},{13,1},{14,2},{15,3},{0,4},{1,5},{2,6},{3,7},{4,8},{5,9},{6... | collective-permute-start | bytes 196616 | tf_op jit(solution)/shard_map/ppermute | solution.py:124
  12.0 74.1 %collective-permute-start.1 = (bf16[1,2,128,128]{3,2,1,0:T(8,128)(2,1)S(1)}, bf16[1,2,128,128]{3,2,1,0:T(8,128)(2,1)S(1)}, u32[]{:S(2)}, u32[]{:S(2)}) collective-permute-start(bf16[1,2,128,128]{3,2,1,0:T(8,128)(2,1)S(1)} %copy-done.3), channel_id=1, source_target_pairs={{8,0},{9,1},{10,2},{11,3},{12,4},{13,5},{14,6},{15,7},{0,8},{1,9},... | collective-permute-start | bytes 196616 | tf_op jit(solution)/shard_map/ppermute | solution.py:124
  13.1 72.9 %collective-permute-start = (bf16[1,2,128,128]{3,2,1,0:T(8,128)(2,1)S(1)}, bf16[1,2,128,128]{3,2,1,0:T(8,128)(2,1)S(1)}, u32[]{:S(2)}, u32[]{:S(2)}) collective-permute-start(bf16[1,2,128,128]{3,2,1,0:T(8,128)(2,1)S(1)} %copy-done.3), channel_id=1, source_target_pairs={{4,0},{5,1},{6,2},{7,3},{8,4},{9,5},{10,6},{11,7},{12,8},{13,9},{1... | collective-permute-start | bytes 196616 | tf_op jit(solution)/shard_map/ppermute | solution.py:124
  86.1 8.8 %collective-permute-start.5 = (bf16[4,2,128,128]{3,2,1,0:T(8,128)(2,1)S(1)}, bf16[4,2,128,128]{3,2,1,0:T(8,128)(2,1)S(1)}, u32[]{:S(2)}, u32[]{:S(2)}) collective-permute-start(bf16[4,2,128,128]{3,2,1,0:T(8,128)(2,1)S(1)} %constant_dynamic-update-slice_fusion.rest_0_), channel_id=1, source_target_pairs={{3,0},{2,1},{1,2},{0,3},{7,4},{6,5},{5,6},{4,7},{11,8},{10,9},{9,1... | collective-permute-start | bytes 786440 | tf_op jit(solution)/shard_map/ppermute | solution.py:128
  87.2 13.3 %collective-permute-start.4 = (bf16[4,2,128,128]{3,2,1,0:T(8,128)(2,1)S(1)}, bf16[4,2,128,128]{3,2,1,0:T(8,128)(2,1)S(1)}, u32[]{:S(2)}, u32[]{:S(2)}) collective-permute-start(bf16[4,2,128,128]{3,2,1,0:T(8,128)(2,1)S(1)} %constant_dynamic-update-slice_fusion.rest_0_), channel_id=1, source_target_pairs={{2,0},{3,1},{0,2},{1,3},{6,4},{7,5},{4,6},{5,7},{10,8},{11,9},{8,1... | collective-permute-start | bytes 786440 | tf_op jit(solution)/shard_map/ppermute | solution.py:128
  88.4 12.1 %collective-permute-start.3 = (bf16[4,2,128,128]{3,2,1,0:T(8,128)(2,1)S(1)}, bf16[4,2,128,128]{3,2,1,0:T(8,128)(2,1)S(1)}, u32[]{:S(2)}, u32[]{:S(2)}) collective-permute-start(bf16[4,2,128,128]{3,2,1,0:T(8,128)(2,1)S(1)} %constant_dynamic-update-slice_fusion.rest_0_), channel_id=1, source_target_pairs={{1,0},{0,1},{3,2},{2,3},{5,4},{4,5},{7,6},{6,7},{9,8},{8,9},{11,10... | collective-permute-start | bytes 786440 | tf_op jit(solution)/shard_map/ppermute | solution.py:128

commit v4 on v3

--- a/solution.py
+++ b/solution.py
@@ -8,13 +8,19 @@
 from jax.sharding import PartitionSpec as P
 
 
-def pack_kernel(n, cols, me_ref, st_ref, inv_ref, send_ref, diag_ref, inv_v, send_v, idx_v, idx_s, sem, sem_i, sem_d, sem_o):
+def diag_kernel(me_ref, inv_ref, diag_ref, sem):
+    rows = inv_ref.shape[0]
+    for j in range(rows):
+        pltpu.make_async_copy(inv_ref.at[j, me_ref[0] * rows + j], diag_ref.at[0, j], sem.at[j]).start()
+    for j in range(rows):
+        pltpu.make_async_copy(inv_ref.at[j, 0], diag_ref.at[0, j], sem.at[j]).wait()
+
+
+def pack_kernel(n, cols, me_ref, st_ref, inv_ref, send_ref, send_v, idx_v, idx_s, sem_i, sem_o):
     length, total = st_ref.shape
     rows = inv_ref.shape[0]
     others = length - 1
     me = me_ref[0]
-    fetch = pltpu.make_async_copy(inv_ref, inv_v, sem)
-    fetch.start()
     st = [st_ref[r : r + 1, :] for r in range(length)]
     lines = []
     for j in range(rows):
@@ -35,20 +41,16 @@
     copy = pltpu.make_async_copy(idx_v, idx_s, sem_i)
     copy.start()
     copy.wait()
-    fetch.wait()
-    for j in range(rows):
-        pltpu.make_async_copy(inv_v.at[j, me * rows + j], diag_ref.at[0, j], sem_d).start()
 
     def to_device(p, carry):
         for j in range(rows):
             for q in range(others):
-                send_v[p, j, q] = inv_v[j, idx_s[j * others + q, p]]
+                send_v[p, j, q] = inv_ref[j, idx_s[j * others + q, p]]
         pltpu.make_async_copy(send_v.at[p], send_ref.at[p], sem_o).start()
         return carry
 
     lax.fori_loop(0, n, to_device, 0)
     pltpu.make_async_copy(send_v, send_ref, sem_o).wait()
-    pltpu.make_async_copy(diag_ref, diag_ref, sem_d).wait()
 
 
 def level_kernel(quad, me_ref, st_ref, recv_ref, *rest):
@@ -93,35 +95,36 @@
     smem = pl.BlockSpec(memory_space=pltpu.SMEM)
     vmem = pl.BlockSpec(memory_space=pltpu.VMEM)
     hbm = pl.BlockSpec(memory_space=pltpu.HBM)
-    quad = 4
+    quad = 8
     steps = n // quad
 
+    diag = pl.pallas_call(
+        diag_kernel,
+        out_shape=jax.ShapeDtypeStruct((1, rows, width, width), jnp.bfloat16),
+        in_specs=[smem, hbm],
+        out_specs=vmem,
+        scratch_shapes=[pltpu.SemaphoreType.DMA((rows,))],
+    )(me1, inverse_blocks)
+    came = [lax.ppermute(diag, "prow", [((i + t * quad) % n, i) for i in range(n)]) for t in range(1, steps)]
     lines = -(-rows * (length - 1) // 8) * 8
     lanes = -(-n // 128) * 128
-    send, diag = pl.pallas_call(
+    send = pl.pallas_call(
         functools.partial(pack_kernel, n, cols),
-        out_shape=(
-            jax.ShapeDtypeStruct((n, rows, length - 1, width, width), jnp.bfloat16),
-            jax.ShapeDtypeStruct((1, rows, width, width), jnp.bfloat16),
-        ),
-        in_specs=[smem, vmem, hbm],
-        out_specs=(hbm, hbm),
+        out_shape=jax.ShapeDtypeStruct((n, rows, length - 1, width, width), jnp.bfloat16),
+        in_specs=[smem, vmem, vmem],
+        out_specs=hbm,
         scratch_shapes=[
-            pltpu.VMEM(inverse_blocks.shape, jnp.bfloat16),
             pltpu.VMEM((n, rows, length - 1, width, width), jnp.bfloat16),
             pltpu.VMEM((lines, lanes), jnp.int32),
             pltpu.SMEM((lines, lanes), jnp.int32),
             pltpu.SemaphoreType.DMA,
             pltpu.SemaphoreType.DMA,
-            pltpu.SemaphoreType.DMA,
-            pltpu.SemaphoreType.DMA,
         ],
-        compiler_params=pltpu.CompilerParams(vmem_limit_bytes=56 * 2**20),
+        compiler_params=pltpu.CompilerParams(vmem_limit_bytes=40 * 2**20),
     )(me1, structure.T, inverse_blocks)
+    send, *came = lax.optimization_barrier((send, *came))
     recv = lax.all_to_all(send, "prow", split_axis=0, concat_axis=0, tiled=True)
-    held = [diag]
-    for t in range(1, steps):
-        held.append(lax.ppermute(diag, "prow", [((i + t * quad) % n, i) for i in range(n)]))
+    held = [diag] + came
     held = jnp.concatenate(held, axis=0)
     spread = [held]
     for a in range(1, quad):

time: 108 us -> 91.9 us (0.85)
  waiting for transfers between devices: 83.8 us -> 62.7 us
  starting transfers between devices: 12.6 us -> 17 us
    ppermute x3 -> x1, waiting for transfers between devices: 71.7 us -> 0.01 us  [shards(): lax.ppermute(diag, 'prow', [((i + t * quad) % n, i) for i in range(n)])]
    ppermute x3 -> x7, waiting for transfers between devices: 12.1 us -> 56.8 us  [shards(): spread.append(lax.ppermute(held, 'prow', [(i ^ a, i) for i in range(n)]))]
    all_to_all x1, waiting for transfers between devices: 0.01 us -> 5.89 us  [shards(): recv = lax.all_to_all(send, 'prow', split_axis=0, concat_axis=0, tiled=True)]
    ppermute x3 -> x7, starting transfers between devices: 2.29 us -> 7.36 us  [shards(): spread.append(lax.ppermute(held, 'prow', [(i ^ a, i) for i in range(n)]))]
    ppermute x3 -> x1, starting transfers between devices: 3.6 us -> 2.37 us  [shards(): lax.ppermute(diag, 'prow', [((i + t * quad) % n, i) for i in range(n)])]
    pallas_call x1 -> x2, Pallas kernels: 3.96 us -> 4.06 us  [the longest x1 2.49 us: shards(): pl.pallas_call(functools.partial(pack_kernel, n, cols), out_shape=jax.Sha...]
  transfers between devices with their start and end apart: 7 -> 9, of which waited for: 3 -> 5; matrix products, arithmetic and copies ran while one was open for 0% -> 0% of each run, Pallas kernels for 0% -> 3%
where the time goes in v4:
time: 91.9 us; the launch traced here: 90.5 us
  waiting for transfers between devices  62.7 us (68%)
  starting transfers between devices  17 us (18%)
  Pallas kernels  9.98 us (11%)
    ppermute x7, waiting for transfers between devices, shards(): spread.append(lax.ppermute(held, 'prow', [(i ^ a, i) for i in range(n)]))  56.8 us
    ppermute x7, starting transfers between devices, shards(): spread.append(lax.ppermute(held, 'prow', [(i ^ a, i) for i in range(n)]))  7.36 us
    all_to_all x1, starting transfers between devices, shards(): recv = lax.all_to_all(send, 'prow', split_axis=0, concat_axis=0, tiled=True)  7.24 us
    pallas_call x1, Pallas kernels, shards(): pl.pallas_call(functools.partial(level_kernel, quad), out_shape=jax.Shape...  5.92 us
    all_to_all x1, waiting for transfers between devices, shards(): recv = lax.all_to_all(send, 'prow', split_axis=0, concat_axis=0, tiled=True)  5.89 us
    pallas_call x1, Pallas kernels, shards(): pl.pallas_call(functools.partial(pack_kernel, n, cols), out_shape=jax.Sha...  2.49 us
    ppermute x1, starting transfers between devices, shards(): lax.ppermute(diag, 'prow', [((i + t * quad) % n, i) for i in range(n)])  2.37 us
  transfers between devices with their start and end apart: 9, of which 5 were waited for; matrix products, arithmetic and copies ran while one was open for 0% of the time, Pallas kernels for 3%

profile of v4, /device:TPU:13, one launch (start us, length us, event | category | flops | bytes accessed | tf_op | source)
XLA Modules:
  0.0 90.5 jit_solution(6157242306869838540)
XLA Ops:
  0.0 0.0 copy-start
  0.0 1.6 %shard_map.47 = bf16[1,2,128,128]{3,2,1,0:T(8,128)(2,1)} custom-call(s32[1]{0:T(128)} %bitcast.me_ref, bf16[2,32,128,128]{3,2,1,0:T(8,128)(2,1)} %inv_ref.3), custom_call_target="tpu_custom_call" | custom-call | tf_op jit(solution)/shard_map/pallas_call | solution.py:101
  1.6 2.4 %collective-permute-start = (bf16[1,2,128,128]{3,2,1,0:T(8,128)(2,1)}, bf16[1,2,128,128]{3,2,1,0:T(8,128)(2,1)S(1)}, u32[]{:S(2)}, u32[]{:S(2)}) collective-permute-start(bf16[1,2,128,128]{3,2,1,0:T(8,128)(2,1)} %shard_map.47), channel_id=1, source_target_pairs={{8,0},{9,1},{10,2},{11,3},{12,4},{13,5},{14,6},{15,7},{0,8},{1,9},... | collective-permute-start | bytes 196616 | tf_op jit(solution)/shard_map/ppermute | solution.py:108
  4.0 0.0 copy-done
  4.0 0.0 copy-start.3
  4.0 0.7 copy-done.3
  4.6 2.5 %shard_map.46 = bf16[16,2,3,128,128]{4,3,2,1,0:T(8,128)(2,1)} custom-call(s32[1]{0:T(128)} %bitcast.me_ref, s32[4,128]{1,0:T(4,128)S(1)} %bitcast.4, bf16[2,32,128,128]{3,2,1,0:T(8,128)(2,1)S(1)} %copy-done), custom_call_target="tpu_custom_call" | custom-call | tf_op jit(solution)/shard_map/pallas_call | solution.py:111
  7.1 0.0 copy-start.5
  7.1 0.0 copy-start.1
  7.2 0.0 copy-start.2
  7.2 0.0 copy-start.4
  7.2 0.0 collective-permute-done
  7.2 7.2 %all-to-all-start = ((bf16[16,2,3,128,128]{4,3,2,1,0:T(8,128)(2,1)}), bf16[16,2,3,128,128]{4,3,2,1,0:T(8,128)(2,1)}, u32[]{:S(2)}, u32[]{:S(2)}) async-start(bf16[16,2,3,128,128]{4,3,2,1,0:T(8,128)(2,1)} %shard_map.46), calls=%async_computation | async-start | bytes 6291456 | tf_op jit(solution)/shard_map/all_to_all | solution.py:126
  14.4 0.0 copy-done.5
  14.5 0.2 collective-permute-start.7
  14.7 2.5 %collective-permute-start.6 = (bf16[2,2,128,128]{3,2,1,0:T(8,128)(2,1)S(1)}, bf16[2,2,128,128]{3,2,1,0:T(8,128)(2,1)S(1)}, u32[]{:S(2)}, u32[]{:S(2)}) collective-permute-start(bf16[2,2,128,128]{3,2,1,0:T(8,128)(2,1)S(1)} %pad_maximum_fusion.rest_0_), channel_id=1, source_target_pairs={{6,0},{7,1},{4,2},{5,3},{2,4},{3,5},{0,6},{1,7},{14,8},{15,9},{12,... | collective-permute-start | bytes 393224 | tf_op jit(solution)/shard_map/ppermute | solution.py:131
  17.1 0.6 collective-permute-start.5
  17.7 1.2 %collective-permute-start.4 = (bf16[2,2,128,128]{3,2,1,0:T(8,128)(2,1)S(1)}, bf16[2,2,128,128]{3,2,1,0:T(8,128)(2,1)S(1)}, u32[]{:S(2)}, u32[]{:S(2)}) collective-permute-start(bf16[2,2,128,128]{3,2,1,0:T(8,128)(2,1)S(1)} %pad_maximum_fusion.rest_0_), channel_id=1, source_target_pairs={{4,0},{5,1},{6,2},{7,3},{0,4},{1,5},{2,6},{3,7},{12,8},{13,9},{14,... | collective-permute-start | bytes 393224 | tf_op jit(solution)/shard_map/ppermute | solution.py:131
  18.9 0.5 collective-permute-start.3
  19.4 51.0 %collective-permute-done.7.rest_7_ = bf16[2,2,128,128]{3,2,1,0:T(8,128)(2,1)S(1)} collective-permute-done((bf16[2,2,128,128]{3,2,1,0:T(8,128)(2,1)S(1)}, bf16[2,2,128,128]{3,2,1,0:T(8,128)(2,1)S(1)}, u32[]{:S(2)}, u32[]{:S(2)}) %collective-permute-start.7) | collective-permute-done | bytes 131104 | tf_op jit(solution)/shard_map/ppermute | solution.py:131
  70.5 1.6 %collective-permute-start.2 = (bf16[2,2,128,128]{3,2,1,0:T(8,128)(2,1)S(1)}, bf16[2,2,128,128]{3,2,1,0:T(8,128)(2,1)S(1)}, u32[]{:S(2)}, u32[]{:S(2)}) collective-permute-start(bf16[2,2,128,128]{3,2,1,0:T(8,128)(2,1)S(1)} %pad_maximum_fusion.rest_0_), channel_id=1, source_target_pairs={{2,0},{3,1},{0,2},{1,3},{6,4},{7,5},{4,6},{5,7},{10,8},{11,9},{8,1... | collective-permute-start | bytes 393224 | tf_op jit(solution)/shard_map/ppermute | solution.py:131
  72.1 1.1 %collective-permute-done.6.rest_6_ = bf16[2,2,128,128]{3,2,1,0:T(8,128)(2,1)S(1)} collective-permute-done((bf16[2,2,128,128]{3,2,1,0:T(8,128)(2,1)S(1)}, bf16[2,2,128,128]{3,2,1,0:T(8,128)(2,1)S(1)}, u32[]{:S(2)}, u32[]{:S(2)}) %collective-permute-start.6) | collective-permute-done | bytes 131104 | tf_op jit(solution)/shard_map/ppermute | solution.py:131
  73.1 0.8 collective-permute-start.1
  73.9 2.6 %collective-permute-done.5.rest_5_ = bf16[2,2,128,128]{3,2,1,0:T(8,128)(2,1)S(1)} collective-permute-done((bf16[2,2,128,128]{3,2,1,0:T(8,128)(2,1)S(1)}, bf16[2,2,128,128]{3,2,1,0:T(8,128)(2,1)S(1)}, u32[]{:S(2)}, u32[]{:S(2)}) %collective-permute-start.5) | collective-permute-done | bytes 131104 | tf_op jit(solution)/shard_map/ppermute | solution.py:131
  76.5 2.2 %collective-permute-done.4.rest_4_ = bf16[2,2,128,128]{3,2,1,0:T(8,128)(2,1)S(1)} collective-permute-done((bf16[2,2,128,128]{3,2,1,0:T(8,128)(2,1)S(1)}, bf16[2,2,128,128]{3,2,1,0:T(8,128)(2,1)S(1)}, u32[]{:S(2)}, u32[]{:S(2)}) %collective-permute-start.4) | collective-permute-done | bytes 131104 | tf_op jit(solution)/shard_map/ppermute | solution.py:131
  78.7 0.0 collective-permute-done.3.rest_3_
  78.7 0.0 collective-permute-done.2.rest_2_
  78.7 0.0 collective-permute-done.1.rest_1_
  78.7 5.9 %all-to-all-done.recv_ref = bf16[16,2,3,128,128]{4,3,2,1,0:T(8,128)(2,1)} async-done(((bf16[16,2,3,128,128]{4,3,2,1,0:T(8,128)(2,1)}), bf16[16,2,3,128,128]{4,3,2,1,0:T(8,128)(2,1)}, u32[]{:S(2)}, u32[]{:S(2)}) %all-to-all-start) | async-done | bytes 3145760 | tf_op jit(solution)/shard_map/all_to_all | solution.py:126
  84.6 0.0 copy-done.1
  84.6 0.0 copy-done.2
  84.6 0.0 copy-done.4
  84.6 5.9 %shard_map.48 = f32[8,128,128]{2,1,0:T(8,128)} custom-call(s32[1]{0:T(128)} %bitcast.me_ref, s32[4,128]{1,0:T(4,128)S(1)} %bitcast.5, bf16[16,2,3,128,128]{4,3,2,1,0:T(8,128)(2,1)} %all-to-all-done.recv_ref, bf16[2,2,128,128]{3,2,1,0:T(8,128)(2,1)S(1)} %pad_maximum_fusion.rest_0_, bf16[2,2,128,128]{3,2,1,0:T(8,128)(2,1)S(1)} %collective-permute-done.1.rest_1_, ...), custom_call_target="tpu_custom_call" | custom-call | tf_op jit(solution)/shard_map/pallas_call | solution.py:133
  (1 shorter events, 0.0 us)
Async XLA Ops:
  0.0 4.0 %copy-start = (bf16[2,32,128,128]{3,2,1,0:T(8,128)(2,1)S(1)}, bf16[2,32,128,128]{3,2,1,0:T(8,128)(2,1)}, u32[]{:S(2)}) copy-start(bf16[2,32,128,128]{3,2,1,0:T(8,128)(2,1)} %inv_ref.3) | copy-start | bytes 6291460
  1.6 5.6 %collective-permute-start = (bf16[1,2,128,128]{3,2,1,0:T(8,128)(2,1)}, bf16[1,2,128,128]{3,2,1,0:T(8,128)(2,1)S(1)}, u32[]{:S(2)}, u32[]{:S(2)}) collective-permute-start(bf16[1,2,128,128]{3,2,1,0:T(8,128)(2,1)} %shard_map.47), channel_id=1, source_target_pairs={{8,0},{9,1},{10,2},{11,3},{12,4},{13,5},{14,6},{15,7},{0,8},{1,9},... | collective-permute-start | bytes 196616 | tf_op jit(solution)/shard_map/ppermute | solution.py:108
  4.0 0.7 copy-start.3
  7.1 7.3 %copy-start.5 = (bf16[1,2,128,128]{3,2,1,0:T(8,128)(2,1)S(1)}, bf16[1,2,128,128]{3,2,1,0:T(8,128)(2,1)}, u32[]{:S(2)}) copy-start(bf16[1,2,128,128]{3,2,1,0:T(8,128)(2,1)} %shard_map.47) | copy-start | bytes 196612
  7.1 77.4 %copy-start.1 = (bf16[8,4,128,128]{3,2,1,0:T(8,128)(2,1)S(1)}, bf16[8,4,128,128]{3,2,1,0:T(8,128)(2,1)}, u32[]{:S(2)}) copy-start(bf16[8,4,128,128]{3,2,1,0:T(8,128)(2,1)} %param.4) | copy-start | bytes 3145732
  7.2 77.4 %copy-start.2 = (f32[8,128,128]{2,1,0:T(8,128)S(1)}, f32[8,128,128]{2,1,0:T(8,128)}, u32[]{:S(2)}) copy-start(f32[8,128,128]{2,1,0:T(8,128)} %rest_9_.1) | copy-start | bytes 1572868
  7.2 77.4 %copy-start.4 = (s32[128,4]{0,1:T(4,128)S(1)}, s32[128,4]{0,1:T(4,128)}, u32[]{:S(2)}) copy-start(s32[128,4]{0,1:T(4,128)} %param.7) | copy-start | bytes 6148
  7.2 77.4 %all-to-all-start = ((bf16[16,2,3,128,128]{4,3,2,1,0:T(8,128)(2,1)}), bf16[16,2,3,128,128]{4,3,2,1,0:T(8,128)(2,1)}, u32[]{:S(2)}, u32[]{:S(2)}) async-start(bf16[16,2,3,128,128]{4,3,2,1,0:T(8,128)(2,1)} %shard_map.46), calls=%async_computation | async-start | bytes 6291456 | tf_op jit(solution)/shard_map/all_to_all | solution.py:126
  14.5 56.0 %collective-permute-start.7 = (bf16[2,2,128,128]{3,2,1,0:T(8,128)(2,1)S(1)}, bf16[2,2,128,128]{3,2,1,0:T(8,128)(2,1)S(1)}, u32[]{:S(2)}, u32[]{:S(2)}) collective-permute-start(bf16[2,2,128,128]{3,2,1,0:T(8,128)(2,1)S(1)} %pad_maximum_fusion.rest_0_), channel_id=1, source_target_pairs={{7,0},{6,1},{5,2},{4,3},{3,4},{2,5},{1,6},{0,7},{15,8},{14,9},{13,... | collective-permute-start | bytes 393224 | tf_op jit(solution)/shard_map/ppermute | solution.py:131
  14.7 58.5 %collective-permute-start.6 = (bf16[2,2,128,128]{3,2,1,0:T(8,128)(2,1)S(1)}, bf16[2,2,128,128]{3,2,1,0:T(8,128)(2,1)S(1)}, u32[]{:S(2)}, u32[]{:S(2)}) collective-permute-start(bf16[2,2,128,128]{3,2,1,0:T(8,128)(2,1)S(1)} %pad_maximum_fusion.rest_0_), channel_id=1, source_target_pairs={{6,0},{7,1},{4,2},{5,3},{2,4},{3,5},{0,6},{1,7},{14,8},{15,9},{12,... | collective-permute-start | bytes 393224 | tf_op jit(solution)/shard_map/ppermute | solution.py:131
  17.1 59.4 %collective-permute-start.5 = (bf16[2,2,128,128]{3,2,1,0:T(8,128)(2,1)S(1)}, bf16[2,2,128,128]{3,2,1,0:T(8,128)(2,1)S(1)}, u32[]{:S(2)}, u32[]{:S(2)}) collective-permute-start(bf16[2,2,128,128]{3,2,1,0:T(8,128)(2,1)S(1)} %pad_maximum_fusion.rest_0_), channel_id=1, source_target_pairs={{5,0},{4,1},{7,2},{6,3},{1,4},{0,5},{3,6},{2,7},{13,8},{12,9},{15,... | collective-permute-start | bytes 393224 | tf_op jit(solution)/shard_map/ppermute | solution.py:131
  17.7 60.9 %collective-permute-start.4 = (bf16[2,2,128,128]{3,2,1,0:T(8,128)(2,1)S(1)}, bf16[2,2,128,128]{3,2,1,0:T(8,128)(2,1)S(1)}, u32[]{:S(2)}, u32[]{:S(2)}) collective-permute-start(bf16[2,2,128,128]{3,2,1,0:T(8,128)(2,1)S(1)} %pad_maximum_fusion.rest_0_), channel_id=1, source_target_pairs={{4,0},{5,1},{6,2},{7,3},{0,4},{1,5},{2,6},{3,7},{12,8},{13,9},{14,... | collective-permute-start | bytes 393224 | tf_op jit(solution)/shard_map/ppermute | solution.py:131
  18.9 59.7 %collective-permute-start.3 = (bf16[2,2,128,128]{3,2,1,0:T(8,128)(2,1)S(1)}, bf16[2,2,128,128]{3,2,1,0:T(8,128)(2,1)S(1)}, u32[]{:S(2)}, u32[]{:S(2)}) collective-permute-start(bf16[2,2,128,128]{3,2,1,0:T(8,128)(2,1)S(1)} %pad_maximum_fusion.rest_0_), channel_id=1, source_target_pairs={{3,0},{2,1},{1,2},{0,3},{7,4},{6,5},{5,6},{4,7},{11,8},{10,9},{9,1... | collective-permute-start | bytes 393224 | tf_op jit(solution)/shard_map/ppermute | solution.py:131
  70.5 8.2 %collective-permute-start.2 = (bf16[2,2,128,128]{3,2,1,0:T(8,128)(2,1)S(1)}, bf16[2,2,128,128]{3,2,1,0:T(8,128)(2,1)S(1)}, u32[]{:S(2)}, u32[]{:S(2)}) collective-permute-start(bf16[2,2,128,128]{3,2,1,0:T(8,128)(2,1)S(1)} %pad_maximum_fusion.rest_0_), channel_id=1, source_target_pairs={{2,0},{3,1},{0,2},{1,3},{6,4},{7,5},{4,6},{5,7},{10,8},{11,9},{8,1... | collective-permute-start | bytes 393224 | tf_op jit(solution)/shard_map/ppermute | solution.py:131
  73.1 5.5 %collective-permute-start.1 = (bf16[2,2,128,128]{3,2,1,0:T(8,128)(2,1)S(1)}, bf16[2,2,128,128]{3,2,1,0:T(8,128)(2,1)S(1)}, u32[]{:S(2)}, u32[]{:S(2)}) collective-permute-start(bf16[2,2,128,128]{3,2,1,0:T(8,128)(2,1)S(1)} %pad_maximum_fusion.rest_0_), channel_id=1, source_target_pairs={{1,0},{0,1},{3,2},{2,3},{5,4},{4,5},{7,6},{6,7},{9,8},{8,9},{11,10... | collective-permute-start | bytes 393224 | tf_op jit(solution)/shard_map/ppermute | solution.py:131

commit v5 on v4

--- a/solution.py
+++ b/solution.py
@@ -53,30 +53,35 @@
     pltpu.make_async_copy(send_v, send_ref, sem_o).wait()
 
 
-def level_kernel(quad, me_ref, st_ref, recv_ref, *rest):
-    diag_refs, rest = rest[:quad], rest[quad:]
+def level_kernel(n, quad, me_ref, st_ref, recv_ref, *rest):
+    diag_refs, rest = rest[:2], rest[2:]
     fac_ref, dfi_ref, out_ref, diag_v, line_v, out_v, sems, sem_o = rest
     cols, deep, width = fac_ref.shape
     length = deep // width
     rows = recv_ref.shape[1]
-    steps = diag_refs[0].shape[0]
+    steps = n // quad
     me = me_ref[0]
-    for k in range(cols):
-        for r in range(length):
-            anc = st_ref[r, me * cols + k]
-            src = recv_ref.at[lax.div(anc, rows), lax.rem(anc, rows)]
-            pltpu.make_async_copy(src, line_v.at[k, r], sems.at[k]).start()
-    for a in range(quad):
-        for t in range(steps):
-            owner = lax.bitwise_xor(lax.rem(me + t * quad, steps * quad), a)
+    count = recv_ref.shape[0]
+    parts = sems.shape[0]
+    each = count // parts
+    fetch = [
+        pltpu.make_async_copy(recv_ref.at[pl.ds(i * each, each)], line_v.at[pl.ds(i * each, each)], sems.at[i]) for i in range(parts)
+    ]
+    for f in fetch:
+        f.start()
+    for a in range(2):
+        for t in range(diag_refs[a].shape[0]):
+            owner = lax.bitwise_xor(lax.rem(me + t % steps * quad, n), t // steps * 2 + a)
             diag_v[pl.ds(owner * rows, rows)] = diag_refs[a][t]
     for k in range(cols):
         fac = fac_ref[k]
-        pltpu.make_async_copy(line_v.at[k], line_v.at[k], sems.at[k]).wait()
+        if k == 0:
+            for f in fetch:
+                f.wait()
         product = []
         for r in range(length):
             anc = st_ref[r, me * cols + k]
-            line = [diag_v[anc] if s == r else line_v[k, r, s if s < r else s - 1] for s in range(length)]
+            line = [diag_v[anc] if s == r else line_v[lax.div(anc, rows), lax.rem(anc, rows), s if s < r else s - 1] for s in range(length)]
             line = jnp.concatenate(line, axis=1)
             product.append(jnp.dot(line, fac, preferred_element_type=jnp.float32).astype(jnp.bfloat16))
         product = jnp.concatenate(product, axis=0)
@@ -126,20 +131,20 @@
     recv = lax.all_to_all(send, "prow", split_axis=0, concat_axis=0, tiled=True)
     held = [diag] + came
     held = jnp.concatenate(held, axis=0)
-    spread = [held]
-    for a in range(1, quad):
-        spread.append(lax.ppermute(held, "prow", [(i ^ a, i) for i in range(n)]))
+    chips = [held] + [lax.ppermute(held, "prow", [(i ^ a, i) for i in range(n)]) for a in range(2, quad, 2)]
+    chips = jnp.concatenate(chips, axis=0)
+    spread = [chips, lax.ppermute(chips, "prow", [(i ^ 1, i) for i in range(n)])]
     deep = length * width
     return pl.pallas_call(
-        functools.partial(level_kernel, quad),
+        functools.partial(level_kernel, n, quad),
         out_shape=jax.ShapeDtypeStruct((cols, width, width), jnp.float32),
-        in_specs=[smem, smem, hbm] + [vmem] * (quad + 2),
+        in_specs=[smem, smem, hbm] + [vmem] * 4,
         out_specs=hbm,
         scratch_shapes=[
             pltpu.VMEM((ancestors, width, width), jnp.bfloat16),
-            pltpu.VMEM((cols, length, length - 1, width, width), jnp.bfloat16),
+            pltpu.VMEM(recv.shape, jnp.bfloat16),
             pltpu.VMEM((cols, width, width), jnp.float32),
-            pltpu.SemaphoreType.DMA((cols,)),
+            pltpu.SemaphoreType.DMA((8,)),
             pltpu.SemaphoreType.DMA,
         ],
         compiler_params=pltpu.CompilerParams(vmem_limit_bytes=51 * 2**20),

time: 91.9 us -> 91.2 us (level)
  starting transfers between devices: 17 us -> 13 us
  waiting for transfers between devices: 62.7 us -> 66.6 us
    all_to_all x1, waiting for transfers between devices: 5.89 us -> 10.1 us  [shards(): recv = lax.all_to_all(send, 'prow', split_axis=0, concat_axis=0, tiled=True)]
    ppermute x7 -> x4, starting transfers between devices: 7.36 us -> 3.37 us  [the longest x3 2.71 us: shards(): lax.ppermute(held, 'prow', [(i ^ a, i) for i in range(n)])]
    ppermute x7 -> x4, waiting for transfers between devices: 56.8 us -> 56.5 us  [the longest x3 54.9 us: shards(): lax.ppermute(held, 'prow', [(i ^ a, i) for i in range(n)])]
  transfers between devices with their start and end apart: 9 -> 6, of which waited for: 5 -> 5; matrix products, arithmetic and copies ran while one was open for 0% -> 0% of each run, Pallas kernels for 3% -> 3%
where the time goes in v5:
time: 91.2 us; the launch traced here: 90.1 us
  waiting for transfers between devices  66.6 us (73%)
  starting transfers between devices  13 us (14%)
  Pallas kernels  9.65 us (11%)
    ppermute x3, waiting for transfers between devices, shards(): lax.ppermute(held, 'prow', [(i ^ a, i) for i in range(n)])  54.9 us
    all_to_all x1, waiting for transfers between devices, shards(): recv = lax.all_to_all(send, 'prow', split_axis=0, concat_axis=0, tiled=True)  10.1 us
    all_to_all x1, starting transfers between devices, shards(): recv = lax.all_to_all(send, 'prow', split_axis=0, concat_axis=0, tiled=True)  7.24 us
    pallas_call x1, Pallas kernels, shards(): pl.pallas_call(functools.partial(level_kernel, n, quad), out_shape=jax.Sh...  5.59 us
    ppermute x3, starting transfers between devices, shards(): lax.ppermute(held, 'prow', [(i ^ a, i) for i in range(n)])  2.71 us
    pallas_call x1, Pallas kernels, shards(): pl.pallas_call(functools.partial(pack_kernel, n, cols), out_shape=jax.Sha...  2.49 us
    ppermute x1, starting transfers between devices, shards(): lax.ppermute(diag, 'prow', [((i + t * quad) % n, i) for i in range(n)])  2.37 us
  transfers between devices with their start and end apart: 6, of which 5 were waited for; matrix products, arithmetic and copies ran while one was open for 0% of the time, Pallas kernels for 3%

profile of v5, /device:TPU:13, one launch (start us, length us, event | category | flops | bytes accessed | tf_op | source)
XLA Modules:
  0.0 90.1 jit_solution(18048838962144515205)
XLA Ops:
  0.0 0.0 copy-start
  0.0 1.6 %shard_map.47 = bf16[1,2,128,128]{3,2,1,0:T(8,128)(2,1)} custom-call(s32[1]{0:T(128)} %bitcast.me_ref, bf16[2,32,128,128]{3,2,1,0:T(8,128)(2,1)} %inv_ref.3), custom_call_target="tpu_custom_call" | custom-call | tf_op jit(solution)/shard_map/pallas_call | solution.py:106
  1.6 2.4 %collective-permute-start = (bf16[1,2,128,128]{3,2,1,0:T(8,128)(2,1)}, bf16[1,2,128,128]{3,2,1,0:T(8,128)(2,1)S(1)}, u32[]{:S(2)}, u32[]{:S(2)}) collective-permute-start(bf16[1,2,128,128]{3,2,1,0:T(8,128)(2,1)} %shard_map.47), channel_id=1, source_target_pairs={{8,0},{9,1},{10,2},{11,3},{12,4},{13,5},{14,6},{15,7},{0,8},{1,9},... | collective-permute-start | bytes 196616 | tf_op jit(solution)/shard_map/ppermute | solution.py:113
  4.0 0.0 copy-done
  4.0 0.0 copy-start.3
  4.0 0.7 copy-done.3
  4.6 2.5 %shard_map.46 = bf16[16,2,3,128,128]{4,3,2,1,0:T(8,128)(2,1)} custom-call(s32[1]{0:T(128)} %bitcast.me_ref, s32[4,128]{1,0:T(4,128)S(1)} %bitcast.4, bf16[2,32,128,128]{3,2,1,0:T(8,128)(2,1)S(1)} %copy-done), custom_call_target="tpu_custom_call" | custom-call | tf_op jit(solution)/shard_map/pallas_call | solution.py:116
  7.1 0.0 copy-start.5
  7.1 0.0 copy-start.1
  7.2 0.0 copy-start.2
  7.2 0.0 copy-start.4
  7.2 0.0 collective-permute-done
  7.2 7.2 %all-to-all-start = ((bf16[16,2,3,128,128]{4,3,2,1,0:T(8,128)(2,1)}), bf16[16,2,3,128,128]{4,3,2,1,0:T(8,128)(2,1)}, u32[]{:S(2)}, u32[]{:S(2)}) async-start(bf16[16,2,3,128,128]{4,3,2,1,0:T(8,128)(2,1)} %shard_map.46), calls=%async_computation | async-start | bytes 6291456 | tf_op jit(solution)/shard_map/all_to_all | solution.py:131
  14.4 0.0 copy-done.5
  14.5 0.3 collective-permute-start.1
  14.8 0.1 collective-permute-start.2
  14.9 2.3 %collective-permute-start.3 = (bf16[2,2,128,128]{3,2,1,0:T(8,128)(2,1)S(1)}, bf16[2,2,128,128]{3,2,1,0:T(8,128)(2,1)S(1)}, u32[]{:S(2)}, u32[]{:S(2)}) collective-permute-start(bf16[2,2,128,128]{3,2,1,0:T(8,128)(2,1)S(1)} %pad_maximum_fusion), channel_id=1, source_target_pairs={{6,0},{7,1},{4,2},{5,3},{2,4},{3,5},{0,6},{1,7},{14,8},{15,9},{12,... | collective-permute-start | bytes 393224 | tf_op jit(solution)/shard_map/ppermute | solution.py:134
  17.2 18.1 %collective-permute-done.1 = bf16[2,2,128,128]{3,2,1,0:T(8,128)(2,1)S(1)} collective-permute-done((bf16[2,2,128,128]{3,2,1,0:T(8,128)(2,1)S(1)}, bf16[2,2,128,128]{3,2,1,0:T(8,128)(2,1)S(1)}, u32[]{:S(2)}, u32[]{:S(2)}) %collective-permute-start.1) | collective-permute-done | bytes 131104 | tf_op jit(solution)/shard_map/ppermute | solution.py:134
  35.3 34.9 %collective-permute-done.2 = bf16[2,2,128,128]{3,2,1,0:T(8,128)(2,1)S(1)} collective-permute-done((bf16[2,2,128,128]{3,2,1,0:T(8,128)(2,1)S(1)}, bf16[2,2,128,128]{3,2,1,0:T(8,128)(2,1)S(1)}, u32[]{:S(2)}, u32[]{:S(2)}) %collective-permute-start.2) | collective-permute-done | bytes 131104 | tf_op jit(solution)/shard_map/ppermute | solution.py:134
  70.3 1.9 %collective-permute-done.3 = bf16[2,2,128,128]{3,2,1,0:T(8,128)(2,1)S(1)} collective-permute-done((bf16[2,2,128,128]{3,2,1,0:T(8,128)(2,1)S(1)}, bf16[2,2,128,128]{3,2,1,0:T(8,128)(2,1)S(1)}, u32[]{:S(2)}, u32[]{:S(2)}) %collective-permute-start.3) | collective-permute-done | bytes 131104 | tf_op jit(solution)/shard_map/ppermute | solution.py:134
  72.2 0.7 collective-permute-start.4
  72.8 1.5 %collective-permute-done.4.rest_1_ = bf16[8,2,128,128]{3,2,1,0:T(8,128)(2,1)S(1)} collective-permute-done((bf16[8,2,128,128]{3,2,1,0:T(8,128)(2,1)S(1)}, bf16[8,2,128,128]{3,2,1,0:T(8,128)(2,1)S(1)}, u32[]{:S(2)}, u32[]{:S(2)}) %collective-permute-start.4) | collective-permute-done | bytes 524320 | tf_op jit(solution)/shard_map/ppermute | solution.py:136
  74.4 10.1 %all-to-all-done.recv_ref = bf16[16,2,3,128,128]{4,3,2,1,0:T(8,128)(2,1)} async-done(((bf16[16,2,3,128,128]{4,3,2,1,0:T(8,128)(2,1)}), bf16[16,2,3,128,128]{4,3,2,1,0:T(8,128)(2,1)}, u32[]{:S(2)}, u32[]{:S(2)}) %all-to-all-start) | async-done | bytes 3145760 | tf_op jit(solution)/shard_map/all_to_all | solution.py:131
  84.5 0.0 copy-done.1
  84.5 0.0 copy-done.2
  84.5 0.0 copy-done.4
  84.5 5.6 %shard_map.48 = f32[8,128,128]{2,1,0:T(8,128)} custom-call(s32[1]{0:T(128)} %bitcast.me_ref, s32[4,128]{1,0:T(4,128)S(1)} %bitcast.5, bf16[16,2,3,128,128]{4,3,2,1,0:T(8,128)(2,1)} %all-to-all-done.recv_ref, bf16[8,2,128,128]{3,2,1,0:T(8,128)(2,1)S(1)} %constant_dynamic-update-slice_fusion.rest_0_, ...), custom_call_target="tpu_custom_call" | custom-call | tf_op jit(solution)/shard_map/pallas_call | solution.py:138
  (6 shorter events, 0.1 us)
Async XLA Ops:
  0.0 4.0 %copy-start = (bf16[2,32,128,128]{3,2,1,0:T(8,128)(2,1)S(1)}, bf16[2,32,128,128]{3,2,1,0:T(8,128)(2,1)}, u32[]{:S(2)}) copy-start(bf16[2,32,128,128]{3,2,1,0:T(8,128)(2,1)} %inv_ref.3) | copy-start | bytes 6291460
  1.6 5.6 %collective-permute-start = (bf16[1,2,128,128]{3,2,1,0:T(8,128)(2,1)}, bf16[1,2,128,128]{3,2,1,0:T(8,128)(2,1)S(1)}, u32[]{:S(2)}, u32[]{:S(2)}) collective-permute-start(bf16[1,2,128,128]{3,2,1,0:T(8,128)(2,1)} %shard_map.47), channel_id=1, source_target_pairs={{8,0},{9,1},{10,2},{11,3},{12,4},{13,5},{14,6},{15,7},{0,8},{1,9},... | collective-permute-start | bytes 196616 | tf_op jit(solution)/shard_map/ppermute | solution.py:113
  4.0 0.7 copy-start.3
  7.1 7.3 %copy-start.5 = (bf16[1,2,128,128]{3,2,1,0:T(8,128)(2,1)S(1)}, bf16[1,2,128,128]{3,2,1,0:T(8,128)(2,1)}, u32[]{:S(2)}) copy-start(bf16[1,2,128,128]{3,2,1,0:T(8,128)(2,1)} %shard_map.47) | copy-start | bytes 196612
  7.1 77.3 %copy-start.1 = (bf16[8,4,128,128]{3,2,1,0:T(8,128)(2,1)S(1)}, bf16[8,4,128,128]{3,2,1,0:T(8,128)(2,1)}, u32[]{:S(2)}) copy-start(bf16[8,4,128,128]{3,2,1,0:T(8,128)(2,1)} %param.4) | copy-start | bytes 3145732
  7.2 77.3 %copy-start.2 = (f32[8,128,128]{2,1,0:T(8,128)S(1)}, f32[8,128,128]{2,1,0:T(8,128)}, u32[]{:S(2)}) copy-start(f32[8,128,128]{2,1,0:T(8,128)} %rest_3_.1) | copy-start | bytes 1572868
  7.2 77.3 %copy-start.4 = (s32[128,4]{0,1:T(4,128)S(1)}, s32[128,4]{0,1:T(4,128)}, u32[]{:S(2)}) copy-start(s32[128,4]{0,1:T(4,128)} %param.7) | copy-start | bytes 6148
  7.2 77.3 %all-to-all-start = ((bf16[16,2,3,128,128]{4,3,2,1,0:T(8,128)(2,1)}), bf16[16,2,3,128,128]{4,3,2,1,0:T(8,128)(2,1)}, u32[]{:S(2)}, u32[]{:S(2)}) async-start(bf16[16,2,3,128,128]{4,3,2,1,0:T(8,128)(2,1)} %shard_map.46), calls=%async_computation | async-start | bytes 6291456 | tf_op jit(solution)/shard_map/all_to_all | solution.py:131
  14.5 20.8 %collective-permute-start.1 = (bf16[2,2,128,128]{3,2,1,0:T(8,128)(2,1)S(1)}, bf16[2,2,128,128]{3,2,1,0:T(8,128)(2,1)S(1)}, u32[]{:S(2)}, u32[]{:S(2)}) collective-permute-start(bf16[2,2,128,128]{3,2,1,0:T(8,128)(2,1)S(1)} %pad_maximum_fusion), channel_id=1, source_target_pairs={{2,0},{3,1},{0,2},{1,3},{6,4},{7,5},{4,6},{5,7},{10,8},{11,9},{8,1... | collective-permute-start | bytes 393224 | tf_op jit(solution)/shard_map/ppermute | solution.py:134
  14.8 55.4 %collective-permute-start.2 = (bf16[2,2,128,128]{3,2,1,0:T(8,128)(2,1)S(1)}, bf16[2,2,128,128]{3,2,1,0:T(8,128)(2,1)S(1)}, u32[]{:S(2)}, u32[]{:S(2)}) collective-permute-start(bf16[2,2,128,128]{3,2,1,0:T(8,128)(2,1)S(1)} %pad_maximum_fusion), channel_id=1, source_target_pairs={{4,0},{5,1},{6,2},{7,3},{0,4},{1,5},{2,6},{3,7},{12,8},{13,9},{14,... | collective-permute-start | bytes 393224 | tf_op jit(solution)/shard_map/ppermute | solution.py:134
  14.9 57.3 %collective-permute-start.3 = (bf16[2,2,128,128]{3,2,1,0:T(8,128)(2,1)S(1)}, bf16[2,2,128,128]{3,2,1,0:T(8,128)(2,1)S(1)}, u32[]{:S(2)}, u32[]{:S(2)}) collective-permute-start(bf16[2,2,128,128]{3,2,1,0:T(8,128)(2,1)S(1)} %pad_maximum_fusion), channel_id=1, source_target_pairs={{6,0},{7,1},{4,2},{5,3},{2,4},{3,5},{0,6},{1,7},{14,8},{15,9},{12,... | collective-permute-start | bytes 393224 | tf_op jit(solution)/shard_map/ppermute | solution.py:134
  72.2 2.2 %collective-permute-start.4 = (bf16[8,2,128,128]{3,2,1,0:T(8,128)(2,1)S(1)}, bf16[8,2,128,128]{3,2,1,0:T(8,128)(2,1)S(1)}, u32[]{:S(2)}, u32[]{:S(2)}) collective-permute-start(bf16[8,2,128,128]{3,2,1,0:T(8,128)(2,1)S(1)} %constant_dynamic-update-slice_fusion.rest_0_), channel_id=1, source_target_pairs={{1,0},{0,1},{3,2},{2,3},{5,4},{4,5},{7,6},{6,7},{9,8},{8,9},{11,10... | collective-permute-start | bytes 1572872 | tf_op jit(solution)/shard_map/ppermute | solution.py:136

commit v6 on v5

--- a/solution.py
+++ b/solution.py
@@ -55,7 +55,7 @@
 
 def level_kernel(n, quad, me_ref, st_ref, recv_ref, *rest):
     diag_refs, rest = rest[:2], rest[2:]
-    fac_ref, dfi_ref, out_ref, diag_v, line_v, out_v, sems, sem_o = rest
+    fac_ref, dfi_ref, out_ref, diag_v, line_v, product_v, out_v, sems, sem_o = rest
     cols, deep, width = fac_ref.shape
     length = deep // width
     rows = recv_ref.shape[1]
@@ -73,21 +73,20 @@
         for t in range(diag_refs[a].shape[0]):
             owner = lax.bitwise_xor(lax.rem(me + t % steps * quad, n), t // steps * 2 + a)
             diag_v[pl.ds(owner * rows, rows)] = diag_refs[a][t]
+    ancs = [[st_ref[r, me * cols + k] for r in range(length)] for k in range(cols)]
+    for f in fetch:
+        f.wait()
     for k in range(cols):
-        fac = fac_ref[k]
-        if k == 0:
-            for f in fetch:
-                f.wait()
-        product = []
-        for r in range(length):
-            anc = st_ref[r, me * cols + k]
-            line = [diag_v[anc] if s == r else line_v[lax.div(anc, rows), lax.rem(anc, rows), s if s < r else s - 1] for s in range(length)]
+        for r, anc in enumerate(ancs[k]):
+            owner, local = lax.div(anc, rows), lax.rem(anc, rows)
+            line = [diag_v[anc] if s == r else line_v[owner, local, s if s < r else s - 1] for s in range(length)]
             line = jnp.concatenate(line, axis=1)
-            product.append(jnp.dot(line, fac, preferred_element_type=jnp.float32).astype(jnp.bfloat16))
-        product = jnp.concatenate(product, axis=0)
-        term = lax.dot_general(fac, product, (((0,), (0,)), ((), ())), preferred_element_type=jnp.float32)
+            part = jnp.dot(line, fac_ref[k], preferred_element_type=jnp.float32)
+            product_v[k, r * width : (r + 1) * width, :] = part.astype(jnp.bfloat16)
+    for k in range(cols):
+        term = lax.dot_general(fac_ref[k], product_v[k], (((0,), (0,)), ((), ())), preferred_element_type=jnp.float32)
         out_v[k] = dfi_ref[k] + term
-        pltpu.make_async_copy(out_v.at[k], out_ref.at[k], sem_o).start()
+    pltpu.make_async_copy(out_v, out_ref, sem_o).start()
     pltpu.make_async_copy(out_v, out_ref, sem_o).wait()
 
 
@@ -143,6 +142,7 @@
         scratch_shapes=[
             pltpu.VMEM((ancestors, width, width), jnp.bfloat16),
             pltpu.VMEM(recv.shape, jnp.bfloat16),
+            pltpu.VMEM((cols, deep, width), jnp.bfloat16),
             pltpu.VMEM((cols, width, width), jnp.float32),
             pltpu.SemaphoreType.DMA((8,)),
             pltpu.SemaphoreType.DMA,

time: 91.2 us -> 90.4 us (level)
  no operation moved by 1% of the time
where the time goes in v6:
time: 90.4 us; the launch traced here: 89.3 us
  waiting for transfers between devices  66.6 us (74%)
  starting transfers between devices  13 us (14%)
  Pallas kernels  8.86 us (10%)
    ppermute x3, waiting for transfers between devices, shards(): lax.ppermute(held, 'prow', [(i ^ a, i) for i in range(n)])  54.9 us
    all_to_all x1, waiting for transfers between devices, shards(): recv = lax.all_to_all(send, 'prow', split_axis=0, concat_axis=0, tiled=True)  10.1 us
    all_to_all x1, starting transfers between devices, shards(): recv = lax.all_to_all(send, 'prow', split_axis=0, concat_axis=0, tiled=True)  7.24 us
    pallas_call x1, Pallas kernels, shards(): pl.pallas_call(functools.partial(level_kernel, n, quad), out_shape=jax.Sh...  4.8 us
    ppermute x3, starting transfers between devices, shards(): lax.ppermute(held, 'prow', [(i ^ a, i) for i in range(n)])  2.71 us
    pallas_call x1, Pallas kernels, shards(): pl.pallas_call(functools.partial(pack_kernel, n, cols), out_shape=jax.Sha...  2.49 us
    ppermute x1, starting transfers between devices, shards(): lax.ppermute(diag, 'prow', [((i + t * quad) % n, i) for i in range(n)])  2.37 us
  transfers between devices with their start and end apart: 6, of which 5 were waited for; matrix products, arithmetic and copies ran while one was open for 0% of the time, Pallas kernels for 3%

profile of v6, /device:TPU:13, one launch (start us, length us, event | category | flops | bytes accessed | tf_op | source)
XLA Modules:
  0.0 89.3 jit_solution(11611885289453359383)
XLA Ops:
  0.0 0.0 copy-start
  0.0 1.6 %shard_map.47 = bf16[1,2,128,128]{3,2,1,0:T(8,128)(2,1)} custom-call(s32[1]{0:T(128)} %bitcast.me_ref, bf16[2,32,128,128]{3,2,1,0:T(8,128)(2,1)} %inv_ref.3), custom_call_target="tpu_custom_call" | custom-call | tf_op jit(solution)/shard_map/pallas_call | solution.py:105
  1.6 2.4 %collective-permute-start = (bf16[1,2,128,128]{3,2,1,0:T(8,128)(2,1)}, bf16[1,2,128,128]{3,2,1,0:T(8,128)(2,1)S(1)}, u32[]{:S(2)}, u32[]{:S(2)}) collective-permute-start(bf16[1,2,128,128]{3,2,1,0:T(8,128)(2,1)} %shard_map.47), channel_id=1, source_target_pairs={{8,0},{9,1},{10,2},{11,3},{12,4},{13,5},{14,6},{15,7},{0,8},{1,9},... | collective-permute-start | bytes 196616 | tf_op jit(solution)/shard_map/ppermute | solution.py:112
  4.0 0.0 copy-done
  4.0 0.0 copy-start.3
  4.0 0.7 copy-done.3
  4.6 2.5 %shard_map.46 = bf16[16,2,3,128,128]{4,3,2,1,0:T(8,128)(2,1)} custom-call(s32[1]{0:T(128)} %bitcast.me_ref, s32[4,128]{1,0:T(4,128)S(1)} %bitcast.4, bf16[2,32,128,128]{3,2,1,0:T(8,128)(2,1)S(1)} %copy-done), custom_call_target="tpu_custom_call" | custom-call | tf_op jit(solution)/shard_map/pallas_call | solution.py:115
  7.1 0.0 copy-start.5
  7.1 0.0 copy-start.1
  7.2 0.0 copy-start.2
  7.2 0.0 copy-start.4
  7.2 0.0 collective-permute-done
  7.2 7.2 %all-to-all-start = ((bf16[16,2,3,128,128]{4,3,2,1,0:T(8,128)(2,1)}), bf16[16,2,3,128,128]{4,3,2,1,0:T(8,128)(2,1)}, u32[]{:S(2)}, u32[]{:S(2)}) async-start(bf16[16,2,3,128,128]{4,3,2,1,0:T(8,128)(2,1)} %shard_map.46), calls=%async_computation | async-start | bytes 6291456 | tf_op jit(solution)/shard_map/all_to_all | solution.py:130
  14.4 0.0 copy-done.5
  14.5 0.3 collective-permute-start.1
  14.8 0.1 collective-permute-start.2
  14.9 2.3 %collective-permute-start.3 = (bf16[2,2,128,128]{3,2,1,0:T(8,128)(2,1)S(1)}, bf16[2,2,128,128]{3,2,1,0:T(8,128)(2,1)S(1)}, u32[]{:S(2)}, u32[]{:S(2)}) collective-permute-start(bf16[2,2,128,128]{3,2,1,0:T(8,128)(2,1)S(1)} %pad_maximum_fusion), channel_id=1, source_target_pairs={{6,0},{7,1},{4,2},{5,3},{2,4},{3,5},{0,6},{1,7},{14,8},{15,9},{12,... | collective-permute-start | bytes 393224 | tf_op jit(solution)/shard_map/ppermute | solution.py:133
  17.2 18.1 %collective-permute-done.1 = bf16[2,2,128,128]{3,2,1,0:T(8,128)(2,1)S(1)} collective-permute-done((bf16[2,2,128,128]{3,2,1,0:T(8,128)(2,1)S(1)}, bf16[2,2,128,128]{3,2,1,0:T(8,128)(2,1)S(1)}, u32[]{:S(2)}, u32[]{:S(2)}) %collective-permute-start.1) | collective-permute-done | bytes 131104 | tf_op jit(solution)/shard_map/ppermute | solution.py:133
  35.3 34.9 %collective-permute-done.2 = bf16[2,2,128,128]{3,2,1,0:T(8,128)(2,1)S(1)} collective-permute-done((bf16[2,2,128,128]{3,2,1,0:T(8,128)(2,1)S(1)}, bf16[2,2,128,128]{3,2,1,0:T(8,128)(2,1)S(1)}, u32[]{:S(2)}, u32[]{:S(2)}) %collective-permute-start.2) | collective-permute-done | bytes 131104 | tf_op jit(solution)/shard_map/ppermute | solution.py:133
  70.3 1.9 %collective-permute-done.3 = bf16[2,2,128,128]{3,2,1,0:T(8,128)(2,1)S(1)} collective-permute-done((bf16[2,2,128,128]{3,2,1,0:T(8,128)(2,1)S(1)}, bf16[2,2,128,128]{3,2,1,0:T(8,128)(2,1)S(1)}, u32[]{:S(2)}, u32[]{:S(2)}) %collective-permute-start.3) | collective-permute-done | bytes 131104 | tf_op jit(solution)/shard_map/ppermute | solution.py:133
  72.2 0.7 collective-permute-start.4
  72.8 1.5 %collective-permute-done.4.rest_1_ = bf16[8,2,128,128]{3,2,1,0:T(8,128)(2,1)S(1)} collective-permute-done((bf16[8,2,128,128]{3,2,1,0:T(8,128)(2,1)S(1)}, bf16[8,2,128,128]{3,2,1,0:T(8,128)(2,1)S(1)}, u32[]{:S(2)}, u32[]{:S(2)}) %collective-permute-start.4) | collective-permute-done | bytes 524320 | tf_op jit(solution)/shard_map/ppermute | solution.py:135
  74.4 10.1 %all-to-all-done.recv_ref = bf16[16,2,3,128,128]{4,3,2,1,0:T(8,128)(2,1)} async-done(((bf16[16,2,3,128,128]{4,3,2,1,0:T(8,128)(2,1)}), bf16[16,2,3,128,128]{4,3,2,1,0:T(8,128)(2,1)}, u32[]{:S(2)}, u32[]{:S(2)}) %all-to-all-start) | async-done | bytes 3145760 | tf_op jit(solution)/shard_map/all_to_all | solution.py:130
  84.5 0.0 copy-done.1
  84.5 0.0 copy-done.2
  84.5 0.0 copy-done.4
  84.5 4.8 %shard_map.48 = f32[8,128,128]{2,1,0:T(8,128)} custom-call(s32[1]{0:T(128)} %bitcast.me_ref, s32[4,128]{1,0:T(4,128)S(1)} %bitcast.5, bf16[16,2,3,128,128]{4,3,2,1,0:T(8,128)(2,1)} %all-to-all-done.recv_ref, bf16[8,2,128,128]{3,2,1,0:T(8,128)(2,1)S(1)} %constant_dynamic-update-slice_fusion.rest_0_, ...), custom_call_target="tpu_custom_call" | custom-call | tf_op jit(solution)/shard_map/pallas_call | solution.py:137
  (6 shorter events, 0.1 us)
Async XLA Ops:
  0.0 4.0 %copy-start = (bf16[2,32,128,128]{3,2,1,0:T(8,128)(2,1)S(1)}, bf16[2,32,128,128]{3,2,1,0:T(8,128)(2,1)}, u32[]{:S(2)}) copy-start(bf16[2,32,128,128]{3,2,1,0:T(8,128)(2,1)} %inv_ref.3) | copy-start | bytes 6291460
  1.6 5.6 %collective-permute-start = (bf16[1,2,128,128]{3,2,1,0:T(8,128)(2,1)}, bf16[1,2,128,128]{3,2,1,0:T(8,128)(2,1)S(1)}, u32[]{:S(2)}, u32[]{:S(2)}) collective-permute-start(bf16[1,2,128,128]{3,2,1,0:T(8,128)(2,1)} %shard_map.47), channel_id=1, source_target_pairs={{8,0},{9,1},{10,2},{11,3},{12,4},{13,5},{14,6},{15,7},{0,8},{1,9},... | collective-permute-start | bytes 196616 | tf_op jit(solution)/shard_map/ppermute | solution.py:112
  4.0 0.7 copy-start.3
  7.1 7.3 %copy-start.5 = (bf16[1,2,128,128]{3,2,1,0:T(8,128)(2,1)S(1)}, bf16[1,2,128,128]{3,2,1,0:T(8,128)(2,1)}, u32[]{:S(2)}) copy-start(bf16[1,2,128,128]{3,2,1,0:T(8,128)(2,1)} %shard_map.47) | copy-start | bytes 196612
  7.1 77.3 %copy-start.1 = (bf16[8,4,128,128]{3,2,1,0:T(8,128)(2,1)S(1)}, bf16[8,4,128,128]{3,2,1,0:T(8,128)(2,1)}, u32[]{:S(2)}) copy-start(bf16[8,4,128,128]{3,2,1,0:T(8,128)(2,1)} %param.4) | copy-start | bytes 3145732
  7.2 77.3 %copy-start.2 = (f32[8,128,128]{2,1,0:T(8,128)S(1)}, f32[8,128,128]{2,1,0:T(8,128)}, u32[]{:S(2)}) copy-start(f32[8,128,128]{2,1,0:T(8,128)} %rest_3_.1) | copy-start | bytes 1572868
  7.2 77.3 %copy-start.4 = (s32[128,4]{0,1:T(4,128)S(1)}, s32[128,4]{0,1:T(4,128)}, u32[]{:S(2)}) copy-start(s32[128,4]{0,1:T(4,128)} %param.7) | copy-start | bytes 6148
  7.2 77.3 %all-to-all-start = ((bf16[16,2,3,128,128]{4,3,2,1,0:T(8,128)(2,1)}), bf16[16,2,3,128,128]{4,3,2,1,0:T(8,128)(2,1)}, u32[]{:S(2)}, u32[]{:S(2)}) async-start(bf16[16,2,3,128,128]{4,3,2,1,0:T(8,128)(2,1)} %shard_map.46), calls=%async_computation | async-start | bytes 6291456 | tf_op jit(solution)/shard_map/all_to_all | solution.py:130
  14.5 20.8 %collective-permute-start.1 = (bf16[2,2,128,128]{3,2,1,0:T(8,128)(2,1)S(1)}, bf16[2,2,128,128]{3,2,1,0:T(8,128)(2,1)S(1)}, u32[]{:S(2)}, u32[]{:S(2)}) collective-permute-start(bf16[2,2,128,128]{3,2,1,0:T(8,128)(2,1)S(1)} %pad_maximum_fusion), channel_id=1, source_target_pairs={{2,0},{3,1},{0,2},{1,3},{6,4},{7,5},{4,6},{5,7},{10,8},{11,9},{8,1... | collective-permute-start | bytes 393224 | tf_op jit(solution)/shard_map/ppermute | solution.py:133
  14.8 55.4 %collective-permute-start.2 = (bf16[2,2,128,128]{3,2,1,0:T(8,128)(2,1)S(1)}, bf16[2,2,128,128]{3,2,1,0:T(8,128)(2,1)S(1)}, u32[]{:S(2)}, u32[]{:S(2)}) collective-permute-start(bf16[2,2,128,128]{3,2,1,0:T(8,128)(2,1)S(1)} %pad_maximum_fusion), channel_id=1, source_target_pairs={{4,0},{5,1},{6,2},{7,3},{0,4},{1,5},{2,6},{3,7},{12,8},{13,9},{14,... | collective-permute-start | bytes 393224 | tf_op jit(solution)/shard_map/ppermute | solution.py:133
  14.9 57.3 %collective-permute-start.3 = (bf16[2,2,128,128]{3,2,1,0:T(8,128)(2,1)S(1)}, bf16[2,2,128,128]{3,2,1,0:T(8,128)(2,1)S(1)}, u32[]{:S(2)}, u32[]{:S(2)}) collective-permute-start(bf16[2,2,128,128]{3,2,1,0:T(8,128)(2,1)S(1)} %pad_maximum_fusion), channel_id=1, source_target_pairs={{6,0},{7,1},{4,2},{5,3},{2,4},{3,5},{0,6},{1,7},{14,8},{15,9},{12,... | collective-permute-start | bytes 393224 | tf_op jit(solution)/shard_map/ppermute | solution.py:133
  72.2 2.2 %collective-permute-start.4 = (bf16[8,2,128,128]{3,2,1,0:T(8,128)(2,1)S(1)}, bf16[8,2,128,128]{3,2,1,0:T(8,128)(2,1)S(1)}, u32[]{:S(2)}, u32[]{:S(2)}) collective-permute-start(bf16[8,2,128,128]{3,2,1,0:T(8,128)(2,1)S(1)} %constant_dynamic-update-slice_fusion.rest_0_), channel_id=1, source_target_pairs={{1,0},{0,1},{3,2},{2,3},{5,4},{4,5},{7,6},{6,7},{9,8},{8,9},{11,10... | collective-permute-start | bytes 1572872 | tf_op jit(solution)/shard_map/ppermute | solution.py:135

commit v7 on v6

--- a/solution.py
+++ b/solution.py
@@ -16,11 +16,13 @@
         pltpu.make_async_copy(inv_ref.at[j, 0], diag_ref.at[0, j], sem.at[j]).wait()
 
 
-def pack_kernel(n, cols, me_ref, st_ref, inv_ref, send_ref, send_v, idx_v, idx_s, sem_i, sem_o):
+def pack_kernel(n, cols, me_ref, st_ref, inv_ref, send_ref, inv_v, send_v, idx_v, idx_s, sem, sem_i, sem_o):
     length, total = st_ref.shape
     rows = inv_ref.shape[0]
     others = length - 1
     me = me_ref[0]
+    fetch = pltpu.make_async_copy(inv_ref, inv_v, sem)
+    fetch.start()
     st = [st_ref[r : r + 1, :] for r in range(length)]
     lines = []
     for j in range(rows):
@@ -41,11 +43,12 @@
     copy = pltpu.make_async_copy(idx_v, idx_s, sem_i)
     copy.start()
     copy.wait()
+    fetch.wait()
 
     def to_device(p, carry):
         for j in range(rows):
             for q in range(others):
-                send_v[p, j, q] = inv_ref[j, idx_s[j * others + q, p]]
+                send_v[p, j, q] = inv_v[j, idx_s[j * others + q, p]]
         pltpu.make_async_copy(send_v.at[p], send_ref.at[p], sem_o).start()
         return carry
 
@@ -115,16 +118,18 @@
     send = pl.pallas_call(
         functools.partial(pack_kernel, n, cols),
         out_shape=jax.ShapeDtypeStruct((n, rows, length - 1, width, width), jnp.bfloat16),
-        in_specs=[smem, vmem, vmem],
+        in_specs=[smem, vmem, hbm],
         out_specs=hbm,
         scratch_shapes=[
+            pltpu.VMEM(inverse_blocks.shape, jnp.bfloat16),
             pltpu.VMEM((n, rows, length - 1, width, width), jnp.bfloat16),
             pltpu.VMEM((lines, lanes), jnp.int32),
             pltpu.SMEM((lines, lanes), jnp.int32),
             pltpu.SemaphoreType.DMA,
             pltpu.SemaphoreType.DMA,
+            pltpu.SemaphoreType.DMA,
         ],
-        compiler_params=pltpu.CompilerParams(vmem_limit_bytes=40 * 2**20),
+        compiler_params=pltpu.CompilerParams(vmem_limit_bytes=56 * 2**20),
     )(me1, structure.T, inverse_blocks)
     send, *came = lax.optimization_barrier((send, *came))
     recv = lax.all_to_all(send, "prow", split_axis=0, concat_axis=0, tiled=True)

time: 90.4 us -> 90.4 us (level)
  Pallas kernels: 8.86 us -> 10.2 us
    pallas_call x1, Pallas kernels: 2.49 us -> 3.99 us  [shards(): pl.pallas_call(functools.partial(pack_kernel, n, cols), out_shape=jax.Sha...]
  transfers between devices with their start and end apart: 6 -> 6, of which waited for: 5 -> 5; matrix products, arithmetic and copies ran while one was open for 0% -> 0% of each run, Pallas kernels for 3% -> 4%
where the time goes in v7:
time: 90.4 us; the launch traced here: 89.2 us
  waiting for transfers between devices  66.6 us (74%)
  starting transfers between devices  12.2 us (13%)
  Pallas kernels  10.2 us (11%)
    ppermute x3, waiting for transfers between devices, shards(): lax.ppermute(held, 'prow', [(i ^ a, i) for i in range(n)])  54.9 us
    all_to_all x1, waiting for transfers between devices, shards(): recv = lax.all_to_all(send, 'prow', split_axis=0, concat_axis=0, tiled=True)  10.1 us
    all_to_all x1, starting transfers between devices, shards(): recv = lax.all_to_all(send, 'prow', split_axis=0, concat_axis=0, tiled=True)  6.42 us
    pallas_call x1, Pallas kernels, shards(): pl.pallas_call(functools.partial(level_kernel, n, quad), out_shape=jax.Sh...  4.82 us
    pallas_call x1, Pallas kernels, shards(): pl.pallas_call(functools.partial(pack_kernel, n, cols), out_shape=jax.Sha...  3.99 us
    ppermute x3, starting transfers between devices, shards(): lax.ppermute(held, 'prow', [(i ^ a, i) for i in range(n)])  2.71 us
    ppermute x1, starting transfers between devices, shards(): lax.ppermute(diag, 'prow', [((i + t * quad) % n, i) for i in range(n)])  2.37 us
  transfers between devices with their start and end apart: 6, of which 5 were waited for; matrix products, arithmetic and copies ran while one was open for 0% of the time, Pallas kernels for 4%

profile of v7, /device:TPU:13, one launch (start us, length us, event | category | flops | bytes accessed | tf_op | source)
XLA Modules:
  0.0 89.2 jit_solution(7073276360703561211)
XLA Ops:
  0.0 1.4 %shard_map.47 = bf16[1,2,128,128]{3,2,1,0:T(8,128)(2,1)} custom-call(s32[1]{0:T(128)} %bitcast.me_ref, bf16[2,32,128,128]{3,2,1,0:T(8,128)(2,1)} %inv_ref.3), custom_call_target="tpu_custom_call" | custom-call | tf_op jit(solution)/shard_map/pallas_call | solution.py:108
  1.4 2.4 %collective-permute-start = (bf16[1,2,128,128]{3,2,1,0:T(8,128)(2,1)}, bf16[1,2,128,128]{3,2,1,0:T(8,128)(2,1)S(1)}, u32[]{:S(2)}, u32[]{:S(2)}) collective-permute-start(bf16[1,2,128,128]{3,2,1,0:T(8,128)(2,1)} %shard_map.47), channel_id=1, source_target_pairs={{8,0},{9,1},{10,2},{11,3},{12,4},{13,5},{14,6},{15,7},{0,8},{1,9},... | collective-permute-start | bytes 196616 | tf_op jit(solution)/shard_map/ppermute | solution.py:115
  3.8 4.0 %shard_map.46 = bf16[16,2,3,128,128]{4,3,2,1,0:T(8,128)(2,1)} custom-call(s32[1]{0:T(128)} %bitcast.me_ref, s32[4,128]{1,0:T(4,128)} %bitcast.4, bf16[2,32,128,128]{3,2,1,0:T(8,128)(2,1)} %inv_ref.3), custom_call_target="tpu_custom_call" | custom-call | tf_op jit(solution)/shard_map/pallas_call | solution.py:118
  7.8 0.0 copy-start.3
  7.8 0.0 copy-start
  7.8 0.0 copy-start.1
  7.8 0.0 copy-start.2
  7.9 0.0 collective-permute-done
  7.9 6.4 %all-to-all-start = ((bf16[16,2,3,128,128]{4,3,2,1,0:T(8,128)(2,1)}), bf16[16,2,3,128,128]{4,3,2,1,0:T(8,128)(2,1)}, u32[]{:S(2)}, u32[]{:S(2)}) async-start(bf16[16,2,3,128,128]{4,3,2,1,0:T(8,128)(2,1)} %shard_map.46), calls=%async_computation | async-start | bytes 6291456 | tf_op jit(solution)/shard_map/all_to_all | solution.py:135
  14.3 0.0 copy-done.3
  14.3 0.3 collective-permute-start.1
  14.7 0.1 collective-permute-start.2
  14.7 2.3 %collective-permute-start.3 = (bf16[2,2,128,128]{3,2,1,0:T(8,128)(2,1)S(1)}, bf16[2,2,128,128]{3,2,1,0:T(8,128)(2,1)S(1)}, u32[]{:S(2)}, u32[]{:S(2)}) collective-permute-start(bf16[2,2,128,128]{3,2,1,0:T(8,128)(2,1)S(1)} %pad_maximum_fusion), channel_id=1, source_target_pairs={{6,0},{7,1},{4,2},{5,3},{2,4},{3,5},{0,6},{1,7},{14,8},{15,9},{12,... | collective-permute-start | bytes 393224 | tf_op jit(solution)/shard_map/ppermute | solution.py:138
  17.0 18.1 %collective-permute-done.1 = bf16[2,2,128,128]{3,2,1,0:T(8,128)(2,1)S(1)} collective-permute-done((bf16[2,2,128,128]{3,2,1,0:T(8,128)(2,1)S(1)}, bf16[2,2,128,128]{3,2,1,0:T(8,128)(2,1)S(1)}, u32[]{:S(2)}, u32[]{:S(2)}) %collective-permute-start.1) | collective-permute-done | bytes 131104 | tf_op jit(solution)/shard_map/ppermute | solution.py:138
  35.2 34.9 %collective-permute-done.2 = bf16[2,2,128,128]{3,2,1,0:T(8,128)(2,1)S(1)} collective-permute-done((bf16[2,2,128,128]{3,2,1,0:T(8,128)(2,1)S(1)}, bf16[2,2,128,128]{3,2,1,0:T(8,128)(2,1)S(1)}, u32[]{:S(2)}, u32[]{:S(2)}) %collective-permute-start.2) | collective-permute-done | bytes 131104 | tf_op jit(solution)/shard_map/ppermute | solution.py:138
  70.1 1.9 %collective-permute-done.3 = bf16[2,2,128,128]{3,2,1,0:T(8,128)(2,1)S(1)} collective-permute-done((bf16[2,2,128,128]{3,2,1,0:T(8,128)(2,1)S(1)}, bf16[2,2,128,128]{3,2,1,0:T(8,128)(2,1)S(1)}, u32[]{:S(2)}, u32[]{:S(2)}) %collective-permute-start.3) | collective-permute-done | bytes 131104 | tf_op jit(solution)/shard_map/ppermute | solution.py:138
  72.0 0.7 collective-permute-start.4
  72.7 1.5 %collective-permute-done.4.rest_1_ = bf16[8,2,128,128]{3,2,1,0:T(8,128)(2,1)S(1)} collective-permute-done((bf16[8,2,128,128]{3,2,1,0:T(8,128)(2,1)S(1)}, bf16[8,2,128,128]{3,2,1,0:T(8,128)(2,1)S(1)}, u32[]{:S(2)}, u32[]{:S(2)}) %collective-permute-start.4) | collective-permute-done | bytes 524320 | tf_op jit(solution)/shard_map/ppermute | solution.py:140
  74.2 10.1 %all-to-all-done.recv_ref = bf16[16,2,3,128,128]{4,3,2,1,0:T(8,128)(2,1)} async-done(((bf16[16,2,3,128,128]{4,3,2,1,0:T(8,128)(2,1)}), bf16[16,2,3,128,128]{4,3,2,1,0:T(8,128)(2,1)}, u32[]{:S(2)}, u32[]{:S(2)}) %all-to-all-start) | async-done | bytes 3145760 | tf_op jit(solution)/shard_map/all_to_all | solution.py:135
  84.3 0.0 copy-done
  84.3 0.0 copy-done.1
  84.3 0.0 copy-done.2
  84.3 4.8 %shard_map.48 = f32[8,128,128]{2,1,0:T(8,128)} custom-call(s32[1]{0:T(128)} %bitcast.me_ref, s32[4,128]{1,0:T(4,128)S(1)} %bitcast.5, bf16[16,2,3,128,128]{4,3,2,1,0:T(8,128)(2,1)} %all-to-all-done.recv_ref, bf16[8,2,128,128]{3,2,1,0:T(8,128)(2,1)S(1)} %constant_dynamic-update-slice_fusion.rest_0_, ...), custom_call_target="tpu_custom_call" | custom-call | tf_op jit(solution)/shard_map/pallas_call | solution.py:142
  (6 shorter events, 0.1 us)
Async XLA Ops:
  1.4 6.4 %collective-permute-start = (bf16[1,2,128,128]{3,2,1,0:T(8,128)(2,1)}, bf16[1,2,128,128]{3,2,1,0:T(8,128)(2,1)S(1)}, u32[]{:S(2)}, u32[]{:S(2)}) collective-permute-start(bf16[1,2,128,128]{3,2,1,0:T(8,128)(2,1)} %shard_map.47), channel_id=1, source_target_pairs={{8,0},{9,1},{10,2},{11,3},{12,4},{13,5},{14,6},{15,7},{0,8},{1,9},... | collective-permute-start | bytes 196616 | tf_op jit(solution)/shard_map/ppermute | solution.py:115
  7.8 6.5 %copy-start.3 = (bf16[1,2,128,128]{3,2,1,0:T(8,128)(2,1)S(1)}, bf16[1,2,128,128]{3,2,1,0:T(8,128)(2,1)}, u32[]{:S(2)}) copy-start(bf16[1,2,128,128]{3,2,1,0:T(8,128)(2,1)} %shard_map.47) | copy-start | bytes 196612
  7.8 76.5 %copy-start = (bf16[8,4,128,128]{3,2,1,0:T(8,128)(2,1)S(1)}, bf16[8,4,128,128]{3,2,1,0:T(8,128)(2,1)}, u32[]{:S(2)}) copy-start(bf16[8,4,128,128]{3,2,1,0:T(8,128)(2,1)} %param.4) | copy-start | bytes 3145732
  7.8 76.5 %copy-start.1 = (f32[8,128,128]{2,1,0:T(8,128)S(1)}, f32[8,128,128]{2,1,0:T(8,128)}, u32[]{:S(2)}) copy-start(f32[8,128,128]{2,1,0:T(8,128)} %rest_3_.1) | copy-start | bytes 1572868
  7.8 76.5 %copy-start.2 = (s32[128,4]{0,1:T(4,128)S(1)}, s32[128,4]{0,1:T(4,128)}, u32[]{:S(2)}) copy-start(s32[128,4]{0,1:T(4,128)} %param.7) | copy-start | bytes 6148
  7.9 76.5 %all-to-all-start = ((bf16[16,2,3,128,128]{4,3,2,1,0:T(8,128)(2,1)}), bf16[16,2,3,128,128]{4,3,2,1,0:T(8,128)(2,1)}, u32[]{:S(2)}, u32[]{:S(2)}) async-start(bf16[16,2,3,128,128]{4,3,2,1,0:T(8,128)(2,1)} %shard_map.46), calls=%async_computation | async-start | bytes 6291456 | tf_op jit(solution)/shard_map/all_to_all | solution.py:135
  14.3 20.8 %collective-permute-start.1 = (bf16[2,2,128,128]{3,2,1,0:T(8,128)(2,1)S(1)}, bf16[2,2,128,128]{3,2,1,0:T(8,128)(2,1)S(1)}, u32[]{:S(2)}, u32[]{:S(2)}) collective-permute-start(bf16[2,2,128,128]{3,2,1,0:T(8,128)(2,1)S(1)} %pad_maximum_fusion), channel_id=1, source_target_pairs={{2,0},{3,1},{0,2},{1,3},{6,4},{7,5},{4,6},{5,7},{10,8},{11,9},{8,1... | collective-permute-start | bytes 393224 | tf_op jit(solution)/shard_map/ppermute | solution.py:138
  14.7 55.4 %collective-permute-start.2 = (bf16[2,2,128,128]{3,2,1,0:T(8,128)(2,1)S(1)}, bf16[2,2,128,128]{3,2,1,0:T(8,128)(2,1)S(1)}, u32[]{:S(2)}, u32[]{:S(2)}) collective-permute-start(bf16[2,2,128,128]{3,2,1,0:T(8,128)(2,1)S(1)} %pad_maximum_fusion), channel_id=1, source_target_pairs={{4,0},{5,1},{6,2},{7,3},{0,4},{1,5},{2,6},{3,7},{12,8},{13,9},{14,... | collective-permute-start | bytes 393224 | tf_op jit(solution)/shard_map/ppermute | solution.py:138
  14.7 57.3 %collective-permute-start.3 = (bf16[2,2,128,128]{3,2,1,0:T(8,128)(2,1)S(1)}, bf16[2,2,128,128]{3,2,1,0:T(8,128)(2,1)S(1)}, u32[]{:S(2)}, u32[]{:S(2)}) collective-permute-start(bf16[2,2,128,128]{3,2,1,0:T(8,128)(2,1)S(1)} %pad_maximum_fusion), channel_id=1, source_target_pairs={{6,0},{7,1},{4,2},{5,3},{2,4},{3,5},{0,6},{1,7},{14,8},{15,9},{12,... | collective-permute-start | bytes 393224 | tf_op jit(solution)/shard_map/ppermute | solution.py:138
  72.0 2.2 %collective-permute-start.4 = (bf16[8,2,128,128]{3,2,1,0:T(8,128)(2,1)S(1)}, bf16[8,2,128,128]{3,2,1,0:T(8,128)(2,1)S(1)}, u32[]{:S(2)}, u32[]{:S(2)}) collective-permute-start(bf16[8,2,128,128]{3,2,1,0:T(8,128)(2,1)S(1)} %constant_dynamic-update-slice_fusion.rest_0_), channel_id=1, source_target_pairs={{1,0},{0,1},{3,2},{2,3},{5,4},{4,5},{7,6},{6,7},{9,8},{8,9},{11,10... | collective-permute-start | bytes 1572872 | tf_op jit(solution)/shard_map/ppermute | solution.py:140

commit v8 on v7

--- a/solution.py
+++ b/solution.py
@@ -135,7 +135,8 @@
     recv = lax.all_to_all(send, "prow", split_axis=0, concat_axis=0, tiled=True)
     held = [diag] + came
     held = jnp.concatenate(held, axis=0)
-    chips = [held] + [lax.ppermute(held, "prow", [(i ^ a, i) for i in range(n)]) for a in range(2, quad, 2)]
+    pair = jnp.concatenate([held, lax.ppermute(held, "prow", [(i ^ 2, i) for i in range(n)])], axis=0)
+    chips = [pair, lax.ppermute(pair, "prow", [(i ^ 4, i) for i in range(n)])]
     chips = jnp.concatenate(chips, axis=0)
     spread = [chips, lax.ppermute(chips, "prow", [(i ^ 1, i) for i in range(n)])]
     deep = length * width

time: 90.4 us -> 89.5 us (0.990)
  starting transfers between devices: 12.2 us -> 10.5 us
  waiting for transfers between devices: 66.6 us -> 68.2 us
    ppermute x3 -> x2, waiting for transfers between devices: 54.9 us -> 57.8 us  [the longest x1 37.3 us: shards(): chips = [pair, lax.ppermute(pair, 'prow', [(i ^ 4, i) for i in range(n)])]]
    ppermute x3 -> x2, starting transfers between devices: 2.71 us -> 0.76 us  [the longest x1 0.41 us: shards(): chips = [pair, lax.ppermute(pair, 'prow', [(i ^ 4, i) for i in range(n)])]]
    all_to_all x1, waiting for transfers between devices: 10.1 us -> 8.9 us  [shards(): recv = lax.all_to_all(send, 'prow', split_axis=0, concat_axis=0, tiled=True)]
  transfers between devices with their start and end apart: 6 -> 5, of which waited for: 5 -> 4; matrix products, arithmetic and copies ran while one was open for 0% -> 0% of each run, Pallas kernels for 4% -> 4%
where the time goes in v8:
time: 89.5 us; the launch traced here: 89.2 us
  waiting for transfers between devices  68.2 us (76%)
  starting transfers between devices  10.5 us (12%)
  Pallas kernels  10.2 us (11%)
    ppermute x1, waiting for transfers between devices, shards(): chips = [pair, lax.ppermute(pair, 'prow', [(i ^ 4, i) for i in range(n)])]  37.3 us
    ppermute x1, waiting for transfers between devices, shards(): lax.ppermute(held, 'prow', [(i ^ 2, i) for i in range(n)])  20.5 us
    all_to_all x1, waiting for transfers between devices, shards(): recv = lax.all_to_all(send, 'prow', split_axis=0, concat_axis=0, tiled=True)  8.9 us
    all_to_all x1, starting transfers between devices, shards(): recv = lax.all_to_all(send, 'prow', split_axis=0, concat_axis=0, tiled=True)  6.41 us
    pallas_call x1, Pallas kernels, shards(): pl.pallas_call(functools.partial(level_kernel, n, quad), out_shape=jax.Sh...  4.82 us
    pallas_call x1, Pallas kernels, shards(): pl.pallas_call(functools.partial(pack_kernel, n, cols), out_shape=jax.Sha...  4 us
    ppermute x1, starting transfers between devices, shards(): lax.ppermute(diag, 'prow', [((i + t * quad) % n, i) for i in range(n)])  2.37 us
  transfers between devices with their start and end apart: 5, of which 4 were waited for; matrix products, arithmetic and copies ran while one was open for 0% of the time, Pallas kernels for 4%

profile of v8, /device:TPU:13, one launch (start us, length us, event | category | flops | bytes accessed | tf_op | source)
XLA Modules:
  0.0 89.2 jit_solution(1238816407252615403)
XLA Ops:
  0.0 1.4 %shard_map.47 = bf16[1,2,128,128]{3,2,1,0:T(8,128)(2,1)} custom-call(s32[1]{0:T(128)} %bitcast.me_ref, bf16[2,32,128,128]{3,2,1,0:T(8,128)(2,1)} %inv_ref.3), custom_call_target="tpu_custom_call" | custom-call | tf_op jit(solution)/shard_map/pallas_call | solution.py:108
  1.4 2.4 %collective-permute-start = (bf16[1,2,128,128]{3,2,1,0:T(8,128)(2,1)}, bf16[1,2,128,128]{3,2,1,0:T(8,128)(2,1)S(1)}, u32[]{:S(2)}, u32[]{:S(2)}) collective-permute-start(bf16[1,2,128,128]{3,2,1,0:T(8,128)(2,1)} %shard_map.47), channel_id=1, source_target_pairs={{8,0},{9,1},{10,2},{11,3},{12,4},{13,5},{14,6},{15,7},{0,8},{1,9},... | collective-permute-start | bytes 196616 | tf_op jit(solution)/shard_map/ppermute | solution.py:115
  3.8 4.0 %shard_map.46 = bf16[16,2,3,128,128]{4,3,2,1,0:T(8,128)(2,1)} custom-call(s32[1]{0:T(128)} %bitcast.me_ref, s32[4,128]{1,0:T(4,128)} %bitcast.4, bf16[2,32,128,128]{3,2,1,0:T(8,128)(2,1)} %inv_ref.3), custom_call_target="tpu_custom_call" | custom-call | tf_op jit(solution)/shard_map/pallas_call | solution.py:118
  7.8 0.0 copy-start.3
  7.8 0.0 copy-start
  7.8 0.0 copy-start.1
  7.8 0.0 copy-start.2
  7.9 0.0 collective-permute-done
  7.9 6.4 %all-to-all-start = ((bf16[16,2,3,128,128]{4,3,2,1,0:T(8,128)(2,1)}), bf16[16,2,3,128,128]{4,3,2,1,0:T(8,128)(2,1)}, u32[]{:S(2)}, u32[]{:S(2)}) async-start(bf16[16,2,3,128,128]{4,3,2,1,0:T(8,128)(2,1)} %shard_map.46), calls=%async_computation | async-start | bytes 6291456 | tf_op jit(solution)/shard_map/all_to_all | solution.py:135
  14.3 0.0 copy-done.3
  14.3 0.3 collective-permute-start.1
  14.7 20.5 %collective-permute-done.1 = bf16[2,2,128,128]{3,2,1,0:T(8,128)(2,1)S(1)} collective-permute-done((bf16[2,2,128,128]{3,2,1,0:T(8,128)(2,1)S(1)}, bf16[2,2,128,128]{3,2,1,0:T(8,128)(2,1)S(1)}, u32[]{:S(2)}, u32[]{:S(2)}) %collective-permute-start.1) | collective-permute-done | bytes 131104 | tf_op jit(solution)/shard_map/ppermute | solution.py:138
  35.2 0.4 collective-permute-start.2
  35.6 37.3 %collective-permute-done.2 = bf16[4,2,128,128]{3,2,1,0:T(8,128)(2,1)S(1)} collective-permute-done((bf16[4,2,128,128]{3,2,1,0:T(8,128)(2,1)S(1)}, bf16[4,2,128,128]{3,2,1,0:T(8,128)(2,1)S(1)}, u32[]{:S(2)}, u32[]{:S(2)}) %collective-permute-start.2) | collective-permute-done | bytes 262176 | tf_op jit(solution)/shard_map/ppermute | solution.py:139
  72.9 0.1 pad_maximum_fusion.rest_0_
  72.9 0.9 %collective-permute-start.3 = (bf16[8,2,128,128]{3,2,1,0:T(8,128)(2,1)S(1)}, bf16[8,2,128,128]{3,2,1,0:T(8,128)(2,1)S(1)}, u32[]{:S(2)}, u32[]{:S(2)}) collective-permute-start(bf16[8,2,128,128]{3,2,1,0:T(8,128)(2,1)S(1)} %pad_maximum_fusion.rest_0_), channel_id=1, source_target_pairs={{1,0},{0,1},{3,2},{2,3},{5,4},{4,5},{7,6},{6,7},{9,8},{8,9},{11,10... | collective-permute-start | bytes 1572872 | tf_op jit(solution)/shard_map/ppermute | solution.py:141
  73.9 1.5 %collective-permute-done.3.rest_1_ = bf16[8,2,128,128]{3,2,1,0:T(8,128)(2,1)S(1)} collective-permute-done((bf16[8,2,128,128]{3,2,1,0:T(8,128)(2,1)S(1)}, bf16[8,2,128,128]{3,2,1,0:T(8,128)(2,1)S(1)}, u32[]{:S(2)}, u32[]{:S(2)}) %collective-permute-start.3) | collective-permute-done | bytes 524320 | tf_op jit(solution)/shard_map/ppermute | solution.py:141
  75.4 8.9 %all-to-all-done.recv_ref = bf16[16,2,3,128,128]{4,3,2,1,0:T(8,128)(2,1)} async-done(((bf16[16,2,3,128,128]{4,3,2,1,0:T(8,128)(2,1)}), bf16[16,2,3,128,128]{4,3,2,1,0:T(8,128)(2,1)}, u32[]{:S(2)}, u32[]{:S(2)}) %all-to-all-start) | async-done | bytes 3145760 | tf_op jit(solution)/shard_map/all_to_all | solution.py:135
  84.3 0.0 copy-done
  84.3 0.0 copy-done.1
  84.3 0.0 copy-done.2
  84.3 4.8 %shard_map.48 = f32[8,128,128]{2,1,0:T(8,128)} custom-call(s32[1]{0:T(128)} %bitcast.me_ref, s32[4,128]{1,0:T(4,128)S(1)} %bitcast.5, bf16[16,2,3,128,128]{4,3,2,1,0:T(8,128)(2,1)} %all-to-all-done.recv_ref, bf16[8,2,128,128]{3,2,1,0:T(8,128)(2,1)S(1)} %pad_maximum_fusion.rest_0_, bf16[8,2,128,128]{3,2,1,0:T(8,128)(2,1)S(1)} %collective-permute-done.3.rest_1_, ...), custom_call_target="tpu_custom_call" | custom-call | tf_op jit(solution)/shard_map/pallas_call | solution.py:143
  (2 shorter events, 0.0 us)
Async XLA Ops:
  1.4 6.4 %collective-permute-start = (bf16[1,2,128,128]{3,2,1,0:T(8,128)(2,1)}, bf16[1,2,128,128]{3,2,1,0:T(8,128)(2,1)S(1)}, u32[]{:S(2)}, u32[]{:S(2)}) collective-permute-start(bf16[1,2,128,128]{3,2,1,0:T(8,128)(2,1)} %shard_map.47), channel_id=1, source_target_pairs={{8,0},{9,1},{10,2},{11,3},{12,4},{13,5},{14,6},{15,7},{0,8},{1,9},... | collective-permute-start | bytes 196616 | tf_op jit(solution)/shard_map/ppermute | solution.py:115
  7.8 6.5 %copy-start.3 = (bf16[1,2,128,128]{3,2,1,0:T(8,128)(2,1)S(1)}, bf16[1,2,128,128]{3,2,1,0:T(8,128)(2,1)}, u32[]{:S(2)}) copy-start(bf16[1,2,128,128]{3,2,1,0:T(8,128)(2,1)} %shard_map.47) | copy-start | bytes 196612
  7.8 76.5 %copy-start = (bf16[8,4,128,128]{3,2,1,0:T(8,128)(2,1)S(1)}, bf16[8,4,128,128]{3,2,1,0:T(8,128)(2,1)}, u32[]{:S(2)}) copy-start(bf16[8,4,128,128]{3,2,1,0:T(8,128)(2,1)} %param.4) | copy-start | bytes 3145732
  7.8 76.5 %copy-start.1 = (f32[8,128,128]{2,1,0:T(8,128)S(1)}, f32[8,128,128]{2,1,0:T(8,128)}, u32[]{:S(2)}) copy-start(f32[8,128,128]{2,1,0:T(8,128)} %rest_3_.1) | copy-start | bytes 1572868
  7.8 76.5 %copy-start.2 = (s32[128,4]{0,1:T(4,128)S(1)}, s32[128,4]{0,1:T(4,128)}, u32[]{:S(2)}) copy-start(s32[128,4]{0,1:T(4,128)} %param.7) | copy-start | bytes 6148
  7.9 76.5 %all-to-all-start = ((bf16[16,2,3,128,128]{4,3,2,1,0:T(8,128)(2,1)}), bf16[16,2,3,128,128]{4,3,2,1,0:T(8,128)(2,1)}, u32[]{:S(2)}, u32[]{:S(2)}) async-start(bf16[16,2,3,128,128]{4,3,2,1,0:T(8,128)(2,1)} %shard_map.46), calls=%async_computation | async-start | bytes 6291456 | tf_op jit(solution)/shard_map/all_to_all | solution.py:135
  14.3 20.8 %collective-permute-start.1 = (bf16[2,2,128,128]{3,2,1,0:T(8,128)(2,1)S(1)}, bf16[2,2,128,128]{3,2,1,0:T(8,128)(2,1)S(1)}, u32[]{:S(2)}, u32[]{:S(2)}) collective-permute-start(bf16[2,2,128,128]{3,2,1,0:T(8,128)(2,1)S(1)} %pad_maximum_fusion.2), channel_id=1, source_target_pairs={{2,0},{3,1},{0,2},{1,3},{6,4},{7,5},{4,6},{5,7},{10,8},{11,9},{8,1... | collective-permute-start | bytes 393224 | tf_op jit(solution)/shard_map/ppermute | solution.py:138
  35.2 37.7 %collective-permute-start.2 = (bf16[4,2,128,128]{3,2,1,0:T(8,128)(2,1)S(1)}, bf16[4,2,128,128]{3,2,1,0:T(8,128)(2,1)S(1)}, u32[]{:S(2)}, u32[]{:S(2)}) collective-permute-start(bf16[4,2,128,128]{3,2,1,0:T(8,128)(2,1)S(1)} %pad_maximum_fusion.1), channel_id=1, source_target_pairs={{4,0},{5,1},{6,2},{7,3},{0,4},{1,5},{2,6},{3,7},{12,8},{13,9},{14,... | collective-permute-start | bytes 786440 | tf_op jit(solution)/shard_map/ppermute | solution.py:139
  72.9 2.5 %collective-permute-start.3 = (bf16[8,2,128,128]{3,2,1,0:T(8,128)(2,1)S(1)}, bf16[8,2,128,128]{3,2,1,0:T(8,128)(2,1)S(1)}, u32[]{:S(2)}, u32[]{:S(2)}) collective-permute-start(bf16[8,2,128,128]{3,2,1,0:T(8,128)(2,1)S(1)} %pad_maximum_fusion.rest_0_), channel_id=1, source_target_pairs={{1,0},{0,1},{3,2},{2,3},{5,4},{4,5},{7,6},{6,7},{9,8},{8,9},{11,10... | collective-permute-start | bytes 1572872 | tf_op jit(solution)/shard_map/ppermute | solution.py:141

commit v9 on v8

--- a/solution.py
+++ b/solution.py
@@ -58,9 +58,10 @@
 
 def level_kernel(n, quad, me_ref, st_ref, recv_ref, *rest):
     diag_refs, rest = rest[:2], rest[2:]
-    fac_ref, dfi_ref, out_ref, diag_v, line_v, product_v, out_v, sems, sem_o = rest
-    cols, deep, width = fac_ref.shape
-    length = deep // width
+    fac_ref, dfi_ref, out_ref, diag_v, line_v, product_v, out_v, where_s, sems, sem_o = rest
+    cols, width, _ = dfi_ref.shape
+    length = fac_ref.shape[0] // cols
+    ancestors = diag_v.shape[0]
     rows = recv_ref.shape[1]
     steps = n // quad
     me = me_ref[0]
@@ -72,22 +73,37 @@
     ]
     for f in fetch:
         f.start()
+    if ancestors > cols * length:
+
+        def no_place(i, carry):
+            where_s[i] = cols * length
+            return carry
+
+        lax.fori_loop(0, ancestors, no_place, 0)
+    for k in range(cols):
+        for r in range(length):
+            where_s[st_ref[r, me * cols + k]] = k * length + r
     for a in range(2):
         for t in range(diag_refs[a].shape[0]):
             owner = lax.bitwise_xor(lax.rem(me + t % steps * quad, n), t // steps * 2 + a)
             diag_v[pl.ds(owner * rows, rows)] = diag_refs[a][t]
-    ancs = [[st_ref[r, me * cols + k] for r in range(length)] for k in range(cols)]
-    for f in fetch:
+    for i, f in enumerate(fetch):
         f.wait()
+        for owner in range(i * each, (i + 1) * each):
+            for j in range(rows):
+                anc = owner * rows + j
+                at = where_s[anc]
+                own = lax.min(at, cols * length - 1)
+                r = lax.rem(own, length)
+                mates = [own - r + q + (q >= r).astype(jnp.int32) for q in range(length - 1)]
+                line = jnp.concatenate([line_v[owner, j, q] for q in range(length - 1)] + [diag_v[anc]], axis=1)
+                facs = jnp.concatenate([fac_ref[at_q] for at_q in mates + [own]], axis=0)
+                part = jnp.dot(line, facs, preferred_element_type=jnp.float32)
+                product_v[at] = part.astype(jnp.bfloat16)
     for k in range(cols):
-        for r, anc in enumerate(ancs[k]):
-            owner, local = lax.div(anc, rows), lax.rem(anc, rows)
-            line = [diag_v[anc] if s == r else line_v[owner, local, s if s < r else s - 1] for s in range(length)]
-            line = jnp.concatenate(line, axis=1)
-            part = jnp.dot(line, fac_ref[k], preferred_element_type=jnp.float32)
-            product_v[k, r * width : (r + 1) * width, :] = part.astype(jnp.bfloat16)
-    for k in range(cols):
-        term = lax.dot_general(fac_ref[k], product_v[k], (((0,), (0,)), ((), ())), preferred_element_type=jnp.float32)
+        blocks = pl.ds(k * length, length)
+        fac, product = fac_ref[blocks].reshape(length * width, width), product_v[blocks].reshape(length * width, width)
+        term = lax.dot_general(fac, product, (((0,), (0,)), ((), ())), preferred_element_type=jnp.float32)
         out_v[k] = dfi_ref[k] + term
     pltpu.make_async_copy(out_v, out_ref, sem_o).start()
     pltpu.make_async_copy(out_v, out_ref, sem_o).wait()
@@ -148,13 +164,14 @@
         scratch_shapes=[
             pltpu.VMEM((ancestors, width, width), jnp.bfloat16),
             pltpu.VMEM(recv.shape, jnp.bfloat16),
-            pltpu.VMEM((cols, deep, width), jnp.bfloat16),
+            pltpu.VMEM((cols * length + 1, width, width), jnp.bfloat16),
             pltpu.VMEM((cols, width, width), jnp.float32),
-            pltpu.SemaphoreType.DMA((8,)),
+            pltpu.SMEM((ancestors,), jnp.int32),
+            pltpu.SemaphoreType.DMA((4,)),
             pltpu.SemaphoreType.DMA,
         ],
         compiler_params=pltpu.CompilerParams(vmem_limit_bytes=51 * 2**20),
-    )(me1, structure.T, recv, *spread, factor_blocks.reshape(cols, deep, width), diag_factor_inv)
+    )(me1, structure.T, recv, *spread, factor_blocks.reshape(cols * length, width, width), diag_factor_inv)
 
 
 def solution(mesh):

time: 89.5 us -> 89.4 us (level)
  no operation moved by 1% of the time
where the time goes in v9:
time: 89.4 us; the launch traced here: 89.1 us
  waiting for transfers between devices  68.2 us (76%)
  starting transfers between devices  10.5 us (12%)
  Pallas kernels  10.2 us (11%)
    ppermute x1, waiting for transfers between devices, shards(): chips = [pair, lax.ppermute(pair, 'prow', [(i ^ 4, i) for i in range(n)])]  37.3 us
    ppermute x1, waiting for transfers between devices, shards(): lax.ppermute(held, 'prow', [(i ^ 2, i) for i in range(n)])  20.5 us
    all_to_all x1, waiting for transfers between devices, shards(): recv = lax.all_to_all(send, 'prow', split_axis=0, concat_axis=0, tiled=True)  8.9 us
    all_to_all x1, starting transfers between devices, shards(): recv = lax.all_to_all(send, 'prow', split_axis=0, concat_axis=0, tiled=True)  6.41 us
    pallas_call x1, Pallas kernels, shards(): pl.pallas_call(functools.partial(level_kernel, n, quad), out_shape=jax.Sh...  4.77 us
    pallas_call x1, Pallas kernels, shards(): pl.pallas_call(functools.partial(pack_kernel, n, cols), out_shape=jax.Sha...  4 us
    ppermute x1, starting transfers between devices, shards(): lax.ppermute(diag, 'prow', [((i + t * quad) % n, i) for i in range(n)])  2.37 us
  transfers between devices with their start and end apart: 5, of which 4 were waited for; matrix products, arithmetic and copies ran while one was open for 0% of the time, Pallas kernels for 4%

profile of v9, /device:TPU:13, one launch (start us, length us, event | category | flops | bytes accessed | tf_op | source)
XLA Modules:
  0.0 89.1 jit_solution(7766689849215377955)
XLA Ops:
  0.0 1.4 %shard_map.47 = bf16[1,2,128,128]{3,2,1,0:T(8,128)(2,1)} custom-call(s32[1]{0:T(128)} %bitcast.me_ref, bf16[2,32,128,128]{3,2,1,0:T(8,128)(2,1)} %inv_ref.3), custom_call_target="tpu_custom_call" | custom-call | tf_op jit(solution)/shard_map/pallas_call | solution.py:124
  1.4 2.4 %collective-permute-start = (bf16[1,2,128,128]{3,2,1,0:T(8,128)(2,1)}, bf16[1,2,128,128]{3,2,1,0:T(8,128)(2,1)S(1)}, u32[]{:S(2)}, u32[]{:S(2)}) collective-permute-start(bf16[1,2,128,128]{3,2,1,0:T(8,128)(2,1)} %shard_map.47), channel_id=1, source_target_pairs={{8,0},{9,1},{10,2},{11,3},{12,4},{13,5},{14,6},{15,7},{0,8},{1,9},... | collective-permute-start | bytes 196616 | tf_op jit(solution)/shard_map/ppermute | solution.py:131
  3.8 4.0 %shard_map.46 = bf16[16,2,3,128,128]{4,3,2,1,0:T(8,128)(2,1)} custom-call(s32[1]{0:T(128)} %bitcast.me_ref, s32[4,128]{1,0:T(4,128)} %bitcast.4, bf16[2,32,128,128]{3,2,1,0:T(8,128)(2,1)} %inv_ref.3), custom_call_target="tpu_custom_call" | custom-call | tf_op jit(solution)/shard_map/pallas_call | solution.py:134
  7.8 0.0 copy-start.3
  7.8 0.0 copy-start
  7.8 0.0 copy-start.1
  7.8 0.0 copy-start.2
  7.9 0.0 collective-permute-done
  7.9 6.4 %all-to-all-start = ((bf16[16,2,3,128,128]{4,3,2,1,0:T(8,128)(2,1)}), bf16[16,2,3,128,128]{4,3,2,1,0:T(8,128)(2,1)}, u32[]{:S(2)}, u32[]{:S(2)}) async-start(bf16[16,2,3,128,128]{4,3,2,1,0:T(8,128)(2,1)} %shard_map.46), calls=%async_computation | async-start | bytes 6291456 | tf_op jit(solution)/shard_map/all_to_all | solution.py:151
  14.3 0.0 copy-done.3
  14.3 0.3 collective-permute-start.1
  14.7 20.5 %collective-permute-done.1 = bf16[2,2,128,128]{3,2,1,0:T(8,128)(2,1)S(1)} collective-permute-done((bf16[2,2,128,128]{3,2,1,0:T(8,128)(2,1)S(1)}, bf16[2,2,128,128]{3,2,1,0:T(8,128)(2,1)S(1)}, u32[]{:S(2)}, u32[]{:S(2)}) %collective-permute-start.1) | collective-permute-done | bytes 131104 | tf_op jit(solution)/shard_map/ppermute | solution.py:154
  35.2 0.4 collective-permute-start.2
  35.6 37.3 %collective-permute-done.2 = bf16[4,2,128,128]{3,2,1,0:T(8,128)(2,1)S(1)} collective-permute-done((bf16[4,2,128,128]{3,2,1,0:T(8,128)(2,1)S(1)}, bf16[4,2,128,128]{3,2,1,0:T(8,128)(2,1)S(1)}, u32[]{:S(2)}, u32[]{:S(2)}) %collective-permute-start.2) | collective-permute-done | bytes 262176 | tf_op jit(solution)/shard_map/ppermute | solution.py:155
  72.9 0.1 pad_maximum_fusion.rest_0_
  72.9 0.9 %collective-permute-start.3 = (bf16[8,2,128,128]{3,2,1,0:T(8,128)(2,1)S(1)}, bf16[8,2,128,128]{3,2,1,0:T(8,128)(2,1)S(1)}, u32[]{:S(2)}, u32[]{:S(2)}) collective-permute-start(bf16[8,2,128,128]{3,2,1,0:T(8,128)(2,1)S(1)} %pad_maximum_fusion.rest_0_), channel_id=1, source_target_pairs={{1,0},{0,1},{3,2},{2,3},{5,4},{4,5},{7,6},{6,7},{9,8},{8,9},{11,10... | collective-permute-start | bytes 1572872 | tf_op jit(solution)/shard_map/ppermute | solution.py:157
  73.9 1.5 %collective-permute-done.3.rest_1_ = bf16[8,2,128,128]{3,2,1,0:T(8,128)(2,1)S(1)} collective-permute-done((bf16[8,2,128,128]{3,2,1,0:T(8,128)(2,1)S(1)}, bf16[8,2,128,128]{3,2,1,0:T(8,128)(2,1)S(1)}, u32[]{:S(2)}, u32[]{:S(2)}) %collective-permute-start.3) | collective-permute-done | bytes 524320 | tf_op jit(solution)/shard_map/ppermute | solution.py:157
  75.4 8.9 %all-to-all-done.recv_ref = bf16[16,2,3,128,128]{4,3,2,1,0:T(8,128)(2,1)} async-done(((bf16[16,2,3,128,128]{4,3,2,1,0:T(8,128)(2,1)}), bf16[16,2,3,128,128]{4,3,2,1,0:T(8,128)(2,1)}, u32[]{:S(2)}, u32[]{:S(2)}) %all-to-all-start) | async-done | bytes 3145760 | tf_op jit(solution)/shard_map/all_to_all | solution.py:151
  84.3 0.0 copy-done
  84.3 0.0 copy-done.1
  84.3 0.0 copy-done.2
  84.3 4.8 %shard_map.48 = f32[8,128,128]{2,1,0:T(8,128)} custom-call(s32[1]{0:T(128)} %bitcast.me_ref, s32[4,128]{1,0:T(4,128)S(1)} %bitcast.5, bf16[16,2,3,128,128]{4,3,2,1,0:T(8,128)(2,1)} %all-to-all-done.recv_ref, bf16[8,2,128,128]{3,2,1,0:T(8,128)(2,1)S(1)} %pad_maximum_fusion.rest_0_, bf16[8,2,128,128]{3,2,1,0:T(8,128)(2,1)S(1)} %collective-permute-done.3.rest_1_, ...), custom_call_target="tpu_custom_call" | custom-call | tf_op jit(solution)/shard_map/pallas_call | solution.py:159
  (2 shorter events, 0.0 us)
Async XLA Ops:
  1.4 6.4 %collective-permute-start = (bf16[1,2,128,128]{3,2,1,0:T(8,128)(2,1)}, bf16[1,2,128,128]{3,2,1,0:T(8,128)(2,1)S(1)}, u32[]{:S(2)}, u32[]{:S(2)}) collective-permute-start(bf16[1,2,128,128]{3,2,1,0:T(8,128)(2,1)} %shard_map.47), channel_id=1, source_target_pairs={{8,0},{9,1},{10,2},{11,3},{12,4},{13,5},{14,6},{15,7},{0,8},{1,9},... | collective-permute-start | bytes 196616 | tf_op jit(solution)/shard_map/ppermute | solution.py:131
  7.8 6.5 %copy-start.3 = (bf16[1,2,128,128]{3,2,1,0:T(8,128)(2,1)S(1)}, bf16[1,2,128,128]{3,2,1,0:T(8,128)(2,1)}, u32[]{:S(2)}) copy-start(bf16[1,2,128,128]{3,2,1,0:T(8,128)(2,1)} %shard_map.47) | copy-start | bytes 196612
  7.8 76.5 %copy-start = (bf16[8,4,128,128]{3,2,1,0:T(8,128)(2,1)S(1)}, bf16[8,4,128,128]{3,2,1,0:T(8,128)(2,1)}, u32[]{:S(2)}) copy-start(bf16[8,4,128,128]{3,2,1,0:T(8,128)(2,1)} %param.4) | copy-start | bytes 3145732
  7.8 76.5 %copy-start.1 = (f32[8,128,128]{2,1,0:T(8,128)S(1)}, f32[8,128,128]{2,1,0:T(8,128)}, u32[]{:S(2)}) copy-start(f32[8,128,128]{2,1,0:T(8,128)} %rest_3_.1) | copy-start | bytes 1572868
  7.8 76.5 %copy-start.2 = (s32[128,4]{0,1:T(4,128)S(1)}, s32[128,4]{0,1:T(4,128)}, u32[]{:S(2)}) copy-start(s32[128,4]{0,1:T(4,128)} %param.7) | copy-start | bytes 6148
  7.9 76.5 %all-to-all-start = ((bf16[16,2,3,128,128]{4,3,2,1,0:T(8,128)(2,1)}), bf16[16,2,3,128,128]{4,3,2,1,0:T(8,128)(2,1)}, u32[]{:S(2)}, u32[]{:S(2)}) async-start(bf16[16,2,3,128,128]{4,3,2,1,0:T(8,128)(2,1)} %shard_map.46), calls=%async_computation | async-start | bytes 6291456 | tf_op jit(solution)/shard_map/all_to_all | solution.py:151
  14.3 20.8 %collective-permute-start.1 = (bf16[2,2,128,128]{3,2,1,0:T(8,128)(2,1)S(1)}, bf16[2,2,128,128]{3,2,1,0:T(8,128)(2,1)S(1)}, u32[]{:S(2)}, u32[]{:S(2)}) collective-permute-start(bf16[2,2,128,128]{3,2,1,0:T(8,128)(2,1)S(1)} %pad_maximum_fusion.2), channel_id=1, source_target_pairs={{2,0},{3,1},{0,2},{1,3},{6,4},{7,5},{4,6},{5,7},{10,8},{11,9},{8,1... | collective-permute-start | bytes 393224 | tf_op jit(solution)/shard_map/ppermute | solution.py:154
  35.2 37.7 %collective-permute-start.2 = (bf16[4,2,128,128]{3,2,1,0:T(8,128)(2,1)S(1)}, bf16[4,2,128,128]{3,2,1,0:T(8,128)(2,1)S(1)}, u32[]{:S(2)}, u32[]{:S(2)}) collective-permute-start(bf16[4,2,128,128]{3,2,1,0:T(8,128)(2,1)S(1)} %pad_maximum_fusion.1), channel_id=1, source_target_pairs={{4,0},{5,1},{6,2},{7,3},{0,4},{1,5},{2,6},{3,7},{12,8},{13,9},{14,... | collective-permute-start | bytes 786440 | tf_op jit(solution)/shard_map/ppermute | solution.py:155
  72.9 2.5 %collective-permute-start.3 = (bf16[8,2,128,128]{3,2,1,0:T(8,128)(2,1)S(1)}, bf16[8,2,128,128]{3,2,1,0:T(8,128)(2,1)S(1)}, u32[]{:S(2)}, u32[]{:S(2)}) collective-permute-start(bf16[8,2,128,128]{3,2,1,0:T(8,128)(2,1)S(1)} %pad_maximum_fusion.rest_0_), channel_id=1, source_target_pairs={{1,0},{0,1},{3,2},{2,3},{5,4},{4,5},{7,6},{6,7},{9,8},{8,9},{11,10... | collective-permute-start | bytes 1572872 | tf_op jit(solution)/shard_map/ppermute | solution.py:157

commit v10 on v9

--- a/solution.py
+++ b/solution.py
@@ -167,7 +167,7 @@
             pltpu.VMEM((cols * length + 1, width, width), jnp.bfloat16),
             pltpu.VMEM((cols, width, width), jnp.float32),
             pltpu.SMEM((ancestors,), jnp.int32),
-            pltpu.SemaphoreType.DMA((4,)),
+            pltpu.SemaphoreType.DMA((2,)),
             pltpu.SemaphoreType.DMA,
         ],
         compiler_params=pltpu.CompilerParams(vmem_limit_bytes=51 * 2**20),

time: 89.4 us -> 89.3 us (level)
  no operation moved by 1% of the time
where the time goes in v10:
time: 89.3 us; the launch traced here: 89 us
  waiting for transfers between devices  68.2 us (76%)
  starting transfers between devices  10.5 us (12%)
  Pallas kernels  10.1 us (11%)
    ppermute x1, waiting for transfers between devices, shards(): chips = [pair, lax.ppermute(pair, 'prow', [(i ^ 4, i) for i in range(n)])]  37.3 us
    ppermute x1, waiting for transfers between devices, shards(): lax.ppermute(held, 'prow', [(i ^ 2, i) for i in range(n)])  20.5 us
    all_to_all x1, waiting for transfers between devices, shards(): recv = lax.all_to_all(send, 'prow', split_axis=0, concat_axis=0, tiled=True)  8.9 us
    all_to_all x1, starting transfers between devices, shards(): recv = lax.all_to_all(send, 'prow', split_axis=0, concat_axis=0, tiled=True)  6.41 us
    pallas_call x1, Pallas kernels, shards(): pl.pallas_call(functools.partial(level_kernel, n, quad), out_shape=jax.Sh...  4.71 us
    pallas_call x1, Pallas kernels, shards(): pl.pallas_call(functools.partial(pack_kernel, n, cols), out_shape=jax.Sha...  4 us
    ppermute x1, starting transfers between devices, shards(): lax.ppermute(diag, 'prow', [((i + t * quad) % n, i) for i in range(n)])  2.37 us
  transfers between devices with their start and end apart: 5, of which 4 were waited for; matrix products, arithmetic and copies ran while one was open for 0% of the time, Pallas kernels for 4%

profile of v10, /device:TPU:13, one launch (start us, length us, event | category | flops | bytes accessed | tf_op | source)
XLA Modules:
  0.0 89.0 jit_solution(2827202195138326650)
XLA Ops:
  0.0 1.4 %shard_map.47 = bf16[1,2,128,128]{3,2,1,0:T(8,128)(2,1)} custom-call(s32[1]{0:T(128)} %bitcast.me_ref, bf16[2,32,128,128]{3,2,1,0:T(8,128)(2,1)} %inv_ref.3), custom_call_target="tpu_custom_call" | custom-call | tf_op jit(solution)/shard_map/pallas_call | solution.py:124
  1.4 2.4 %collective-permute-start = (bf16[1,2,128,128]{3,2,1,0:T(8,128)(2,1)}, bf16[1,2,128,128]{3,2,1,0:T(8,128)(2,1)S(1)}, u32[]{:S(2)}, u32[]{:S(2)}) collective-permute-start(bf16[1,2,128,128]{3,2,1,0:T(8,128)(2,1)} %shard_map.47), channel_id=1, source_target_pairs={{8,0},{9,1},{10,2},{11,3},{12,4},{13,5},{14,6},{15,7},{0,8},{1,9},... | collective-permute-start | bytes 196616 | tf_op jit(solution)/shard_map/ppermute | solution.py:131
  3.8 4.0 %shard_map.46 = bf16[16,2,3,128,128]{4,3,2,1,0:T(8,128)(2,1)} custom-call(s32[1]{0:T(128)} %bitcast.me_ref, s32[4,128]{1,0:T(4,128)} %bitcast.4, bf16[2,32,128,128]{3,2,1,0:T(8,128)(2,1)} %inv_ref.3), custom_call_target="tpu_custom_call" | custom-call | tf_op jit(solution)/shard_map/pallas_call | solution.py:134
  7.8 0.0 copy-start.3
  7.8 0.0 copy-start
  7.8 0.0 copy-start.1
  7.8 0.0 copy-start.2
  7.9 0.0 collective-permute-done
  7.9 6.4 %all-to-all-start = ((bf16[16,2,3,128,128]{4,3,2,1,0:T(8,128)(2,1)}), bf16[16,2,3,128,128]{4,3,2,1,0:T(8,128)(2,1)}, u32[]{:S(2)}, u32[]{:S(2)}) async-start(bf16[16,2,3,128,128]{4,3,2,1,0:T(8,128)(2,1)} %shard_map.46), calls=%async_computation | async-start | bytes 6291456 | tf_op jit(solution)/shard_map/all_to_all | solution.py:151
  14.3 0.0 copy-done.3
  14.3 0.3 collective-permute-start.1
  14.7 20.5 %collective-permute-done.1 = bf16[2,2,128,128]{3,2,1,0:T(8,128)(2,1)S(1)} collective-permute-done((bf16[2,2,128,128]{3,2,1,0:T(8,128)(2,1)S(1)}, bf16[2,2,128,128]{3,2,1,0:T(8,128)(2,1)S(1)}, u32[]{:S(2)}, u32[]{:S(2)}) %collective-permute-start.1) | collective-permute-done | bytes 131104 | tf_op jit(solution)/shard_map/ppermute | solution.py:154
  35.2 0.4 collective-permute-start.2
  35.6 37.3 %collective-permute-done.2 = bf16[4,2,128,128]{3,2,1,0:T(8,128)(2,1)S(1)} collective-permute-done((bf16[4,2,128,128]{3,2,1,0:T(8,128)(2,1)S(1)}, bf16[4,2,128,128]{3,2,1,0:T(8,128)(2,1)S(1)}, u32[]{:S(2)}, u32[]{:S(2)}) %collective-permute-start.2) | collective-permute-done | bytes 262176 | tf_op jit(solution)/shard_map/ppermute | solution.py:155
  72.9 0.1 pad_maximum_fusion.rest_0_
  72.9 0.9 %collective-permute-start.3 = (bf16[8,2,128,128]{3,2,1,0:T(8,128)(2,1)S(1)}, bf16[8,2,128,128]{3,2,1,0:T(8,128)(2,1)S(1)}, u32[]{:S(2)}, u32[]{:S(2)}) collective-permute-start(bf16[8,2,128,128]{3,2,1,0:T(8,128)(2,1)S(1)} %pad_maximum_fusion.rest_0_), channel_id=1, source_target_pairs={{1,0},{0,1},{3,2},{2,3},{5,4},{4,5},{7,6},{6,7},{9,8},{8,9},{11,10... | collective-permute-start | bytes 1572872 | tf_op jit(solution)/shard_map/ppermute | solution.py:157
  73.9 1.5 %collective-permute-done.3.rest_1_ = bf16[8,2,128,128]{3,2,1,0:T(8,128)(2,1)S(1)} collective-permute-done((bf16[8,2,128,128]{3,2,1,0:T(8,128)(2,1)S(1)}, bf16[8,2,128,128]{3,2,1,0:T(8,128)(2,1)S(1)}, u32[]{:S(2)}, u32[]{:S(2)}) %collective-permute-start.3) | collective-permute-done | bytes 524320 | tf_op jit(solution)/shard_map/ppermute | solution.py:157
  75.4 8.9 %all-to-all-done.recv_ref = bf16[16,2,3,128,128]{4,3,2,1,0:T(8,128)(2,1)} async-done(((bf16[16,2,3,128,128]{4,3,2,1,0:T(8,128)(2,1)}), bf16[16,2,3,128,128]{4,3,2,1,0:T(8,128)(2,1)}, u32[]{:S(2)}, u32[]{:S(2)}) %all-to-all-start) | async-done | bytes 3145760 | tf_op jit(solution)/shard_map/all_to_all | solution.py:151
  84.3 0.0 copy-done
  84.3 0.0 copy-done.1
  84.3 0.0 copy-done.2
  84.3 4.7 %shard_map.48 = f32[8,128,128]{2,1,0:T(8,128)} custom-call(s32[1]{0:T(128)} %bitcast.me_ref, s32[4,128]{1,0:T(4,128)S(1)} %bitcast.5, bf16[16,2,3,128,128]{4,3,2,1,0:T(8,128)(2,1)} %all-to-all-done.recv_ref, bf16[8,2,128,128]{3,2,1,0:T(8,128)(2,1)S(1)} %pad_maximum_fusion.rest_0_, bf16[8,2,128,128]{3,2,1,0:T(8,128)(2,1)S(1)} %collective-permute-done.3.rest_1_, ...), custom_call_target="tpu_custom_call" | custom-call | tf_op jit(solution)/shard_map/pallas_call | solution.py:159
  (2 shorter events, 0.0 us)
Async XLA Ops:
  1.4 6.4 %collective-permute-start = (bf16[1,2,128,128]{3,2,1,0:T(8,128)(2,1)}, bf16[1,2,128,128]{3,2,1,0:T(8,128)(2,1)S(1)}, u32[]{:S(2)}, u32[]{:S(2)}) collective-permute-start(bf16[1,2,128,128]{3,2,1,0:T(8,128)(2,1)} %shard_map.47), channel_id=1, source_target_pairs={{8,0},{9,1},{10,2},{11,3},{12,4},{13,5},{14,6},{15,7},{0,8},{1,9},... | collective-permute-start | bytes 196616 | tf_op jit(solution)/shard_map/ppermute | solution.py:131
  7.8 6.5 %copy-start.3 = (bf16[1,2,128,128]{3,2,1,0:T(8,128)(2,1)S(1)}, bf16[1,2,128,128]{3,2,1,0:T(8,128)(2,1)}, u32[]{:S(2)}) copy-start(bf16[1,2,128,128]{3,2,1,0:T(8,128)(2,1)} %shard_map.47) | copy-start | bytes 196612
  7.8 76.5 %copy-start = (bf16[8,4,128,128]{3,2,1,0:T(8,128)(2,1)S(1)}, bf16[8,4,128,128]{3,2,1,0:T(8,128)(2,1)}, u32[]{:S(2)}) copy-start(bf16[8,4,128,128]{3,2,1,0:T(8,128)(2,1)} %param.4) | copy-start | bytes 3145732
  7.8 76.5 %copy-start.1 = (f32[8,128,128]{2,1,0:T(8,128)S(1)}, f32[8,128,128]{2,1,0:T(8,128)}, u32[]{:S(2)}) copy-start(f32[8,128,128]{2,1,0:T(8,128)} %rest_3_.1) | copy-start | bytes 1572868
  7.8 76.5 %copy-start.2 = (s32[128,4]{0,1:T(4,128)S(1)}, s32[128,4]{0,1:T(4,128)}, u32[]{:S(2)}) copy-start(s32[128,4]{0,1:T(4,128)} %param.7) | copy-start | bytes 6148
  7.9 76.5 %all-to-all-start = ((bf16[16,2,3,128,128]{4,3,2,1,0:T(8,128)(2,1)}), bf16[16,2,3,128,128]{4,3,2,1,0:T(8,128)(2,1)}, u32[]{:S(2)}, u32[]{:S(2)}) async-start(bf16[16,2,3,128,128]{4,3,2,1,0:T(8,128)(2,1)} %shard_map.46), calls=%async_computation | async-start | bytes 6291456 | tf_op jit(solution)/shard_map/all_to_all | solution.py:151
  14.3 20.8 %collective-permute-start.1 = (bf16[2,2,128,128]{3,2,1,0:T(8,128)(2,1)S(1)}, bf16[2,2,128,128]{3,2,1,0:T(8,128)(2,1)S(1)}, u32[]{:S(2)}, u32[]{:S(2)}) collective-permute-start(bf16[2,2,128,128]{3,2,1,0:T(8,128)(2,1)S(1)} %pad_maximum_fusion.2), channel_id=1, source_target_pairs={{2,0},{3,1},{0,2},{1,3},{6,4},{7,5},{4,6},{5,7},{10,8},{11,9},{8,1... | collective-permute-start | bytes 393224 | tf_op jit(solution)/shard_map/ppermute | solution.py:154
  35.2 37.7 %collective-permute-start.2 = (bf16[4,2,128,128]{3,2,1,0:T(8,128)(2,1)S(1)}, bf16[4,2,128,128]{3,2,1,0:T(8,128)(2,1)S(1)}, u32[]{:S(2)}, u32[]{:S(2)}) collective-permute-start(bf16[4,2,128,128]{3,2,1,0:T(8,128)(2,1)S(1)} %pad_maximum_fusion.1), channel_id=1, source_target_pairs={{4,0},{5,1},{6,2},{7,3},{0,4},{1,5},{2,6},{3,7},{12,8},{13,9},{14,... | collective-permute-start | bytes 786440 | tf_op jit(solution)/shard_map/ppermute | solution.py:155
  72.9 2.5 %collective-permute-start.3 = (bf16[8,2,128,128]{3,2,1,0:T(8,128)(2,1)S(1)}, bf16[8,2,128,128]{3,2,1,0:T(8,128)(2,1)S(1)}, u32[]{:S(2)}, u32[]{:S(2)}) collective-permute-start(bf16[8,2,128,128]{3,2,1,0:T(8,128)(2,1)S(1)} %pad_maximum_fusion.rest_0_), channel_id=1, source_target_pairs={{1,0},{0,1},{3,2},{2,3},{5,4},{4,5},{7,6},{6,7},{9,8},{8,9},{11,10... | collective-permute-start | bytes 1572872 | tf_op jit(solution)/shard_map/ppermute | solution.py:157
